TPU v7x, 32 devices: a whole 2x2x4 slice. The times are simulated.
32 devices in a mesh: pipe: 2 (over core), dp: 16 (over z, y, x).
Axes of the slice: x: 2, y: 2, z: 4, core: 2. Of those that a mesh axis runs over, the one named last changes fastest.
Arguments:
- x_global: bfloat16 [32, 197, 768], P('dp'), may hold values from -6 to 6
- x_local: bfloat16 [32, 37, 768], P('dp'), may hold values from -6 to 6
- cot_global: bfloat16 [32, 197, 768], P('dp'), may hold values from -6 to 6
- cot_local: bfloat16 [32, 37, 768], P('dp'), may hold values from -6 to 6
- global_count: int32 [16], P('dp'), may hold values from 1 to 2, as said below
- local_count: int32 [16], P('dp'), may hold values from 1 to 2, as said below
- w_qkv: bfloat16 [2, 768, 2304], P('pipe'), may hold values from -0.21875 to 0.21875
- w_proj: bfloat16 [2, 768, 768], P('pipe'), may hold values from -0.75 to 0.75
- w_fc1: bfloat16 [2, 768, 3072], P('pipe'), may hold values from -0.21875 to 0.21875
- w_fc2: bfloat16 [2, 3072, 768], P('pipe'), may hold values from -0.109375 to 0.109375
- norm1_gain: bfloat16 [2, 768], P('pipe'), may hold values from 0.5 to 1.5
- norm1_shift: bfloat16 [2, 768], P('pipe'), may hold values from -1.75 to 1.75
- q_bias: bfloat16 [2, 768], P('pipe'), may hold values from -1.75 to 1.75
- v_bias: bfloat16 [2, 768], P('pipe'), may hold values from -1.75 to 1.75
- proj_bias: bfloat16 [2, 768], P('pipe'), may hold values from -1.75 to 1.75
- scale_attn: bfloat16 [2, 768], P('pipe'), may hold values from 0.5 to 1.5
- norm2_gain: bfloat16 [2, 768], P('pipe'), may hold values from 0.5 to 1.5
- norm2_shift: bfloat16 [2, 768], P('pipe'), may hold values from -1.75 to 1.75
- fc1_bias: bfloat16 [2, 3072], P('pipe'), may hold values from -1.75 to 1.75
- fc2_bias: bfloat16 [2, 768], P('pipe'), may hold values from -1.75 to 1.75
- scale_mlp: bfloat16 [2, 768], P('pipe'), may hold values from 0.5 to 1.5
- table_global: bfloat16 [2, 732, 12], P('pipe'), may hold values from -6 to 6
- table_local: bfloat16 [2, 124, 12], P('pipe'), may hold values from -6 to 6
Outputs:
- out_global: bfloat16 [2, 32, 197, 768], P('pipe', 'dp')
- out_local: bfloat16 [2, 32, 37, 768], P('pipe', 'dp')
- grad_global_in: bfloat16 [2, 32, 197, 768], P('pipe', 'dp')
- grad_local_in: bfloat16 [2, 32, 37, 768], P('pipe', 'dp')
- grad_w_qkv: float32 [2, 768, 2304], P('pipe', 'dp')
- grad_w_proj: float32 [2, 768, 768], P('pipe', 'dp')
- grad_w_fc1: float32 [2, 768, 3072], P('pipe', 'dp')
- grad_w_fc2: float32 [2, 3072, 768], P('pipe', 'dp')
- grad_norm1_gain: float32 [2, 768], P('pipe')
- grad_norm1_shift: float32 [2, 768], P('pipe')
- grad_q_bias: float32 [2, 768], P('pipe')
- grad_v_bias: float32 [2, 768], P('pipe')
- grad_proj_bias: float32 [2, 768], P('pipe')
- grad_scale_attn: float32 [2, 768], P('pipe')
- grad_norm2_gain: float32 [2, 768], P('pipe')
- grad_norm2_shift: float32 [2, 768], P('pipe')
- grad_fc1_bias: float32 [2, 3072], P('pipe')
- grad_fc2_bias: float32 [2, 768], P('pipe')
- grad_scale_mlp: float32 [2, 768], P('pipe')
- grad_table_global: float32 [2, 732, 12], P('pipe')
- grad_table_local: float32 [2, 124, 12], P('pipe')
Inputs may be any that keep to these rules, and one draw needn't show every extreme that they name: `global_count`: live global crops of each data device: its crops at or after this count are masked; some device has 2 and some has 1. `local_count`: live local crops of each data device: its crops at or after this count are masked; some device has 2 and some has 1.
All inputs are finite; a program needn't handle non-finite values.
Results may differ from a plain program's by a relative error of at most 0.02.
Values may be sent and summed in bfloat16 or wider, within the bound.
A program may use at most 256 MiB of HBM per device.

v0:
```python
import jax
import jax.numpy as jnp
import numpy as np
from jax import lax
from jax.sharding import PartitionSpec as P

GRID_G = 14
GRID_L = 6
MICRO = 2


eps = 1e-06


def passed_along(value, axis, steps):
    count = lax.axis_size(axis)
    first, last = (max(0, -steps), min(count, count - steps))
    return lax.ppermute(value, axis, [(source, source + steps) for source in range(first, last)])


def position_table(grid_side):
    coordinates = np.stack(
        np.meshgrid(np.arange(grid_side), np.arange(grid_side), indexing="ij")
    ).reshape(2, -1)
    relative = coordinates[:, :, None] - coordinates[:, None, :] + grid_side - 1
    entries = (2 * grid_side - 1) ** 2
    lookup = np.zeros((grid_side * grid_side + 1, grid_side * grid_side + 1), np.int32)
    lookup[1:, 1:] = relative[0] * (2 * grid_side - 1) + relative[1]
    lookup[0, 1:] = entries
    lookup[1:, 0] = entries + 1
    lookup[0, 0] = entries + 2
    return lookup


def layer_norm(values, gain, shift):
    centered = values - jnp.mean(values, axis=-1, keepdims=True)
    variance = jnp.mean(centered * centered, axis=-1, keepdims=True)
    return centered * lax.rsqrt(variance + eps) * gain + shift


def gelu_exact(values):
    return jax.nn.gelu(values, approximate=False)


def matmul(left, right):
    return jnp.dot(left, right, preferred_element_type=jnp.float32)


def contract_rows(left, right):
    return lax.dot_general(
        left, right, (((0,), (0,)), ((), ())), preferred_element_type=jnp.float32
    )


def contract_cols(left, right):
    return lax.dot_general(
        left, right, (((1,), (1,)), ((), ())), preferred_element_type=jnp.float32
    )


def as_heads(matrix, tokens, heads):
    return matrix.reshape(-1, tokens, heads, matrix.shape[1] // heads)


def position_bias(table, lookup):
    return jnp.transpose(table.astype(jnp.float32)[lookup], (2, 0, 1))


def attend_forward(queries, key_rows, value_rows, bias):
    scores = (
        jnp.einsum("cqhe,ckhe->chqk", queries, key_rows, preferred_element_type=jnp.float32)
        + bias[None]
    )
    highest = jnp.max(scores, axis=-1, keepdims=True)
    expo = jnp.exp(scores - highest)
    total = jnp.sum(expo, axis=-1, keepdims=True)
    weights = (expo / total).astype(jnp.bfloat16)
    result = jnp.einsum("chqk,ckhe->cqhe", weights, value_rows, preferred_element_type=jnp.float32)
    return (result, highest + jnp.log(total))


def attend_backward(queries, key_rows, value_rows, bias, logsum, grad_out):
    scores = (
        jnp.einsum("cqhe,ckhe->chqk", queries, key_rows, preferred_element_type=jnp.float32)
        + bias[None]
    )
    probs = jnp.exp(scores - logsum)
    grad_probs = jnp.einsum(
        "cqhe,ckhe->chqk", grad_out, value_rows, preferred_element_type=jnp.float32
    )
    grad_values = jnp.einsum(
        "chqk,cqhe->ckhe", probs.astype(jnp.bfloat16), grad_out, preferred_element_type=jnp.float32
    )
    grad_scores = (
        probs * (grad_probs - jnp.sum(probs * grad_probs, axis=-1, keepdims=True))
    ).astype(jnp.bfloat16)
    grad_queries = jnp.einsum(
        "chqk,ckhe->cqhe", grad_scores, key_rows, preferred_element_type=jnp.float32
    )
    grad_keys = jnp.einsum(
        "chqk,cqhe->ckhe", grad_scores, queries, preferred_element_type=jnp.float32
    )
    grad_bias = jnp.sum(grad_scores.astype(jnp.float32), axis=0)
    return (grad_queries, grad_keys, grad_values, grad_bias)


def groups_of(split, total_rows, weights, lookups):
    return ((0, split, weights[15], lookups[0]), (split, total_rows, weights[16], lookups[1]))


def block_forward(entering, weights, lookups, split):
    (
        w_qkv,
        w_proj,
        w_fc1,
        w_fc2,
        norm1_gain,
        norm1_shift,
        q_bias,
        v_bias,
        proj_bias,
        scale_attn,
        norm2_gain,
        norm2_shift,
        fc1_bias,
        fc2_bias,
        scale_mlp,
        table_global,
        table_local,
    ) = weights
    width = w_proj.shape[0]
    heads = table_global.shape[1]
    scale = (width // heads) ** (-0.5)
    upcast = entering.astype(jnp.float32)
    normed = layer_norm(
        upcast, norm1_gain.astype(jnp.float32), norm1_shift.astype(jnp.float32)
    ).astype(jnp.bfloat16)
    mixed = matmul(normed, w_qkv) + jnp.concatenate(
        [q_bias, jnp.zeros_like(q_bias), v_bias]
    ).astype(jnp.float32)
    queries = (mixed[:, :width] * scale).astype(jnp.bfloat16)
    key_rows = mixed[:, width : 2 * width].astype(jnp.bfloat16)
    value_rows = mixed[:, 2 * width :].astype(jnp.bfloat16)
    merged_parts = []
    logsums = []
    for start_row, end_row, table, lookup in groups_of(split, entering.shape[0], weights, lookups):
        tokens = lookup.shape[0]
        result, logsum = attend_forward(
            as_heads(queries[start_row:end_row], tokens, heads),
            as_heads(key_rows[start_row:end_row], tokens, heads),
            as_heads(value_rows[start_row:end_row], tokens, heads),
            position_bias(table, lookup),
        )
        merged_parts.append(result.reshape(-1, width))
        logsums.append(logsum)
    merged = jnp.concatenate(merged_parts, 0).astype(jnp.bfloat16)
    branch = matmul(merged, w_proj) + proj_bias.astype(jnp.float32)
    middle = upcast + scale_attn.astype(jnp.float32) * branch
    normed2 = layer_norm(
        middle, norm2_gain.astype(jnp.float32), norm2_shift.astype(jnp.float32)
    ).astype(jnp.bfloat16)
    hidden = matmul(normed2, w_fc1) + fc1_bias.astype(jnp.float32)
    active = gelu_exact(hidden).astype(jnp.bfloat16)
    branch2 = matmul(active, w_fc2) + fc2_bias.astype(jnp.float32)
    result = middle + scale_mlp.astype(jnp.float32) * branch2
    kept = (
        entering,
        queries,
        key_rows,
        value_rows,
        logsums[0],
        logsums[1],
        merged,
        branch,
        middle,
        hidden,
        branch2,
    )
    return (result, kept)


def block_backward(kept, grad_rows, weights, lookups, split, valid_low):
    (
        w_qkv,
        w_proj,
        w_fc1,
        w_fc2,
        norm1_gain,
        norm1_shift,
        q_bias,
        v_bias,
        proj_bias,
        scale_attn,
        norm2_gain,
        norm2_shift,
        fc1_bias,
        fc2_bias,
        scale_mlp,
        table_global,
        table_local,
    ) = weights
    (
        entering,
        queries,
        key_rows,
        value_rows,
        logsum_g,
        logsum_l,
        merged,
        branch,
        middle,
        hidden,
        branch2,
    ) = kept
    width = w_proj.shape[0]
    heads = table_global.shape[1]
    scale = (width // heads) ** (-0.5)
    grad_mlp = (scale_mlp.astype(jnp.float32) * grad_rows).astype(jnp.bfloat16)
    grad_scale_mlp = jnp.sum(grad_rows * branch2, axis=0)
    grad_fc2_bias = jnp.sum(grad_mlp.astype(jnp.float32), axis=0)
    active = gelu_exact(hidden).astype(jnp.bfloat16)
    grad_active = contract_cols(grad_mlp, w_fc2)
    unused, gelu_pull = jax.vjp(gelu_exact, hidden)
    grad_hidden = gelu_pull(grad_active)[0].astype(jnp.bfloat16)
    grad_fc1_bias = jnp.sum(grad_hidden.astype(jnp.float32), axis=0)
    normed2, norm2_pull = jax.vjp(
        layer_norm, middle, norm2_gain.astype(jnp.float32), norm2_shift.astype(jnp.float32)
    )
    grad_normed2 = contract_cols(grad_hidden, w_fc1)
    grad_middle_norm, grad_norm2_gain, grad_norm2_shift = norm2_pull(grad_normed2)
    grad_middle = grad_rows + grad_middle_norm
    grad_scale_attn = jnp.sum(grad_middle * branch, axis=0)
    grad_branch = (scale_attn.astype(jnp.float32) * grad_middle).astype(jnp.bfloat16)
    grad_proj_bias = jnp.sum(grad_branch.astype(jnp.float32), axis=0)
    grad_merged = contract_cols(grad_branch, w_proj).astype(jnp.bfloat16)
    query_parts, key_parts, value_parts, table_grads = ([], [], [], [])
    for (start_row, end_row, table, lookup), logsum in zip(
        groups_of(split, entering.shape[0], weights, lookups), (logsum_g, logsum_l)
    ):
        tokens = lookup.shape[0]
        grad_q, grad_k, grad_v, grad_bias = attend_backward(
            as_heads(queries[start_row:end_row], tokens, heads),
            as_heads(key_rows[start_row:end_row], tokens, heads),
            as_heads(value_rows[start_row:end_row], tokens, heads),
            position_bias(table, lookup),
            logsum,
            as_heads(grad_merged[start_row:end_row], tokens, heads),
        )
        query_parts.append(grad_q.reshape(-1, width))
        key_parts.append(grad_k.reshape(-1, width))
        value_parts.append(grad_v.reshape(-1, width))
        flat_bias = jnp.transpose(grad_bias, (1, 2, 0)).reshape(tokens * tokens, heads)
        table_grads.append(
            jax.ops.segment_sum(
                flat_bias, jnp.asarray(lookup.reshape(-1)), num_segments=table.shape[0]
            )
        )
    grad_queries = jnp.concatenate(query_parts, 0).astype(jnp.bfloat16) * scale
    grad_keys = jnp.concatenate(key_parts, 0).astype(jnp.bfloat16)
    grad_values = jnp.concatenate(value_parts, 0).astype(jnp.bfloat16)
    grad_mixed = jnp.concatenate([grad_queries, grad_keys, grad_values], 1)
    grad_q_bias = jnp.sum(grad_queries.astype(jnp.float32), axis=0)
    grad_v_bias = jnp.sum(grad_values.astype(jnp.float32), axis=0)
    upcast = entering.astype(jnp.float32)
    normed, norm1_pull = jax.vjp(
        layer_norm, upcast, norm1_gain.astype(jnp.float32), norm1_shift.astype(jnp.float32)
    )
    grad_normed = contract_cols(grad_mixed, w_qkv)
    grad_input_norm, grad_norm1_gain, grad_norm1_shift = norm1_pull(grad_normed)
    grad_input = grad_middle + grad_input_norm
    operands = (
        (normed.astype(jnp.bfloat16), grad_mixed * valid_low),
        (merged, grad_branch * valid_low),
        (normed2.astype(jnp.bfloat16), grad_hidden * valid_low),
        (active, grad_mlp * valid_low),
    )
    smalls = (
        grad_norm1_gain,
        grad_norm1_shift,
        grad_q_bias,
        grad_v_bias,
        grad_proj_bias,
        grad_scale_attn,
        grad_norm2_gain,
        grad_norm2_shift,
        grad_fc1_bias,
        grad_fc2_bias,
        grad_scale_mlp,
        table_grads[0],
        table_grads[1],
    )
    return (grad_input, operands, smalls)


def add_up(total, term):
    if total is None:
        return term
    return tuple((a + b for a, b in zip(total, term)))


def pick(condition, upper, lower):
    return jax.tree.map(lambda a, b: jnp.where(condition, a, b), upper, lower)


def body(
    x_global,
    x_local,
    cot_global,
    cot_local,
    global_count,
    local_count,
    w_qkv,
    w_proj,
    w_fc1,
    w_fc2,
    norm1_gain,
    norm1_shift,
    q_bias,
    v_bias,
    proj_bias,
    scale_attn,
    norm2_gain,
    norm2_shift,
    fc1_bias,
    fc2_bias,
    scale_mlp,
    table_global,
    table_local,
):
    section = lax.axis_index("pipe")
    weights = tuple(
        (
            p[0]
            for p in (
                w_qkv,
                w_proj,
                w_fc1,
                w_fc2,
                norm1_gain,
                norm1_shift,
                q_bias,
                v_bias,
                proj_bias,
                scale_attn,
                norm2_gain,
                norm2_shift,
                fc1_bias,
                fc2_bias,
                scale_mlp,
                table_global,
                table_local,
            )
        )
    )
    lookups = (position_table(GRID_G), position_table(GRID_L))
    width = x_global.shape[2]
    tokens_g = x_global.shape[1]
    tokens_l = x_local.shape[1]
    global_micro = x_global.shape[0] // MICRO
    local_micro = x_local.shape[0] // MICRO
    split = global_micro * tokens_g

    def micro_rows(array_g, array_l, index):
        return jnp.concatenate(
            [
                array_g[index * global_micro : (index + 1) * global_micro].reshape(-1, width),
                array_l[index * local_micro : (index + 1) * local_micro].reshape(-1, width),
            ],
            0,
        )

    def live_rows(count, slots, per_micro, tokens, index):
        live = (jnp.arange(slots, dtype=jnp.int32) < count[0]).astype(jnp.float32)
        chosen = live[index * per_micro : (index + 1) * per_micro]
        return jnp.broadcast_to(chosen[:, None], (per_micro, tokens)).reshape(-1)

    def row_mask(index):
        return jnp.concatenate(
            [
                live_rows(global_count, x_global.shape[0], global_micro, tokens_g, index),
                live_rows(local_count, x_local.shape[0], local_micro, tokens_l, index),
            ],
            0,
        )[:, None]

    received = jnp.zeros((split + local_micro * tokens_l, width), jnp.bfloat16)
    results, stash = ([], [])
    for tick in range(MICRO + 1):
        entering = jnp.where(
            section == 0, micro_rows(x_global, x_local, min(tick, MICRO - 1)), received
        )
        result, kept = block_forward(entering, weights, lookups, split)
        result_low = result.astype(jnp.bfloat16)
        results.append(result_low)
        stash.append(kept)
        if tick < MICRO:
            received = passed_along(result_low, "pipe", 1)
    coming = jnp.zeros_like(received)
    grad_outs = []
    operand_list = []
    small_totals = None
    for tick in range(MICRO + 1):
        later = min(tick, MICRO - 1)
        earlier = max(tick - 1, 0)
        cot_rows = micro_rows(cot_global, cot_local, later).astype(jnp.float32) * row_mask(later)
        grad_rows = jnp.where(section == 1, cot_rows, coming.astype(jnp.float32))
        chosen = pick(section == 1, stash[later + 1], stash[earlier])
        kept = chosen
        valid = jnp.where(section == 1, float(tick < MICRO), float(tick >= 1)).astype(jnp.float32)
        grad_input, operands, smalls = block_backward(
            kept, grad_rows, weights, lookups, split, valid.astype(jnp.bfloat16)
        )
        operand_list.append(operands)
        smalls = tuple((valid * s for s in smalls))
        small_totals = add_up(small_totals, smalls)
        grad_low = grad_input.astype(jnp.bfloat16)
        grad_outs.append(grad_low)
        if tick < MICRO:
            coming = passed_along(grad_low, "pipe", -1)

    def product(position):
        left_rows = jnp.concatenate([entry[position][0] for entry in operand_list], 0)
        right_rows = jnp.concatenate([entry[position][1] for entry in operand_list], 0)
        return contract_rows(left_rows, right_rows)

    share_totals = (
        lax.psum_scatter(product(0), "dp", scatter_dimension=0, tiled=True),
        lax.psum_scatter(product(1), "dp", scatter_dimension=0, tiled=True),
        lax.psum_scatter(product(2), "dp", scatter_dimension=0, tiled=True),
        lax.psum_scatter(product(3), "dp", scatter_dimension=0, tiled=True),
    )
    sum_totals = lax.psum(small_totals, "dp")
    outputs_g, outputs_l, inputs_g, inputs_l = ([], [], [], [])
    for index in range(MICRO):
        produced = jnp.where(section == 0, results[index], results[index + 1])
        produced = jnp.where(row_mask(index) > 0, produced, jnp.zeros_like(produced))
        returned = jnp.where(section == 1, grad_outs[index], grad_outs[index + 1])
        outputs_g.append(produced[:split].reshape(global_micro, tokens_g, width))
        outputs_l.append(produced[split:].reshape(local_micro, tokens_l, width))
        inputs_g.append(returned[:split].reshape(global_micro, tokens_g, width))
        inputs_l.append(returned[split:].reshape(local_micro, tokens_l, width))
    out_global = jnp.concatenate(outputs_g, 0)[None]
    out_local = jnp.concatenate(outputs_l, 0)[None]
    grad_global_in = jnp.concatenate(inputs_g, 0)[None]
    grad_local_in = jnp.concatenate(inputs_l, 0)[None]
    grad_qkv, grad_proj, grad_fc1, grad_fc2 = (s[None] for s in share_totals)
    (
        grad_n1g,
        grad_n1s,
        grad_qb,
        grad_vb,
        grad_pb,
        grad_sa,
        grad_n2g,
        grad_n2s,
        grad_f1b,
        grad_f2b,
        grad_sm,
        grad_tg,
        grad_tl,
    ) = (s[None] for s in sum_totals)
    return (
        out_global,
        out_local,
        grad_global_in,
        grad_local_in,
        grad_qkv,
        grad_proj,
        grad_fc1,
        grad_fc2,
        grad_n1g,
        grad_n1s,
        grad_qb,
        grad_vb,
        grad_pb,
        grad_sa,
        grad_n2g,
        grad_n2s,
        grad_f1b,
        grad_f2b,
        grad_sm,
        grad_tg,
        grad_tl,
    )


def solution(mesh):
    in_specs = (
        P("dp", None, None),
        P("dp", None, None),
        P("dp", None, None),
        P("dp", None, None),
        P("dp"),
        P("dp"),
        P("pipe", None, None),
        P("pipe", None, None),
        P("pipe", None, None),
        P("pipe", None, None),
        P("pipe", None),
        P("pipe", None),
        P("pipe", None),
        P("pipe", None),
        P("pipe", None),
        P("pipe", None),
        P("pipe", None),
        P("pipe", None),
        P("pipe", None),
        P("pipe", None),
        P("pipe", None),
        P("pipe", None, None),
        P("pipe", None, None),
    )
    out_specs = (
        P("pipe", "dp", None, None),
        P("pipe", "dp", None, None),
        P("pipe", "dp", None, None),
        P("pipe", "dp", None, None),
        P("pipe", "dp", None),
        P("pipe", "dp", None),
        P("pipe", "dp", None),
        P("pipe", "dp", None),
        P("pipe", None),
        P("pipe", None),
        P("pipe", None),
        P("pipe", None),
        P("pipe", None),
        P("pipe", None),
        P("pipe", None),
        P("pipe", None),
        P("pipe", None),
        P("pipe", None),
        P("pipe", None),
        P("pipe", None, None),
        P("pipe", None, None),
    )
    return jax.shard_map(body, mesh=mesh, in_specs=in_specs, out_specs=out_specs, check_vma=False)
```

profile of v0, /device:TPU:0, one launch (start us, length us, event | category | flops | bytes accessed | tf_op | source)
XLA Modules:
  0.0 2152.6 jit_solution(16785539580732203534)
XLA Ops:
  9.9 3.1 fusion.606
  25.4 4.5 gather_fusion.1
  52.0 142.9 %gather_fusion = f32[38809,12]{1,0:T(8,128)} fusion(f32[732,12]{1,0:T(8,128)} %bitcast_convert_fusion, s32[38912]{0:T(1024)} %pad_clamp_fusion), kind=kCustom, calls=%fused_computation | custom fusion | bytes 3880900 | tf_op jit(solution)/shard_map/gather | solution.py:66
  194.9 12.1 copy.168
  207.1 4.1 reshape.1331
  211.1 3.3 copy.169
  218.2 2.5 fusion.613
  225.9 3.0 fusion.598
  230.6 3.8 fusion.36
  234.5 8.5 add_convert_fusion.13
  243.0 3.1 collective-permute-start
  268.7 2.6 convert_reduce_fusion.8
  295.1 2.5 fusion.616
  301.3 4.2 fusion.596
  309.4 4.0 fusion.39
  313.5 11.9 select_select_fusion
  335.2 2.6 convert_reduce_fusion.6
  362.9 2.5 fusion.619
  369.1 4.1 fusion.588
  375.6 2.8 fusion.592
  378.5 25.0 %multiply_convert_fusion = (bf16[234,3072]{1,0:T(8,128)(2,1)}, f32[234,3072]{1,0:T(8,128)}, f32[234,3072]{1,0:T(8,128)}, bf16[234,3072]{1,0:T(8,128)(2,1)}, f32[...) fusion(f32[234,3072]{1,0:T(8,128)} %copy-done.218, ...), kind=kOutput, calls=%fused_computation.94 | convolution fusion | flops 1248099840 | bytes 35649360 | tf_op jit(solution)/shard_map/dot_general | solution.py:46
  403.5 5.7 broadcast_multiply_fusion.1
  409.3 5.7 multiply_reduce_fusion.8
  458.7 3.6 fusion.578
  485.4 11.5 fusion.365
  509.9 3.2 fusion.621
  515.0 6.2 convert_reduce_fusion.1
  521.2 5.8 multiply_reduce_fusion.7
  527.4 2.7 convert_reduce_fusion.19
  542.8 3.6 multiply_reduce_fusion.1
  558.6 3.7 fusion.579
  580.6 3.3 fusion.622
  584.8 2.4 multiply_reduce_fusion.4
  587.3 6.6 broadcast_multiply_fusion
  594.1 3.0 multiply_reduce_fusion.6
  613.0 3.6 multiply_reduce_fusion
  631.5 3.2 fusion.580
  635.6 2.9 fusion.336
  651.3 4.8 fusion.253
  656.1 3.3 copy.273
  659.4 3.8 reshape.1358
  663.2 11.0 copy.274
  674.2 208.3 %scatter_custom_fusion.1 = f32[732,12]{1,0:T(8,128)} fusion(s32[38809]{0:T(1024)} %constant.182, f32[38809,12]{1,0:T(8,128)} %copy.274, f32[]{:T(128)} %constant.49.clone.1), kind=kCustom, calls=%fused_computation.669 | custom fusion | flops 465708 | bytes 35648 | tf_op jit(solution)/shard_map/scatter-add | solution.py:254
  882.5 3.3 copy.270
  885.7 3.8 reshape.1350
  889.6 11.0 copy.271
  900.5 208.7 %scatter_custom_fusion = f32[732,12]{1,0:T(8,128)} fusion(s32[38809]{0:T(1024)} %constant.182, f32[38809,12]{1,0:T(8,128)} %copy.271, f32[]{:T(128)} %constant.49.clone.1), kind=kCustom, calls=%fused_computation.671 | custom fusion | flops 465708 | bytes 35648 | tf_op jit(solution)/shard_map/scatter-add | solution.py:254
  1109.3 3.3 copy.276
  1112.6 3.8 reshape.1366
  1116.4 11.0 copy.277
  1127.4 2.5 fusion.421
  1135.5 9.8 scatter_custom_fusion.4
  1150.8 9.8 scatter_custom_fusion.3
  1168.0 189.2 %scatter_fusion = f32[732,12]{1,0:T(8,128)} fusion(f32[732,12]{1,0:T(8,128)} %multiply_add_fusion, s32[38809]{0:T(1024)} %constant.182, f32[38809,12]{1,0:T(8,128)} %copy.277), kind=kCustom, calls=%fused_computation.4 | custom fusion | flops 465708 | bytes 5743732 | tf_op jit(solution)/shard_map/scatter-add | solution.py:254
  1358.7 9.8 scatter_fusion.1
  1369.9 4.1 fusion.289
  1377.6 16.5 fusion.45
  1394.4 10.1 fusion.24
  1405.6 10.0 fusion.30
  1424.6 65.5 %all-reduce.5.cloned.1.call-done = (f32[1,768]{1,0:T(1,128)}, f32[1,768]{1,0:T(1,128)}, f32[1,768]{1,0:T(1,128)}, f32[1,768]{1,0:T(1,128)}, f32[1,768]{1,0:T(1,1...) async-done(((f32[1,768]{1,0:T(1,128)}, f32[1,768]{1,0:T(1,128)}, ...) | async-done | bytes 84112 | tf_op jit(solution)/shard_map/psum | solution.py:432
  1493.4 129.2 %reduce-scatter.7.cloned.1.call-done = f32[48,768]{1,0:T(8,128)} async-done(((f32[768,768]{1,0:T(8,128)}), f32[48,768]{1,0:T(8,128)}) %reduce-scatter.7.cloned.1.call-update) | async-done | bytes 147472 | tf_op jit(solution)/shard_map/reduce_scatter | solution.py:428
  1622.6 156.4 %reduce-scatter.5.cloned.1.call-done = f32[48,2304]{1,0:T(8,128)} async-done(((f32[768,2304]{1,0:T(8,128)}), f32[48,2304]{1,0:T(8,128)}) %reduce-scatter.5.cloned.1.call-update) | async-done | bytes 442384 | tf_op jit(solution)/shard_map/reduce_scatter | solution.py:427
  1779.0 177.0 %reduce-scatter.9.cloned.1.call-done = f32[48,3072]{1,0:T(8,128)} async-done(((f32[768,3072]{1,0:T(8,128)}), f32[48,3072]{1,0:T(8,128)}) %reduce-scatter.9.cloned.1.call-update) | async-done | bytes 589840 | tf_op jit(solution)/shard_map/reduce_scatter | solution.py:429
  1956.0 175.9 %reduce-scatter.11.cloned.1.call-done = f32[192,768]{1,0:T(8,128)} async-done(((f32[3072,768]{1,0:T(8,128)}), f32[192,768]{1,0:T(8,128)}) %reduce-scatter.11.cloned.1.call-update) | async-done | bytes 589840 | tf_op jit(solution)/shard_map/reduce_scatter | solution.py:430
  (799 shorter events, 362.7 us)
Async XLA Ops:
  7.2 9.8 copy-start
  7.2 6.5 copy-start.214
  7.2 6.5 copy-start.215
  7.2 1482.9 %all-reduce.5.cloned.1.call-start = ((), (), s32[]{:S(2)}) async-start(), calls=%async_computation.8 | async-start | bytes 970752 | tf_op jit(solution)/shard_map/psum | solution.py:432
  16.9 617.8 %copy-start.118 = (f32[768]{0:T(1024)}, f32[768]{0:T(1024)S(1)}, u32[]{:S(2)}) copy-start(f32[768]{0:T(1024)S(1)} %get-tuple-element.297) | copy-start | bytes 9220
  225.1 9.3 copy-start.179
  225.9 8.6 slice-start
  234.4 8.6 copy-start.217
  234.5 13.5 copy-start.117
  234.5 14.4 copy-start.69
  243.0 25.7 %collective-permute-start = (bf16[234,768]{1,0:T(8,128)(2,1)}, bf16[234,768]{1,0:T(8,128)(2,1)}, u32[]{:S(2)}, u32[]{:S(2)}) collective-permute-start(bf16[234,768]{1,0:T(8,128)(2,1)} %get-tuple-element.258), channel_id=1, source_target_pairs={{0,16},{1,17},{2,18},{3,19},{4,20},{5,21},{6,22},{7,23},{8,24},{9,... | collective-permute-start | bytes 1078280 | tf_op jit(solution)/shard_map/ppermute | solution.py:18
  313.4 12.0 copy-start.218
  313.5 14.4 copy-start.202
  325.4 9.7 collective-permute-start.1
  378.5 25.0 %copy-start.26 = (bf16[1,197,768]{2,1,0:T(8,128)(2,1)S(1)}, bf16[1,197,768]{2,1,0:T(8,128)(2,1)}, u32[]{:S(2)}) copy-start(bf16[1,197,768]{2,1,0:T(8,128)(2,1)} %copy.430) | copy-start | bytes 907780
  378.5 25.0 %copy-start.83 = (bf16[1,37,768]{2,1,0:T(8,128)(2,1)S(1)}, bf16[1,37,768]{2,1,0:T(8,128)(2,1)}, u32[]{:S(2)}) copy-start(bf16[1,37,768]{2,1,0:T(8,128)(2,1)} %copy.434) | copy-start | bytes 170500
  378.5 25.0 %copy-start.160 = (f32[768]{0:T(1024)S(1)}, f32[768]{0:T(1024)}, u32[]{:S(2)}) copy-start(f32[768]{0:T(1024)} %copy-done.158) | copy-start | bytes 9220
  378.5 25.0 %copy-start.169 = (f32[234]{0:T(256)S(1)}, f32[234]{0:T(256)}, u32[]{:S(2)}) copy-start(f32[234]{0:T(256)} %concatenate.131) | copy-start | bytes 2812
  426.6 7.0 copy-start.108
  466.0 47.2 %collective-permute-start.2 = (bf16[234,768]{1,0:T(8,128)(2,1)}, bf16[234,768]{1,0:T(8,128)(2,1)}, u32[]{:S(2)}, u32[]{:S(2)}) collective-permute-start(bf16[234,768]{1,0:T(8,128)(2,1)} %get-tuple-element.220), channel_id=1, source_target_pairs={{16,0},{17,1},{18,2},{19,3},{20,4},{21,5},{22,6},{23,7},{24,8},{25... | collective-permute-start | bytes 1078280 | tf_op jit(solution)/shard_map/ppermute | solution.py:18
  485.4 11.6 copy-start.106
  485.4 11.6 copy-start.107
  485.4 12.5 copy-start.104
  485.4 12.5 copy-start.105
  485.4 13.4 copy-start.91
  485.4 14.3 copy-start.101
  565.6 19.2 collective-permute-start.3
  578.4 6.4 copy-start.24
  578.4 6.4 copy-start.28
  578.4 6.4 copy-start.85
  578.4 6.4 copy-start.87
  578.4 6.4 copy-start.112
  578.4 6.4 copy-start.113
  578.5 6.4 copy-start.114
  578.5 6.4 copy-start.162
  578.5 6.4 copy-start.167
  578.5 6.3 copy-start.171
  580.6 6.7 copy-start.220
  580.6 13.4 slice-start.2
  587.3 6.7 copy-start.102
  587.3 6.7 copy-start.33
  587.3 6.7 copy-start.182
  587.3 6.7 copy-start.199
  587.3 6.7 copy-start.208
  587.3 6.7 slice-start.3
  623.1 15.3 copy-start.174
  623.1 25.6 %copy-start.175 = (f32[768]{0:T(1024)S(1)}, f32[768]{0:T(1024)}, u32[]{:S(2)}) copy-start(f32[768]{0:T(1024)} %get-tuple-element.107) | copy-start | bytes 9220
  628.4 12.6 copy-start.173
  628.4 15.2 copy-start.172
  628.4 22.9 %copy-start.13 = (f32[12,197,197]{1,2,0:T(8,128)S(1)}, f32[12,197,197]{1,2,0:T(8,128)}, u32[]{:S(2)}) copy-start(f32[12,197,197]{1,2,0:T(8,128)} %fusion.622) | copy-start | bytes 5588500
  631.4 19.8 copy-start.2
  631.4 19.8 copy-start.7
  631.4 19.8 copy-start.9
  631.5 19.8 copy-start.10
  631.5 19.8 copy-start.12
  631.5 19.8 copy-start.135
  634.8 16.5 copy-start.197
  1116.4 11.0 copy-start.145
  1116.4 11.0 copy-start.147
  1358.7 9.8 copy-start.157
  1369.8 252.8 %reduce-scatter.7.cloned.1.call-start = ((), (), s32[]{:S(2)}) async-start(), calls=%async_computation.5 | async-start | bytes 2506752 | tf_op jit(solution)/shard_map/reduce_scatter | solution.py:428
  1374.0 405.0 %reduce-scatter.5.cloned.1.call-start = ((), (), s32[]{:S(2)}) async-start(), calls=%async_computation.4 | async-start | bytes 7520256 | tf_op jit(solution)/shard_map/reduce_scatter | solution.py:427
  1394.1 561.9 %reduce-scatter.9.cloned.1.call-start = ((), (), s32[]{:S(2)}) async-start(), calls=%async_computation.6 | async-start | bytes 10027008 | tf_op jit(solution)/shard_map/reduce_scatter | solution.py:429
  1404.5 727.4 %reduce-scatter.11.cloned.1.call-start = ((), (), s32[]{:S(2)}) async-start(), calls=%async_computation.7 | async-start | bytes 10027008 | tf_op jit(solution)/shard_map/reduce_scatter | solution.py:430
  (171 other events, 584.3 us)
Sparse Core Ops, SparseCore 0:
  1369.9 120.1 all-reduce.4
  1495.6 126.9 reduce-scatter.6
  1629.4 149.5 reduce-scatter.4
  1786.1 169.9 reduce-scatter.8
  1962.1 169.7 reduce-scatter.10
where the time goes:
time: 2180 us; the launch traced here: 2150 us
  other arithmetic  745 us (34%)
  waiting for transfers between devices  704 us (32%)
  local copies, waits for them, and re-layouts  439 us (20%)
  matrix products  237 us (11%)
    scatter-add x6, other arithmetic, block_backward(): jax.ops.segment_sum(flat_bias, jnp.asarray(lookup.reshape(-1)), num_segme...  636 us
    reduce_scatter x1, waiting for transfers between devices, body(): lax.psum_scatter(product(2), 'dp', scatter_dimension=0, tiled=True)  177 us
    reduce_scatter x1, waiting for transfers between devices, body(): lax.psum_scatter(product(3), 'dp', scatter_dimension=0, tiled=True)  176 us
    gather x8, local copies, waits for them, and re-layouts, position_bias(): return jnp.transpose(table.astype(jnp.float32)[lookup], (2, 0, 1))  172 us
    reduce_scatter x1, waiting for transfers between devices, body(): lax.psum_scatter(product(0), 'dp', scatter_dimension=0, tiled=True)  156 us
    reduce_scatter x1, waiting for transfers between devices, body(): lax.psum_scatter(product(1), 'dp', scatter_dimension=0, tiled=True)  129 us
    dot_general x12, matrix products, matmul(): return jnp.dot(left, right, preferred_element_type=jnp.float32)  81 us
    reshape x18, local copies, waits for them, and re-layouts, block_backward(): jnp.transpose(grad_bias, (1, 2, 0)).reshape(tokens * tokens, heads)  70.9 us
  transfers between devices with their start and end apart: 9, of which 5 were waited for; matrix products, arithmetic and copies ran while one was open for 7% of the time, Pallas kernels for 0%

commit v1 on v0

v1 whole, which is shorter than its diff:
```python
import functools
import jax
import jax.numpy as jnp
import numpy as np
from jax import lax
from jax.experimental import pallas as pl
from jax.experimental.pallas import tpu as pltpu
from jax.sharding import PartitionSpec as P

GRID_G = 14
GRID_L = 6
ROWS = 256
LOCAL_ROW = 208
LANES_G = 512
LANES_L = 128
FRONT_L = 51
BLOCK = 256
NEG = -1e30
eps = 1e-06
F32 = jnp.float32
BF16 = jnp.bfloat16
INV_SQRT2 = 0.7071067811865476
INV_SQRT_2PI = 0.3989422804014327
N1G, N1S, QB, VB, PB, SA, N2G, N2S, F2B, SM, F1B = range(11)


def spread_index(grid, rows, lanes, front, cls_lane):
    side = 2 * grid - 1
    entries = side * side
    index = np.full((rows, lanes), -1, np.int32)
    for q in range(grid):
        for a in range(side):
            for k in range(grid):
                index[q, front + a * grid + k] = (side - 1 - a) * side + (q - k + grid - 1)
    index[rows - 2, :] = entries
    index[rows - 2, cls_lane] = entries + 2
    index[rows - 1, :] = entries + 1
    return index


INDEX_G = spread_index(GRID_G, 16, LANES_G, 1, 0)
INDEX_L = spread_index(GRID_L, 8, LANES_L, FRONT_L, LOCAL_ROW - 128)


def one_hot(index, count):
    flat = jnp.asarray(index.reshape(1, -1))
    return (lax.broadcasted_iota(jnp.int32, (count, flat.shape[1]), 0) == flat).astype(BF16)


def spread(table, index):
    heads = table.shape[1]
    flat = lax.dot_general(
        table, one_hot(index, table.shape[0]), (((0,), (0,)), ((), ())), preferred_element_type=F32
    )
    return flat.astype(BF16).reshape(heads, *index.shape)


def gather_back(values, index, count):
    heads = values.shape[0]
    flat = values.reshape(heads, -1)
    high = flat.astype(BF16)
    low = (flat - high.astype(F32)).astype(BF16)
    both = jnp.concatenate([high, low], 0)
    sums = lax.dot_general(
        one_hot(index, count), both, (((1,), (1,)), ((), ())), preferred_element_type=F32
    )
    return sums[:, :heads] + sums[:, heads:]


def dot(a, b):
    return lax.dot_general(a, b, (((1,), (0,)), ((), ())), preferred_element_type=F32)


def dot_cols(a, b):
    return lax.dot_general(a, b, (((1,), (1,)), ((), ())), preferred_element_type=F32)


def dot_rows(a, b):
    return lax.dot_general(a, b, (((0,), (0,)), ((), ())), preferred_element_type=F32)


def fetch(layer, pairs, sems):
    section = lax.axis_index("pipe")
    for number, (own, other, held) in enumerate(pairs):

        @pl.when(section == layer)
        def _():
            pltpu.make_async_copy(own, held, sems.at[number]).start()

        @pl.when(section != layer)
        def _():
            pltpu.make_async_copy(other, held, sems.at[number]).start()


def arrive(pairs, sems, number):
    own, other, held = pairs[number]
    pltpu.make_async_copy(own, held, sems.at[number]).wait()


def normalised(x):
    centered = x - jnp.mean(x, axis=-1, keepdims=True)
    rstd = lax.rsqrt(jnp.mean(centered * centered, axis=-1, keepdims=True) + eps)
    return centered * rstd, rstd


def row_steps(step, body):
    def one(i, carry):
        body(pl.ds(pl.multiple_of(i * step, step), step))
        return carry

    lax.fori_loop(0, ROWS // step, one, 0)


def build_bias(spread_g, spread_l, bias):
    for r in range(GRID_G):
        shifted = pltpu.roll(spread_g, (LANES_G - (GRID_G - 1 - r) * GRID_G) % LANES_G, 1)
        bias[pl.ds(1 + GRID_G * r, GRID_G), :] = shifted[:GRID_G, :ROWS]
    for r in range(GRID_L):
        shifted = pltpu.roll(spread_l, GRID_L * r, 1)
        bias[pl.ds(LOCAL_ROW + 1 + GRID_L * r, GRID_L), pl.ds(128, 128)] = shifted[:GRID_L, :]
    tokens_g = GRID_G * GRID_G + 1
    tokens_l = GRID_L * GRID_L + 1
    top = bias[:LOCAL_ROW, :]
    row = lax.broadcasted_iota(jnp.int32, top.shape, 0)
    col = lax.broadcasted_iota(jnp.int32, top.shape, 1)
    top = jnp.where(col == 0, spread_g[15:16, :ROWS], top)
    top = jnp.where(row == 0, spread_g[14:15, :ROWS], top)
    top = jnp.where(row >= tokens_g, 0.0, top)
    top = jnp.where(col >= tokens_g, NEG, top)
    low = bias[LOCAL_ROW:, 128:]
    row = lax.broadcasted_iota(jnp.int32, low.shape, 0)
    col = lax.broadcasted_iota(jnp.int32, low.shape, 1) - (LOCAL_ROW - 128)
    low = jnp.where(col == 0, spread_l[7:8], low)
    low = jnp.where(row == 0, spread_l[6:7], low)
    low = jnp.where(row >= tokens_l, 0.0, low)
    low = jnp.where((col >= 0) & (col < tokens_l), low, NEG)
    bottom = jnp.concatenate([jnp.full((ROWS - LOCAL_ROW, 128), NEG, F32), low], 1)
    return jnp.concatenate([top, bottom], 0)


def forward_kernel(
    layer, scale,
    x_ref, vec_ref, sg_ref, sl_ref,
    own_qkv, own_proj, own_fc1, own_fc2, oth_qkv, oth_proj, oth_fc1, oth_fc2,
    out_ref, n1_ref, q_ref, k_ref, v_ref, p_ref, merged_ref, branch_ref, middle_ref,
    n2_ref, act_ref, dact_ref, branch2_ref,
    w_qkv, w_proj, w_fc1, w_fc2, bias, sems,
):
    pairs = (
        (own_qkv, oth_qkv, w_qkv), (own_proj, oth_proj, w_proj),
        (own_fc1, oth_fc1, w_fc1), (own_fc2, oth_fc2, w_fc2),
    )
    fetch(layer, pairs, sems)
    width = x_ref.shape[1]
    heads = p_ref.shape[0]

    def vec(row):
        return vec_ref[row:row + 1, :]

    def norm1(rows):
        xhat, _ = normalised(x_ref[rows, :].astype(F32))
        n1_ref[rows, :] = (xhat * vec(N1G) + vec(N1S)).astype(BF16)

    row_steps(32, norm1)
    arrive(pairs, sems, 0)
    n1 = n1_ref[...]
    for b in range(0, width, BLOCK):
        cols = slice(b, b + BLOCK)
        mixed = dot(n1, w_qkv[:, b:b + BLOCK]) + vec_ref[QB:QB + 1, cols]
        q_ref[:, cols] = (mixed * scale).astype(BF16)
        k_ref[:, cols] = dot(n1, w_qkv[:, width + b:width + b + BLOCK]).astype(BF16)
        mixed = dot(n1, w_qkv[:, 2 * width + b:2 * width + b + BLOCK]) + vec_ref[VB:VB + 1, cols]
        v_ref[:, cols] = mixed.astype(BF16)
    lane = lax.broadcasted_iota(jnp.int32, (1, 128), 1)
    for pair in range(heads // 2):
        cols = slice(pair * 128, pair * 128 + 128)
        q, k, v = q_ref[:, cols], k_ref[:, cols], v_ref[:, cols]
        result = None
        for half in range(2):
            head = 2 * pair + half
            mine = (lane < 64) if half == 0 else (lane >= 64)
            scores = dot_cols(q, jnp.where(mine, k, jnp.zeros_like(k))) + build_bias(
                sg_ref[head].astype(F32), sl_ref[head].astype(F32), bias.at[head % 2]
            )
            expo = jnp.exp(scores - jnp.max(scores, axis=-1, keepdims=True))
            probs = expo * (1.0 / jnp.sum(expo, axis=-1, keepdims=True))
            p_ref[head] = probs
            part = dot(probs.astype(BF16), jnp.where(mine, v, jnp.zeros_like(v)))
            result = part if result is None else result + part
        merged_ref[:, cols] = result.astype(BF16)
    arrive(pairs, sems, 1)
    merged = merged_ref[...]
    for b in range(0, width, BLOCK):
        cols = slice(b, b + BLOCK)
        branch = dot(merged, w_proj[:, cols]) + vec_ref[PB:PB + 1, cols]
        branch_ref[:, cols] = branch
        middle_ref[:, cols] = x_ref[:, cols].astype(F32) + vec_ref[SA:SA + 1, cols] * branch

    def norm2(rows):
        xhat, _ = normalised(middle_ref[rows, :])
        n2_ref[rows, :] = (xhat * vec(N2G) + vec(N2S)).astype(BF16)

    row_steps(32, norm2)
    arrive(pairs, sems, 2)
    n2 = n2_ref[...]
    for b in range(0, w_fc1.shape[1], BLOCK):
        cols = slice(b, b + BLOCK)
        part = b // width
        hidden = dot(n2, w_fc1[:, cols]) + vec_ref[
            F1B + part:F1B + part + 1, b - part * width:b - part * width + BLOCK
        ]
        cdf = 0.5 + 0.5 * lax.erf(hidden * INV_SQRT2)
        act_ref[:, cols] = (hidden * cdf).astype(BF16)
        dact_ref[:, cols] = cdf + hidden * (INV_SQRT_2PI * jnp.exp(-0.5 * hidden * hidden))
    arrive(pairs, sems, 3)
    for b in range(0, width, BLOCK):
        cols = slice(b, b + BLOCK)
        branch2 = dot(act_ref[...], w_fc2[:, cols]) + vec_ref[F2B:F2B + 1, cols]
        branch2_ref[:, cols] = branch2
        out_ref[:, cols] = (middle_ref[:, cols] + vec_ref[SM:SM + 1, cols] * branch2).astype(BF16)


def backward_kernel(
    layer, scale,
    x_ref, g_ref, vec_ref, q_ref, k_ref, v_ref, p_ref, branch_ref, middle_ref, dact_ref, branch2_ref,
    own_qkv, own_proj, own_fc1, own_fc2, oth_qkv, oth_proj, oth_fc1, oth_fc2,
    gx_ref, gmixed_ref, gbranch_ref, ghidden_ref, gb2_ref, small_ref, tg_ref, tl_ref,
    w_qkv, w_proj, w_fc1, w_fc2, gmid, gnorm, gmerged, gs_ref, sems,
):
    pairs = (
        (own_fc2, oth_fc2, w_fc2), (own_fc1, oth_fc1, w_fc1),
        (own_proj, oth_proj, w_proj), (own_qkv, oth_qkv, w_qkv),
    )
    fetch(layer, pairs, sems)
    width = x_ref.shape[1]
    heads = p_ref.shape[0]
    small_ref[...] = jnp.zeros_like(small_ref)

    def vec(row):
        return vec_ref[row:row + 1, :]

    def add_small(row, values):
        small_ref[row:row + 1, :] += jnp.sum(values, axis=0, keepdims=True)

    def scaled(rows):
        grad = g_ref[rows, :].astype(F32)
        low = (vec(SM) * grad).astype(BF16)
        gb2_ref[rows, :] = low
        add_small(SM, grad * branch2_ref[rows, :])
        add_small(F2B, low.astype(F32))

    row_steps(32, scaled)
    arrive(pairs, sems, 0)
    gb2 = gb2_ref[...]
    for b in range(0, w_fc1.shape[1], BLOCK):
        cols = slice(b, b + BLOCK)
        part = b // width
        ghidden = (dot_cols(gb2, w_fc2[cols, :]) * dact_ref[:, cols]).astype(BF16)
        ghidden_ref[:, cols] = ghidden
        small_ref[F1B + part:F1B + part + 1, b - part * width:b - part * width + BLOCK] = jnp.sum(
            ghidden.astype(F32), axis=0, keepdims=True
        )
    arrive(pairs, sems, 1)
    for b in range(0, width, BLOCK):
        gnorm[:, b:b + BLOCK] = dot_cols(ghidden_ref[...], w_fc1[b:b + BLOCK, :])

    def norm_back(values, grad, gain):
        xhat, rstd = normalised(values)
        scaled_grad = grad * gain
        mean1 = jnp.mean(scaled_grad, axis=-1, keepdims=True)
        mean2 = jnp.mean(scaled_grad * xhat, axis=-1, keepdims=True)
        return xhat, rstd * (scaled_grad - mean1 - xhat * mean2)

    def norm2(rows):
        grad = gnorm[rows, :]
        xhat, through = norm_back(middle_ref[rows, :], grad, vec(N2G))
        grad_middle = g_ref[rows, :].astype(F32) + through
        gmid[rows, :] = grad_middle
        add_small(N2G, grad * xhat)
        add_small(N2S, grad)
        add_small(SA, grad_middle * branch_ref[rows, :])
        low = (vec(SA) * grad_middle).astype(BF16)
        gbranch_ref[rows, :] = low
        add_small(PB, low.astype(F32))

    row_steps(32, norm2)
    arrive(pairs, sems, 2)
    for b in range(0, width, BLOCK):
        gmerged[:, b:b + BLOCK] = dot_cols(gbranch_ref[...], w_proj[b:b + BLOCK, :]).astype(BF16)
    lane = lax.broadcasted_iota(jnp.int32, (1, 128), 1)
    lane_all = lax.broadcasted_iota(jnp.int32, (1, ROWS), 1)
    for pair in range(heads // 2):
        cols = slice(pair * 128, pair * 128 + 128)
        q, k, v, gm = q_ref[:, cols], k_ref[:, cols], v_ref[:, cols], gmerged[:, cols]
        gq = gk = gv = 0.0
        for half in range(2):
            head = 2 * pair + half
            mine = (lane < 64) if half == 0 else (lane >= 64)

            def only(values):
                return jnp.where(mine, values, jnp.zeros_like(values))

            probs = p_ref[head]
            grad_probs = dot_cols(gm, only(v))
            total = jnp.sum(probs * grad_probs, axis=-1, keepdims=True)
            gscores = (probs * (grad_probs - total)).astype(BF16)
            gv += dot_rows(probs.astype(BF16), only(gm))
            gq += dot(gscores, only(k))
            gk += dot_rows(gscores, only(q))
            wide = gscores.astype(F32)
            gs = gs_ref.at[head % 2]
            gs[...] = jnp.where((lane_all == 0) | (lane_all == LOCAL_ROW), 0.0, wide)
            acc = jnp.zeros((GRID_G, LANES_G), F32)
            for r in range(GRID_G):
                block = gs[pl.ds(1 + GRID_G * r, GRID_G), :]
                block = jnp.concatenate([block, jnp.zeros_like(block)], 1)
                acc += pltpu.roll(block, (GRID_G - 1 - r) * GRID_G, 1)
            first_row = wide[0:1, :]
            to_class = jnp.sum(wide[:LOCAL_ROW, :], axis=0, keepdims=True) - first_row
            to_class = jnp.where(lane_all == 0, to_class, 0.0)
            blank = jnp.zeros((1, LANES_G - ROWS), F32)
            tg_ref[head, 0:GRID_G, :] = acc
            tg_ref[head, 14:15, :] = jnp.concatenate([first_row, blank], 1)
            tg_ref[head, 15:16, :] = jnp.concatenate([to_class, blank], 1)
            acc = jnp.zeros((GRID_L, LANES_L), F32)
            for r in range(GRID_L):
                block = gs[pl.ds(LOCAL_ROW + 1 + GRID_L * r, GRID_L), pl.ds(128, 128)]
                acc += pltpu.roll(block, (LANES_L - GRID_L * r) % LANES_L, 1)
            first_row = wide[LOCAL_ROW:LOCAL_ROW + 1, 128:]
            to_class = jnp.sum(wide[LOCAL_ROW:, 128:], axis=0, keepdims=True) - first_row
            to_class = jnp.where(lane == LOCAL_ROW - 128, to_class, 0.0)
            tl_ref[head, 0:GRID_L, :] = acc
            tl_ref[head, 6:7, :] = first_row
            tl_ref[head, 7:8, :] = to_class
        gmixed_ref[:, cols] = gq.astype(BF16) * jnp.asarray(scale, BF16)
        gmixed_ref[:, slice(width + cols.start, width + cols.stop)] = gk.astype(BF16)
        gmixed_ref[:, slice(2 * width + cols.start, 2 * width + cols.stop)] = gv.astype(BF16)

    def biases(rows):
        add_small(QB, gmixed_ref[rows, :width].astype(F32))
        add_small(VB, gmixed_ref[rows, 2 * width:].astype(F32))

    row_steps(32, biases)
    arrive(pairs, sems, 3)
    for b in range(0, width, BLOCK):
        gnorm[:, b:b + BLOCK] = dot_cols(gmixed_ref[...], w_qkv[b:b + BLOCK, :])

    def norm1(rows):
        grad = gnorm[rows, :]
        xhat, through = norm_back(x_ref[rows, :].astype(F32), grad, vec(N1G))
        add_small(N1G, grad * xhat)
        add_small(N1S, grad)
        gx_ref[rows, :] = (gmid[rows, :] + through).astype(BF16)

    row_steps(32, norm1)


def shape(*dims, dtype=BF16):
    return jax.ShapeDtypeStruct(dims, dtype)


def forward(layer, x, vec, sg, sl, own, other):
    width = x.shape[1]
    hidden = own[2].shape[1]
    heads = sg.shape[0]
    scale = (width // heads) ** (-0.5)
    inside = pl.BlockSpec(memory_space=pltpu.VMEM)
    outside = pl.BlockSpec(memory_space=pl.ANY)
    return pl.pallas_call(
        functools.partial(forward_kernel, layer, scale),
        out_shape=(
            shape(ROWS, width), shape(ROWS, width), shape(ROWS, width), shape(ROWS, width),
            shape(ROWS, width), shape(heads, ROWS, ROWS, dtype=F32), shape(ROWS, width),
            shape(ROWS, width, dtype=F32), shape(ROWS, width, dtype=F32), shape(ROWS, width),
            shape(ROWS, hidden), shape(ROWS, hidden, dtype=F32), shape(ROWS, width, dtype=F32),
        ),
        in_specs=[inside] * 4 + [outside] * 8,
        out_specs=(inside,) * 13,
        scratch_shapes=[pltpu.VMEM(w.shape, BF16) for w in own]
        + [pltpu.VMEM((2, ROWS, ROWS), F32), pltpu.SemaphoreType.DMA((4,))],
        compiler_params=pltpu.CompilerParams(vmem_limit_bytes=60 * 2**20),
        name="layer_forward",
    )(x, vec, sg, sl, *own, *other)


def backward(layer, x, grad, vec, kept, heads, own, other):
    width = x.shape[1]
    hidden = own[2].shape[1]
    scale = (width // heads) ** (-0.5)
    inside = pl.BlockSpec(memory_space=pltpu.VMEM)
    outside = pl.BlockSpec(memory_space=pl.ANY)
    _, n1, q, k, v, probs, merged, branch, middle, n2, act, dact, branch2 = kept
    return pl.pallas_call(
        functools.partial(backward_kernel, layer, scale),
        out_shape=(
            shape(ROWS, width), shape(ROWS, 3 * width), shape(ROWS, width), shape(ROWS, hidden),
            shape(ROWS, width), shape(16, width, dtype=F32),
            shape(heads, 16, LANES_G, dtype=F32), shape(heads, 8, LANES_L, dtype=F32),
        ),
        in_specs=[inside] * 11 + [outside] * 8,
        out_specs=(inside,) * 8,
        scratch_shapes=[pltpu.VMEM(w.shape, BF16) for w in own]
        + [
            pltpu.VMEM((ROWS, width), F32), pltpu.VMEM((ROWS, width), F32),
            pltpu.VMEM((ROWS, width), BF16), pltpu.VMEM((2, ROWS, ROWS), F32),
            pltpu.SemaphoreType.DMA((4,)),
        ],
        compiler_params=pltpu.CompilerParams(vmem_limit_bytes=60 * 2**20),
        name="layer_backward",
    )(x, grad, vec, q, k, v, probs, branch, middle, dact, branch2, *own, *other)


def swapped(value):
    return lax.ppermute(value, "pipe", [(0, 1), (1, 0)])


def body(
    x_global, x_local, cot_global, cot_local, global_count, local_count,
    w_qkv, w_proj, w_fc1, w_fc2,
    norm1_gain, norm1_shift, q_bias, v_bias, proj_bias, scale_attn,
    norm2_gain, norm2_shift, fc1_bias, fc2_bias, scale_mlp,
    table_global, table_local,
):
    section = lax.axis_index("pipe")
    width = x_global.shape[2]
    heads = table_global.shape[2]
    tokens_g, tokens_l = x_global.shape[1], x_local.shape[1]
    own = (w_qkv[0], w_proj[0], w_fc1[0], w_fc2[0])
    other = tuple(swapped(w) for w in own)
    vec = jnp.concatenate(
        [norm1_gain, norm1_shift, q_bias, v_bias, proj_bias, scale_attn, norm2_gain, norm2_shift,
         fc2_bias, scale_mlp, fc1_bias.reshape(-1, width)], 0)
    sg = spread(table_global[0], INDEX_G)
    sl = spread(table_local[0], INDEX_L)
    smalls_own = (vec, sg, sl)
    smalls_other = tuple(swapped(s) for s in smalls_own)

    def by_layer(mine, theirs):
        first = jnp.where(section == 0, mine, theirs)
        second = jnp.where(section == 0, theirs, mine)
        return first, second

    (vec0, vec1), (sg0, sg1), (sl0, sl1) = (by_layer(a, b) for a, b in zip(smalls_own, smalls_other))
    vec0, vec1 = vec0.astype(F32), vec1.astype(F32)

    def packed(array_g, array_l):
        crop_g = lax.dynamic_index_in_dim(array_g, section, 0, keepdims=False)
        crop_l = lax.dynamic_index_in_dim(array_l, section, 0, keepdims=False)
        crop_g = jnp.pad(crop_g, ((0, LOCAL_ROW - tokens_g), (0, 0)))
        crop_l = jnp.pad(crop_l, ((0, ROWS - LOCAL_ROW - tokens_l), (0, 0)))
        return jnp.concatenate([crop_g, crop_l], 0)

    x = packed(x_global, x_local)
    live_g = (global_count[0] > section).astype(BF16)
    live_l = (local_count[0] > section).astype(BF16)
    cot = packed(cot_global * live_g, cot_local * live_l)

    kept0 = forward(0, x, vec0, sg0, sl0, own, other)
    first = kept0[0]
    kept1 = forward(1, first, vec1, sg1, sl1, own, other)
    second = kept1[0]
    back1 = backward(1, first, cot, vec1, kept1, heads, own, other)
    grad_first = back1[0]
    back0 = backward(0, x, grad_first, vec0, kept0, heads, own, other)
    grad_x = back0[0]

    def exchange(layer0, layer1):
        keep = jnp.where(section == 0, layer0, layer1)
        send = jnp.where(section == 0, layer1, layer0)
        return keep, swapped(send)

    def both_crops(keep, came):
        low = jnp.where(section == 0, keep, came)
        high = jnp.where(section == 0, came, keep)
        return (
            jnp.stack([low[:tokens_g], high[:tokens_g]]),
            jnp.stack([low[LOCAL_ROW:LOCAL_ROW + tokens_l], high[LOCAL_ROW:LOCAL_ROW + tokens_l]]),
        )

    out_g, out_l = both_crops(*exchange(first, second))
    crop = jnp.arange(2, dtype=jnp.int32)[:, None, None]
    out_g = jnp.where(crop < global_count[0], out_g, jnp.zeros_like(out_g))
    out_l = jnp.where(crop < local_count[0], out_l, jnp.zeros_like(out_l))
    gin_g, gin_l = both_crops(*exchange(grad_x, grad_first))

    def operand(layer0, layer1):
        return jnp.concatenate(exchange(layer0, layer1), 0)

    lefts = [operand(kept0[i], kept1[i]) for i in (1, 6, 9, 10)]
    rights = [operand(back0[i], back1[i]) for i in (1, 2, 3, 4)]
    shares = [
        lax.psum_scatter(dot_rows(a, b).astype(BF16), "dp", scatter_dimension=0, tiled=True).astype(F32)
        for a, b in zip(lefts, rights)
    ]
    keep, came = [], []
    for i in (5, 6, 7):
        a, b = exchange(back0[i], back1[i])
        keep.append(a)
        came.append(b)
    small, tg, tl = (a + b for a, b in zip(keep, came))
    tg = gather_back(tg, INDEX_G, table_global.shape[1])
    tl = gather_back(tl, INDEX_L, table_local.shape[1])
    small, tg, tl = lax.psum((small, tg, tl), "dp")
    hidden = fc1_bias.shape[1]
    return (
        out_g[None], out_l[None], gin_g[None], gin_l[None],
        *(s[None] for s in shares),
        small[N1G:N1G + 1], small[N1S:N1S + 1], small[QB:QB + 1], small[VB:VB + 1],
        small[PB:PB + 1], small[SA:SA + 1], small[N2G:N2G + 1], small[N2S:N2S + 1],
        small[F1B:F1B + hidden // width].reshape(1, hidden),
        small[F2B:F2B + 1], small[SM:SM + 1],
        tg[None], tl[None],
    )


def solution(mesh):
    three, two = P("pipe", None, None), P("pipe", None)
    rows = P("dp", None, None)
    in_specs = (rows,) * 4 + (P("dp"),) * 2 + (three,) * 4 + (two,) * 11 + (three,) * 2
    crops = P("pipe", "dp", None, None)
    out_specs = (crops,) * 4 + (P("pipe", "dp", None),) * 4 + (two,) * 11 + (three,) * 2
    return jax.shard_map(body, mesh=mesh, in_specs=in_specs, out_specs=out_specs, check_vma=False)
```

time: 2180 us -> 797 us (0.37)
  other arithmetic: 745 us -> 21.8 us
  local copies, waits for them, and re-layouts: 439 us -> 21.4 us
  matrix products: 237 us -> 24 us
  waiting for transfers between devices: 704 us -> 621 us
  Pallas kernels: 0 us -> 79 us
    scatter-add x6 -> x0, other arithmetic: 636 us -> none  [block_backward(): jax.ops.segment_sum(flat_bias, jnp.asarray(lookup.reshape(-1)), num_segme...]
    dot_general x70 -> x8, matrix products: 237 us -> 24 us  [the longest x4 15.8 us: dot_rows(): lax.dot_general(a, b, (((0,), (0,)), ((), ())), preferred_element_type=F32)]
    gather x8 -> x0, local copies, waits for them, and re-layouts: 172 us -> none  [position_bias(): return jnp.transpose(table.astype(jnp.float32)[lookup], (2, 0, 1))]
    reshape x43 -> x3, local copies, waits for them, and re-layouts: 102 us -> 0.03 us  [the longest x2 0.02 us: spread(): return flat.astype(BF16).reshape(heads, *index.shape)]
    reduce_scatter x4, waiting for transfers between devices: 639 us -> 541 us  [body(): lax.psum_scatter(dot_rows(a, b).astype(BF16), 'dp', scatter_dimension=0,...]
    pallas_call x0 -> x4, Pallas kernels: none -> 79 us  [the longest x2 45.9 us: backward(): pl.pallas_call(functools.partial(backward_kernel, layer, scale), out_shap...]
    slice x63 -> x1, local copies, waits for them, and re-layouts: 78.7 us -> 1.65 us  [body(): small[SM:SM + 1]]
    reduce_sum x42 -> x0, other arithmetic: 51.5 us -> none  [the longest x12 15.6 us: layer_norm(): centered = values - jnp.mean(values, axis=-1, keepdims=True)]
  transfers between devices with their start and end apart: 9 -> 25, of which waited for: 5 -> 11; matrix products, arithmetic and copies ran while one was open for 7% -> 7% of each run, Pallas kernels for 0% -> 0%
where the time goes in v1:
time: 797 us; the launch traced here: 791 us
  waiting for transfers between devices  621 us (78%)
  Pallas kernels  79 us (10%)
  matrix products  24 us (3%)
  other arithmetic  21.8 us (3%)
  local copies, waits for them, and re-layouts  21.4 us (3%)
  between operations  16.2 us (2%)
  starting transfers between devices  8.22 us (1%)
    reduce_scatter x4, waiting for transfers between devices, body(): lax.psum_scatter(dot_rows(a, b).astype(BF16), 'dp', scatter_dimension=0,...  541 us
    psum x1, waiting for transfers between devices, body(): small, tg, tl = lax.psum((small, tg, tl), 'dp')  63.8 us
    pallas_call x2, Pallas kernels, backward(): pl.pallas_call(functools.partial(backward_kernel, layer, scale), out_shap...  45.9 us
    pallas_call x2, Pallas kernels, forward(): pl.pallas_call(functools.partial(forward_kernel, layer, scale), out_shape...  33.1 us
    unnamed x80, local copies, waits for them, and re-layouts  16.4 us
  transfers between devices with their start and end apart: 25, of which 11 were waited for; matrix products, arithmetic and copies ran while one was open for 7% of the time, Pallas kernels for 0%

profile of v1, /device:TPU:0, one launch (start us, length us, event | category | flops | bytes accessed | tf_op | source)
XLA Modules:
  0.0 791.1 jit_solution(1515287204224246040)
XLA Ops:
  7.3 0.5 collective-permute-start.5
  8.3 0.7 reduce
  9.0 1.6 concatenate.54
  12.5 1.1 dynamic-slice_multiply_fusion.1
  13.6 1.0 constant_dynamic-slice_fusion
  14.6 1.9 dynamic-slice_multiply_fusion
  16.6 0.6 constant_dynamic-slice_fusion.1
  17.5 0.8 fusion.35.g_ref
  18.3 3.7 fusion.4
  22.1 0.8 fusion.34.x_ref
  23.1 0.6 select_convert_fusion
  23.8 5.1 collective-permute-done.2
  29.2 0.6 broadcast_select_fusion.29
  29.9 0.4 collective-permute-done.1
  30.3 0.8 broadcast_select_fusion.25
  31.2 1.0 copy-done.2
  32.2 16.5 %layer_forward.2 = (bf16[256,768]{1,0:T(8,128)(2,1)}, bf16[256,768]{1,0:T(8,128)(2,1)}, bf16[256,768]{1,0:T(8,128)(2,1)}, bf16[256,768]{1,0:T(8,128)(2,1)}, bf16...) custom-call(bf16[256,768]{1,0:T(8,128)(2,1)} %fusion.34.x_ref, ...), custom_call_target="tpu_custom_call" | custom-call | tf_op jit(solution)/shard_map/layer_forward/pallas_call | solution.py:369
  48.7 16.6 %layer_forward.3 = (bf16[256,768]{1,0:T(8,128)(2,1)}, bf16[256,768]{1,0:T(8,128)(2,1)}, bf16[256,768]{1,0:T(8,128)(2,1)}, bf16[256,768]{1,0:T(8,128)(2,1)}, bf16...) custom-call(bf16[256,768]{1,0:T(8,128)(2,1)} %get-tuple-element.63.x, ...), custom_call_target="tpu_custom_call" | custom-call | tf_op jit(solution)/shard_map/layer_forward/pallas_call | solution.py:369
  65.3 23.0 %layer_backward.2 = (bf16[256,768]{1,0:T(8,128)(2,1)}, bf16[256,2304]{1,0:T(8,128)(2,1)}, bf16[256,768]{1,0:T(8,128)(2,1)}, bf16[256,3072]{1,0:T(8,128)(2,1)}, b...) custom-call(bf16[256,768]{1,0:T(8,128)(2,1)} %get-tuple-element.63.x_ref, ...), custom_call_target="tpu_custom_call" | custom-call | tf_op jit(solution)/shard_map/layer_backward/pallas_call | solution.py:393
  88.3 22.9 %layer_backward.3 = (bf16[256,768]{1,0:T(8,128)(2,1)}, bf16[256,2304]{1,0:T(8,128)(2,1)}, bf16[256,768]{1,0:T(8,128)(2,1)}, bf16[256,3072]{1,0:T(8,128)(2,1)}, b...) custom-call(bf16[256,768]{1,0:T(8,128)(2,1)} %fusion.34.x_ref, ...), custom_call_target="tpu_custom_call" | custom-call | tf_op jit(solution)/shard_map/layer_backward/pallas_call | solution.py:393
  111.3 1.2 collective-permute-start.19
  112.6 0.8 collective-permute-start.17
  113.4 1.1 collective-permute-start.18
  114.5 1.1 broadcast_select_fusion.11
  115.8 0.5 collective-permute-start.11
  116.6 0.6 fusion.46
  117.2 0.6 select_add_fusion.2
  118.4 4.0 fusion
  122.4 0.6 fusion.41
  123.2 0.7 copy-done.26
  123.9 2.9 convolution_convert_fusion.3
  126.9 1.2 copy-done.11
  128.4 0.7 copy-done.17
  129.4 2.4 collective-permute-done.9
  131.8 3.9 convolution_convert_fusion.2
  135.7 1.3 copy-done.6
  137.1 1.7 broadcast_select_fusion.3
  139.5 3.3 collective-permute-done.13
  142.8 4.3 convolution_convert_fusion.1
  147.2 1.3 copy-done.5
  148.6 1.7 broadcast_select_fusion.1
  151.0 3.3 collective-permute-done.16
  154.3 4.6 convolution_convert_fusion
  159.0 1.0 copy-done.3
  160.4 0.4 collective-permute-start.8
  160.9 1.1 collective-permute-done.7
  162.2 1.3 copy.66
  163.6 0.7 copy.67
  164.5 1.3 copy.68
  165.8 0.7 copy.69
  166.6 63.8 %all-reduce.7.cloned.1.call-done = (f32[16,768]{1,0:T(8,128)}, f32[1,732,12]{1,2,0:T(8,128)}, f32[1,124,12]{1,2,0:T(8,128)}) async-done(((f32[16,768]{1,0:T(8,128)}, f32[1,732,12]{1,2,0:T(8,128)}, f32[1,124,12]{1,2,0:T(8,128)}), (f32[16,768]{1,0:T(8,128)}, f32[1,732,12]{1,2,0:T(8,128)}, f32[1,124,12]{1,2,0:T(8,128)})) %all-reduce.7.cloned.1.call-update) | async-done | bytes 90256 | tf_op jit(solution)/shard_map/psum | solution.py:503
  230.4 1.5 copy.70
  231.8 1.3 copy.71
  233.1 0.7 slice_bitcast_fusion.8
  233.9 0.6 copy.78
  234.5 1.7 fusion.54
  236.1 123.4 %reduce-scatter.7.cloned.1.call-done = bf16[48,768]{1,0:T(8,128)(2,1)} async-done(((bf16[768,768]{1,0:T(8,128)(2,1)}), bf16[48,768]{1,0:T(8,128)(2,1)}) %reduce-scatter.7.cloned.1.call-update) | async-done | bytes 73744 | tf_op jit(solution)/shard_map/reduce_scatter | solution.py:492
  359.6 1.6 bitcast_convert_fusion.3
  361.1 136.8 %reduce-scatter.5.cloned.1.call-done = bf16[48,2304]{1,0:T(8,128)(2,1)} async-done(((bf16[768,2304]{1,0:T(8,128)(2,1)}), bf16[48,2304]{1,0:T(8,128)(2,1)}) %reduce-scatter.5.cloned.1.call-update) | async-done | bytes 221200 | tf_op jit(solution)/shard_map/reduce_scatter | solution.py:492
  498.0 1.7 bitcast_convert_fusion.2
  499.7 140.3 %reduce-scatter.9.cloned.1.call-done = bf16[48,3072]{1,0:T(8,128)(2,1)} async-done(((bf16[768,3072]{1,0:T(8,128)(2,1)}), bf16[48,3072]{1,0:T(8,128)(2,1)}) %reduce-scatter.9.cloned.1.call-update) | async-done | bytes 294928 | tf_op jit(solution)/shard_map/reduce_scatter | solution.py:492
  639.9 1.8 bitcast_convert_fusion.1
  641.8 140.5 %reduce-scatter.11.cloned.1.call-done = bf16[192,768]{1,0:T(8,128)(2,1)} async-done(((bf16[3072,768]{1,0:T(8,128)(2,1)}), bf16[192,768]{1,0:T(8,128)(2,1)}) %reduce-scatter.11.cloned.1.call-update) | async-done | bytes 294928 | tf_op jit(solution)/shard_map/reduce_scatter | solution.py:492
  782.3 1.8 bitcast_convert_fusion
  (134 shorter events, 6.4 us)
Async XLA Ops:
  7.2 9.4 %copy-start = (bf16[2,197,768]{2,0,1:T(2,128)(2,1)S(1)}, bf16[2,197,768]{2,0,1:T(2,128)(2,1)}, u32[]{:S(2)}) copy-start(bf16[2,197,768]{2,0,1:T(2,128)(2,1)} %param.27) | copy-start | bytes 1815556
  7.2 223.2 %all-reduce.7.cloned.1.call-start = ((), (), s32[]{:S(2)}) async-start(), calls=%async_computation.8 | async-start | bytes 212992 | tf_op jit(solution)/shard_map/psum | solution.py:503
  7.3 23.9 %collective-permute-start.5 = (bf16[768,3072]{1,0:T(8,128)(2,1)}, bf16[768,3072]{1,0:T(8,128)(2,1)}, u32[]{:S(2)}, u32[]{:S(2)}) collective-permute-start(bf16[768,3072]{1,0:T(8,128)(2,1)} %bitcast.82), channel_id=1, source_target_pairs={{0,16},{16,0},{1,17},{17,1},{2,18},{18,2},{3,19},{19,3},{4,20},{20... | collective-permute-start | bytes 14155784 | tf_op jit(solution)/shard_map/ppermute | solution.py:414
  7.8 23.4 %collective-permute-start.6 = (bf16[3072,768]{1,0:T(8,128)(2,1)}, bf16[3072,768]{1,0:T(8,128)(2,1)}, u32[]{:S(2)}, u32[]{:S(2)}) collective-permute-start(bf16[3072,768]{1,0:T(8,128)(2,1)} %bitcast.87), channel_id=1, source_target_pairs={{0,16},{16,0},{1,17},{17,1},{2,18},{18,2},{3,19},{19,3},{4,20},{20... | collective-permute-start | bytes 14155784 | tf_op jit(solution)/shard_map/ppermute | solution.py:414
  7.9 23.3 %collective-permute-start.3 = (bf16[768,2304]{1,0:T(8,128)(2,1)}, bf16[768,2304]{1,0:T(8,128)(2,1)}, u32[]{:S(2)}, u32[]{:S(2)}) collective-permute-start(bf16[768,2304]{1,0:T(8,128)(2,1)} %bitcast.92), channel_id=1, source_target_pairs={{0,16},{16,0},{1,17},{17,1},{2,18},{18,2},{3,19},{19,3},{4,20},{20... | collective-permute-start | bytes 10616840 | tf_op jit(solution)/shard_map/ppermute | solution.py:414
  10.6 12.3 %collective-permute-start = (bf16[14,768]{1,0:T(8,128)(2,1)S(1)}, bf16[14,768]{1,0:T(8,128)(2,1)S(1)}, u32[]{:S(2)}, u32[]{:S(2)}) collective-permute-start(bf16[14,768]{1,0:T(8,128)(2,1)S(1)} %concatenate.54), channel_id=1, source_target_pairs={{0,16},{16,0},{1,17},{17,1},{2,18},{18,2},{3,19},{19,3},{4,20},{20... | collective-permute-start | bytes 64520 | tf_op jit(solution)/shard_map/ppermute | solution.py:414
  10.8 20.4 %collective-permute-start.4 = (bf16[768,768]{1,0:T(8,128)(2,1)}, bf16[768,768]{1,0:T(8,128)(2,1)S(1)}, u32[]{:S(2)}, u32[]{:S(2)}) collective-permute-start(bf16[768,768]{1,0:T(8,128)(2,1)} %bitcast.97), channel_id=1, source_target_pairs={{0,16},{16,0},{1,17},{17,1},{2,18},{18,2},{3,19},{19,3},{4,20},{20... | collective-permute-start | bytes 3538952 | tf_op jit(solution)/shard_map/ppermute | solution.py:414
  16.5 0.8 copy-start.28
  16.5 0.8 copy-start.30
  16.6 1.7 copy-start.27
  16.6 1.7 copy-start.29
  23.0 5.9 collective-permute-start.2
  28.9 1.4 collective-permute-start.1
  31.1 1.0 copy-start.2
  88.3 23.0 %copy-start.24 = (f32[12,8,128]{2,1,0:T(8,128)S(1)}, f32[12,8,128]{2,1,0:T(8,128)}, u32[]{:S(2)}) copy-start(f32[12,8,128]{2,1,0:T(8,128)} %get-tuple-element.104) | copy-start | bytes 147460
  88.3 24.3 %copy-start.22 = (f32[16,768]{1,0:T(8,128)S(1)}, f32[16,768]{1,0:T(8,128)}, u32[]{:S(2)}) copy-start(f32[16,768]{1,0:T(8,128)} %get-tuple-element.100) | copy-start | bytes 147460
  88.3 25.1 %copy-start.9 = (f32[12,16,512]{2,1,0:T(8,128)S(1)}, f32[12,16,512]{2,1,0:T(8,128)}, u32[]{:S(2)}) copy-start(f32[12,16,512]{2,1,0:T(8,128)} %get-tuple-element.102) | copy-start | bytes 1179652
  111.2 3.3 copy-start.21
  111.3 4.5 copy-start.19
  111.3 4.5 copy-start.20
  111.3 5.0 collective-permute-start.19
  112.6 4.7 collective-permute-start.17
  113.4 4.4 collective-permute-start.18
  114.5 1.8 copy-start.25
  115.6 1.6 copy-start.23
  115.6 2.3 copy-start.10
  115.6 7.5 collective-permute-start.12
  115.8 7.4 collective-permute-start.11
  123.1 236.5 %reduce-scatter.7.cloned.1.call-start = ((), (), s32[]{:S(2)}) async-start(), calls=%async_computation.5 | async-start | bytes 1253376 | tf_op jit(solution)/shard_map/reduce_scatter | solution.py:492
  123.2 0.7 copy-start.26
  123.9 3.0 copy-start.12
  126.8 1.3 copy-start.11
  126.9 371.1 %reduce-scatter.5.cloned.1.call-start = ((), (), s32[]{:S(2)}) async-start(), calls=%async_computation.4 | async-start | bytes 3760128 | tf_op jit(solution)/shard_map/reduce_scatter | solution.py:492
  128.1 1.0 copy-start.17
  128.1 1.1 copy-start.18
  128.3 3.5 collective-permute-start.10
  129.3 2.5 collective-permute-start.9
  135.7 1.4 copy-start.6
  135.7 504.2 %reduce-scatter.9.cloned.1.call-start = ((), (), s32[]{:S(2)}) async-start(), calls=%async_computation.6 | async-start | bytes 5013504 | tf_op jit(solution)/shard_map/reduce_scatter | solution.py:492
  137.1 1.9 copy-start.14
  137.1 1.9 copy-start.16
  138.8 4.0 collective-permute-start.14
  139.1 3.7 collective-permute-start.13
  147.2 1.4 copy-start.5
  147.2 635.1 %reduce-scatter.11.cloned.1.call-start = ((), (), s32[]{:S(2)}) async-start(), calls=%async_computation.7 | async-start | bytes 5013504 | tf_op jit(solution)/shard_map/reduce_scatter | solution.py:492
  148.6 1.9 copy-start.13
  148.6 1.9 copy-start.15
  150.3 4.0 collective-permute-start.15
  150.6 3.8 collective-permute-start.16
  159.0 1.0 copy-start.3
  159.0 1.1 copy-start.8
  159.0 1.4 copy-start.4
  159.0 1.4 copy-start.7
  160.1 1.8 collective-permute-start.7
  160.4 3.9 collective-permute-start.8
  165.8 618.3 %copy-start.1 = (bf16[2,197,768]{2,0,1:T(2,128)(2,1)S(1)}, bf16[2,197,768]{2,0,1:T(2,128)(2,1)}, u32[]{:S(2)}) copy-start(bf16[2,197,768]{2,0,1:T(2,128)(2,1)} %param.27) | copy-start | bytes 1815556
Sparse Core Ops, SparseCore 0:
  123.2 107.1 all-reduce.6
  235.1 124.3 reduce-scatter.6
  364.7 133.2 reduce-scatter.4
  503.0 136.9 reduce-scatter.8
  645.8 136.4 reduce-scatter.10

commit v2 on v1

--- a/solution.py
+++ b/solution.py
@@ -410,6 +410,340 @@
     )(x, grad, vec, q, k, v, probs, branch, middle, dact, branch2, *own, *other)
 
 
+MESH = pl.DeviceIdType.MESH
+SIDE = 2
+
+
+def remote(source, target, sent, came, **device):
+    return pltpu.make_async_remote_copy(
+        src_ref=source, dst_ref=target, send_sem=sent, recv_sem=came,
+        device_id=device, device_id_type=MESH,
+    )
+
+
+def add_rows(total, start, extra, count):
+    def one(i, carry):
+        rows = pl.ds(pl.multiple_of(start + i * 16, 16), 16)
+        here = pl.ds(pl.multiple_of(i * 16, 16), 16)
+        total[rows, :] = (total[rows, :].astype(F32) + extra[here, :].astype(F32)).astype(BF16)
+        return carry
+
+    lax.fori_loop(0, count // 16, one, 0)
+
+
+def scatter_kernel(count, *refs):
+    first, second = refs[:8], refs[8:16]
+    out_qkv, out_proj, out_fc1, out_fc2 = refs[16:20]
+    held = refs[20:28]
+    sum_a, sum_b, sum_c = refs[28:31]
+    in_a1, in_a2, in_a3, in_b1, in_b2, in_b3, in_c1, in_c2, in_c3 = refs[31:40]
+    local_sem, swap_sent, swap_came = refs[40:43]
+    sent, came = refs[43:52], refs[52:61]
+    depth = count // (SIDE * SIDE)
+    width = held[0].shape[1]
+    section = lax.axis_index("pipe")
+    place = lax.axis_index("dp")
+    x = place % SIDE
+    y = (place // SIDE) % SIDE
+    z = place // (SIDE * SIDE)
+
+    def index(zz, yy, xx):
+        return (zz * SIDE + yy) * SIDE + xx
+
+    across_x, across_y = index(z, y, 1 - x), index(z, 1 - y, x)
+
+    barrier = pltpu.get_barrier_semaphore()
+    pl.semaphore_signal(barrier, inc=1, device_id={"pipe": 1 - section}, device_id_type=MESH)
+    for peer in (across_x, across_y):
+        pl.semaphore_signal(barrier, inc=1, device_id={"dp": peer}, device_id_type=MESH)
+    for step in range(1, depth):
+        peer = index((z + step) % depth, y, x)
+        pl.semaphore_signal(barrier, inc=1, device_id={"dp": peer}, device_id_type=MESH)
+    pl.semaphore_wait(barrier, 3 + depth - 1)
+
+    order = (0, 4, 2, 6, 1, 5, 3, 7)
+    for i in order:
+        mine = held[i].at[pl.ds(0, ROWS), :]
+        theirs = held[i].at[pl.ds(ROWS, ROWS), :]
+
+        @pl.when(section == 0)
+        def _():
+            remote(second[i], theirs, swap_sent.at[i], swap_came.at[i], pipe=1 - section).start()
+            pltpu.make_async_copy(first[i], mine, local_sem.at[i]).start()
+
+        @pl.when(section != 0)
+        def _():
+            remote(first[i], theirs, swap_sent.at[i], swap_came.at[i], pipe=1 - section).start()
+            pltpu.make_async_copy(second[i], mine, local_sem.at[i]).start()
+
+    def operands(*numbers):
+        for i in numbers:
+            mine = held[i].at[pl.ds(0, ROWS), :]
+            theirs = held[i].at[pl.ds(ROWS, ROWS), :]
+            pltpu.make_async_copy(first[i], mine, local_sem.at[i]).wait()
+            remote(first[i], theirs, swap_sent.at[i], swap_came.at[i], pipe=1 - section).wait_recv()
+
+    def product(left, right, total, offset):
+        def one(i, carry):
+            start = pl.multiple_of(i * BLOCK, BLOCK)
+            rows = left[:, pl.ds(start, BLOCK)]
+            for b in range(0, right.shape[1], width):
+                part = dot_rows(rows, right[:, b:b + width])
+                total[pl.ds(start, BLOCK), offset + b:offset + b + width] = part.astype(BF16)
+            return carry
+
+        lax.fori_loop(0, left.shape[1] // BLOCK, one, 0)
+
+    def target(k):
+        low = jnp.where(k < depth - 1 - z, depth - 1 - k, k - (depth - 1 - z))
+        high = jnp.where(k < z, k, depth - 1 - (k - z))
+        return jnp.where(z < depth // 2, low, high)
+
+    targets = [target(k) for k in range(depth)]
+    ups = [jnp.where(targets[k] > z, 1, 0) for k in range(depth - 1)]
+    starts_line = (z == 0) | (z == depth - 1)
+
+    def chunk(total, zz, yy, xx):
+        rows = total.shape[0] // count
+        return pl.ds(pl.multiple_of(index(zz, yy, xx) * rows, rows), rows)
+
+    def accumulate(total, zz, yy, xx, extra):
+        rows = total.shape[0] // count
+        add_rows(total, pl.multiple_of(index(zz, yy, xx) * rows, rows), extra, rows)
+
+    def line_copy(total, slots, group, k, c, yy, xx, width_of):
+        up = ups[k]
+        slot = (targets[k] + up) * width_of + c
+        number = k * width_of + c
+        source = total.at[chunk(total, targets[k], yy, xx), :]
+        peer = index(z + 2 * up - 1, y, x)
+        return slot, remote(
+            source, slots.at[slot], sent[group].at[number], came[group].at[slot], dp=peer
+        )
+
+    def line_receive(total, slots, group, k, slot, yy, xx):
+        here = slots.at[slot]
+        peer = index(z + 1 - 2 * ups[k], y, x)
+        remote(here, here, sent[group].at[0], came[group].at[slot], dp=peer).wait_recv()
+        accumulate(total, targets[k], yy, xx, here)
+
+    c_parts = ((1 - y, 1 - x), (y, 1 - x), (1 - y, x), (y, x))
+    operands(0, 4)
+    product(held[0], held[4], sum_c, 0)
+
+    @pl.when(starts_line)
+    def _():
+        for k in range(depth - 1):
+            for c, (yy, xx) in enumerate(c_parts):
+                line_copy(sum_c, in_c1, 6, k, c, yy, xx, 4)[1].start()
+
+    def line_c(k, c):
+        yy, xx = c_parts[c]
+
+        @pl.when(jnp.logical_not(starts_line))
+        def _():
+            slot, copy = line_copy(sum_c, in_c1, 6, k, c, yy, xx, 4)
+            line_receive(sum_c, in_c1, 6, k, slot, yy, xx)
+            copy.start()
+
+    def first_copy(which, i):
+        yy_other = i < depth
+        zz = targets[i % depth]
+        if which == 0:
+            where = (zz, 1 - y if yy_other else y, 1 - x)
+            total, slots, peer = sum_a, in_a1, across_x
+        else:
+            where = (zz, 1 - y, 1 - x if yy_other else x)
+            total, slots, peer = sum_b, in_b1, across_y
+        source = total.at[chunk(total, *where), :]
+        group = 0 if which == 0 else 3
+        return remote(source, slots.at[i], sent[group].at[i], came[group].at[i], dp=peer)
+
+    def second_copy(which, i):
+        where = (targets[i], 1 - y, x) if which == 0 else (targets[i], y, 1 - x)
+        total, slots, peer = (sum_a, in_a2, across_y) if which == 0 else (sum_b, in_b2, across_x)
+        group = 1 if which == 0 else 4
+        source = total.at[chunk(total, *where), :]
+        return remote(source, slots.at[i], sent[group].at[i], came[group].at[i], dp=peer)
+
+    def first_receive(which, i):
+        first_copy(which, i).wait_recv()
+        zz = targets[i % depth]
+        if which == 0:
+            where = (zz, 1 - y if i < depth else y, x)
+            accumulate(sum_a, *where, in_a1.at[i])
+        else:
+            where = (zz, y, 1 - x if i < depth else x)
+            accumulate(sum_b, *where, in_b1.at[i])
+        if i < depth:
+            second_copy(which, i).start()
+
+    def line(which, k):
+        total, came_in, slots = (sum_a, in_a2, in_a3) if which == 0 else (sum_b, in_b2, in_b3)
+        group = 2 if which == 0 else 5
+        second_copy(which, k).wait_recv()
+        accumulate(total, targets[k], y, x, came_in.at[k])
+        if k < depth - 1:
+            slot, copy = line_copy(total, slots, group, k, 0, y, x, 1)
+
+            @pl.when(jnp.logical_not(starts_line))
+            def _():
+                line_receive(total, slots, group, k, slot, y, x)
+
+            copy.start()
+
+    def line_end(total, slots, group, slot_below, slot_above, add):
+        @pl.when(z > 0)
+        def _():
+            here = slots.at[slot_below]
+            peer = index(z - 1, y, x)
+            remote(here, here, sent[group].at[0], came[group].at[slot_below], dp=peer).wait_recv()
+            add(here)
+
+        @pl.when(z < depth - 1)
+        def _():
+            here = slots.at[slot_above]
+            peer = index(z + 1, y, x)
+            remote(here, here, sent[group].at[0], came[group].at[slot_above], dp=peer).wait_recv()
+            add(here)
+
+    def finish(which):
+        total, slots, group = (sum_a, in_a3, 2) if which == 0 else (sum_b, in_b3, 5)
+        own = chunk(total, z, y, x)
+        if which == 0:
+            hidden = out_fc1.shape[1]
+            out_fc1[...] = total[own, :hidden].astype(F32)
+            out_proj[...] = total[own, hidden:].astype(F32)
+
+            def add(here):
+                out_fc1[...] += here[:, :hidden].astype(F32)
+                out_proj[...] += here[:, hidden:].astype(F32)
+        else:
+            out_fc2[...] = total[own, :].astype(F32)
+
+            def add(here):
+                out_fc2[...] += here[...].astype(F32)
+
+        line_end(total, slots, group, z + 1, z, add)
+
+    operands(2, 6, 1, 5)
+    product(held[2], held[6], sum_a, 0)
+    product(held[1], held[5], sum_a, held[6].shape[1])
+    for i in range(2 * depth):
+        first_copy(0, i).start()
+    operands(3, 7)
+    product(held[3], held[7], sum_b, 0)
+    for i in range(2 * depth):
+        first_copy(1, i).start()
+
+    for i in range(depth):
+        first_receive(1, i)
+        first_receive(0, i)
+        if i < 4:
+            line_c(0, i)
+    for c in range(depth, 4):
+        line_c(0, c)
+    for i in range(depth):
+        first_receive(1, depth + i)
+        first_receive(0, depth + i)
+        if i < 4 and depth > 2:
+            line_c(1, i)
+    for k in range(2, depth - 1):
+        for c in range(4):
+            line_c(k, c)
+
+    def end_c(c):
+        yy, xx = c_parts[c]
+        line_end(
+            sum_c, in_c1, 6, (z + 1) * 4 + c, z * 4 + c,
+            lambda here: accumulate(sum_c, z, yy, xx, here),
+        )
+
+    def copy_c2(c):
+        yy, xx = c_parts[c]
+        source = sum_c.at[chunk(sum_c, z, yy, xx), :]
+        return remote(source, in_c2.at[c], sent[7].at[c], came[7].at[c], dp=across_x)
+
+    def copy_c3():
+        source = sum_c.at[chunk(sum_c, z, 1 - y, x), :]
+        return remote(source, in_c3, sent[8].at[0], came[8].at[0], dp=across_y)
+
+    line(1, 0)
+    line(0, 0)
+    for c in range(2):
+        end_c(c)
+        copy_c2(c).start()
+    end_c(2)
+    end_c(3)
+    for k in range(1, depth - 1):
+        line(1, k)
+        line(0, k)
+        if k == 1:
+            copy_c2(0).wait_recv()
+            accumulate(sum_c, z, 1 - y, x, in_c2.at[0])
+            copy_c3().start()
+            copy_c2(1).wait_recv()
+            accumulate(sum_c, z, y, x, in_c2.at[1])
+    line(1, depth - 1)
+    line(0, depth - 1)
+    copy_c3().wait_recv()
+    out_qkv[...] = sum_c[chunk(sum_c, z, y, x), :].astype(F32) + in_c3[...].astype(F32)
+    finish(1)
+    finish(0)
+
+    for i in order:
+        theirs = held[i].at[pl.ds(ROWS, ROWS), :]
+        remote(first[i], theirs, swap_sent.at[i], swap_came.at[i], pipe=1 - section).wait_send()
+    for which in range(2):
+        for i in range(2 * depth):
+            first_copy(which, i).wait_send()
+        for i in range(depth):
+            second_copy(which, i).wait_send()
+        for k in range(depth - 1):
+            total, slots = (sum_a, in_a3) if which == 0 else (sum_b, in_b3)
+            line_copy(total, slots, 2 if which == 0 else 5, k, 0, y, x, 1)[1].wait_send()
+    for k in range(depth - 1):
+        for c, (yy, xx) in enumerate(c_parts):
+            line_copy(sum_c, in_c1, 6, k, c, yy, xx, 4)[1].wait_send()
+    copy_c2(0).wait_send()
+    copy_c2(1).wait_send()
+    copy_c3().wait_send()
+
+
+def scattered(count, first, second):
+    widths = [a.shape[1] for a in first]
+    n1, merged, n2, act, gmixed, gbranch, ghidden, gb2 = widths
+    depth = count // (SIDE * SIDE)
+    inside = pl.BlockSpec(memory_space=pltpu.VMEM)
+    outside = pl.BlockSpec(memory_space=pl.ANY)
+    rows, rows_b = n1 // count, act // count
+    cols_a = ghidden + gbranch
+    dma = pltpu.SemaphoreType.DMA
+    copies = (2 * depth, depth, depth - 1, 2 * depth, depth, depth - 1, 4 * (depth - 1), 2, 1)
+    arrivals = (2 * depth, depth, depth + 1, 2 * depth, depth, depth + 1, 4 * (depth + 1), 2, 1)
+    return pl.pallas_call(
+        functools.partial(scatter_kernel, count),
+        out_shape=(
+            shape(rows, gmixed, dtype=F32), shape(rows, gbranch, dtype=F32),
+            shape(rows, ghidden, dtype=F32), shape(rows_b, gb2, dtype=F32),
+        ),
+        in_specs=[outside] * 16,
+        out_specs=(inside,) * 4,
+        scratch_shapes=[pltpu.VMEM((2 * ROWS, w), BF16) for w in widths]
+        + [pltpu.VMEM((n1, cols_a), BF16), pltpu.VMEM((act, gb2), BF16), pltpu.VMEM((n1, gmixed), BF16)]
+        + [pltpu.VMEM((slots, rows, cols_a), BF16) for slots in (2 * depth, depth, depth + 1)]
+        + [pltpu.VMEM((slots, rows_b, gb2), BF16) for slots in (2 * depth, depth, depth + 1)]
+        + [pltpu.VMEM((4 * (depth + 1), rows, gmixed), BF16), pltpu.VMEM((2, rows, gmixed), BF16),
+           pltpu.VMEM((rows, gmixed), BF16)]
+        + [dma((8,)), dma((8,)), dma((8,))]
+        + [dma((c,)) for c in copies] + [dma((a,)) for a in arrivals],
+        compiler_params=pltpu.CompilerParams(
+            vmem_limit_bytes=60 * 2**20, collective_id=1, has_side_effects=True
+        ),
+        name="gradient_scatter",
+    )(*first, *second)
+
+
 def swapped(value):
     return lax.ppermute(value, "pipe", [(0, 1), (1, 0)])
 
@@ -483,15 +817,19 @@
     out_l = jnp.where(crop < local_count[0], out_l, jnp.zeros_like(out_l))
     gin_g, gin_l = both_crops(*exchange(grad_x, grad_first))
 
-    def operand(layer0, layer1):
-        return jnp.concatenate(exchange(layer0, layer1), 0)
-
-    lefts = [operand(kept0[i], kept1[i]) for i in (1, 6, 9, 10)]
-    rights = [operand(back0[i], back1[i]) for i in (1, 2, 3, 4)]
-    shares = [
-        lax.psum_scatter(dot_rows(a, b).astype(BF16), "dp", scatter_dimension=0, tiled=True).astype(F32)
-        for a, b in zip(lefts, rights)
-    ]
+    count = lax.axis_size("dp")
+    first_operands = [kept0[i] for i in (1, 6, 9, 10)] + [back0[i] for i in (1, 2, 3, 4)]
+    second_operands = [kept1[i] for i in (1, 6, 9, 10)] + [back1[i] for i in (1, 2, 3, 4)]
+    if count % (2 * SIDE * SIDE) == 0 and width % (16 * count) == 0:
+        shares = scattered(count, first_operands, second_operands)
+    else:
+        whole = [jnp.concatenate(exchange(a, b), 0) for a, b in zip(first_operands, second_operands)]
+        shares = [
+            lax.psum_scatter(
+                dot_rows(a, b).astype(BF16), "dp", scatter_dimension=0, tiled=True
+            ).astype(F32)
+            for a, b in zip(whole[:4], whole[4:])
+        ]
     keep, came = [], []
     for i in (5, 6, 7):
         a, b = exchange(back0[i], back1[i])

time: 797 us -> 387 us (0.49)
  waiting for transfers between devices: 621 us -> 108 us
  Pallas kernels: 79 us -> 217 us
  matrix products: 24 us -> 8.21 us
  other arithmetic: 21.8 us -> 9.92 us
    reduce_scatter x4 -> x0, waiting for transfers between devices: 541 us -> none  [body(): lax.psum_scatter(dot_rows(a, b).astype(BF16), 'dp', scatter_dimension=0,...]
    pallas_call x0 -> x1, Pallas kernels: none -> 138 us  [scattered(): pl.pallas_call(functools.partial(scatter_kernel, count), out_shape=(shape...]
    psum x1, waiting for transfers between devices: 63.8 us -> 102 us  [body(): small, tg, tl = lax.psum((small, tg, tl), 'dp')]
    dot_general x4 -> x0, matrix products: 15.8 us -> none  [dot_rows(): lax.dot_general(a, b, (((0,), (0,)), ((), ())), preferred_element_type=F32)]
    ppermute x20 -> x12, waiting for transfers between devices: 15.6 us -> 5.62 us  [swapped(): return lax.ppermute(value, 'pipe', [(0, 1), (1, 0)])]
    unnamed x80 -> x64, local copies, waits for them, and re-layouts: 16.4 us -> 12.9 us
  transfers between devices with their start and end apart: 25 -> 13, of which waited for: 11 -> 3; matrix products, arithmetic and copies ran while one was open for 7% -> 5% of each run, Pallas kernels for 0% -> 0%
where the time goes in v2:
time: 387 us; the launch traced here: 381 us
  Pallas kernels  217 us (56%)
  waiting for transfers between devices  108 us (28%)
  local copies, waits for them, and re-layouts  17.9 us (5%)
  between operations  16.4 us (4%)
  other arithmetic  9.92 us (3%)
  matrix products  8.21 us (2%)
    pallas_call x1, Pallas kernels, scattered(): pl.pallas_call(functools.partial(scatter_kernel, count), out_shape=(shape...  138 us
    psum x1, waiting for transfers between devices, body(): small, tg, tl = lax.psum((small, tg, tl), 'dp')  102 us
    pallas_call x2, Pallas kernels, backward(): pl.pallas_call(functools.partial(backward_kernel, layer, scale), out_shap...  46 us
    pallas_call x2, Pallas kernels, forward(): pl.pallas_call(functools.partial(forward_kernel, layer, scale), out_shape...  33.1 us
    unnamed x64, local copies, waits for them, and re-layouts  12.9 us
  transfers between devices with their start and end apart: 13, of which 3 were waited for; matrix products, arithmetic and copies ran while one was open for 5% of the time, Pallas kernels for 0%

profile of v2, /device:TPU:0, one launch (start us, length us, event | category | flops | bytes accessed | tf_op | source)
XLA Modules:
  0.0 380.9 jit_solution(8349266970825137802)
XLA Ops:
  7.2 0.0 copy-start
  7.3 0.0 all-reduce.7.cloned.1.call-start
  7.3 0.5 collective-permute-start.5
  7.8 0.1 collective-permute-start.6
  7.9 0.4 collective-permute-start.3
  8.3 0.7 reduce
  9.1 1.6 concatenate.30
  10.7 0.1 collective-permute-start
  10.8 0.4 collective-permute-start.4
  12.6 1.1 dynamic-slice_multiply_fusion.1
  13.6 1.0 constant_dynamic-slice_fusion
  14.7 1.9 dynamic-slice_multiply_fusion
  16.6 0.6 constant_dynamic-slice_fusion.1
  17.3 0.8 fusion.11.g_ref
  18.1 0.8 fusion.10.x_ref
  18.8 0.2 convolution_convert_fusion
  19.1 3.7 fusion.4
  22.9 0.1 copy.76
  23.0 0.1 collective-permute-start.2
  23.1 0.6 select_convert_fusion
  23.8 5.1 %collective-permute-done.2 = bf16[12,8,128]{2,1,0:T(8,128)(2,1)S(1)} collective-permute-done((bf16[12,8,128]{2,1,0:T(8,128)(2,1)S(1)}, bf16[12,8,128]{2,1,0:T(8,128)(2,1)S(1)}, u32[]{:S(2)}, u32[]{:S(2)}) %collective-permute-start.2) | collective-permute-done | bytes 24608 | tf_op jit(solution)/shard_map/ppermute | solution.py:748
  28.9 0.4 collective-permute-start.1
  29.3 0.6 broadcast_select_fusion.13
  29.9 0.4 collective-permute-done.1
  30.4 0.8 broadcast_select_fusion.9
  31.2 1.0 copy-done.2
  32.2 16.5 %layer_forward.2 = (bf16[256,768]{1,0:T(8,128)(2,1)}, bf16[256,768]{1,0:T(8,128)(2,1)}, bf16[256,768]{1,0:T(8,128)(2,1)}, bf16[256,768]{1,0:T(8,128)(2,1)}, bf16...) custom-call(bf16[256,768]{1,0:T(8,128)(2,1)} %fusion.10.x_ref, ...), custom_call_target="tpu_custom_call" | custom-call | tf_op jit(solution)/shard_map/layer_forward/pallas_call | solution.py:369
  48.7 16.7 %layer_forward.3 = (bf16[256,768]{1,0:T(8,128)(2,1)}, bf16[256,768]{1,0:T(8,128)(2,1)}, bf16[256,768]{1,0:T(8,128)(2,1)}, bf16[256,768]{1,0:T(8,128)(2,1)}, bf16...) custom-call(bf16[256,768]{1,0:T(8,128)(2,1)} %get-tuple-element.67.x, ...), custom_call_target="tpu_custom_call" | custom-call | tf_op jit(solution)/shard_map/layer_forward/pallas_call | solution.py:369
  65.4 23.1 %layer_backward.2 = (bf16[256,768]{1,0:T(8,128)(2,1)}, bf16[256,2304]{1,0:T(8,128)(2,1)}, bf16[256,768]{1,0:T(8,128)(2,1)}, bf16[256,3072]{1,0:T(8,128)(2,1)}, b...) custom-call(bf16[256,768]{1,0:T(8,128)(2,1)} %get-tuple-element.67.x_ref, ...), custom_call_target="tpu_custom_call" | custom-call | tf_op jit(solution)/shard_map/layer_backward/pallas_call | solution.py:393
  88.4 22.9 %layer_backward.3 = (bf16[256,768]{1,0:T(8,128)(2,1)}, bf16[256,2304]{1,0:T(8,128)(2,1)}, bf16[256,768]{1,0:T(8,128)(2,1)}, bf16[256,3072]{1,0:T(8,128)(2,1)}, b...) custom-call(bf16[256,768]{1,0:T(8,128)(2,1)} %fusion.10.x_ref, ...), custom_call_target="tpu_custom_call" | custom-call | tf_op jit(solution)/shard_map/layer_backward/pallas_call | solution.py:393
  111.4 137.9 %gradient_scatter.1 = (f32[48,2304]{1,0:T(8,128)}, f32[48,768]{1,0:T(8,128)}, f32[48,3072]{1,0:T(8,128)}, f32[192,768]{1,0:T(8,128)}) custom-call(bf16[256,768]{1,0:T(8,128)(2,1)} %get-tuple-element.87.refs_0_, bf16[256,768]{1,0:T(8,128)(2,1)} %get-tuple-element.88.refs_1_, bf16[256,768]{1,0:T(8,128)(2,1)} %get-tuple-element.89.refs_2_, ...), custom_call_target="tpu_custom_call" | custom-call | tf_op jit(solution)/shard_map/gradient_scatter/pallas_call | solution.py:724
  249.4 0.1 collective-permute-start.11
  249.5 0.5 collective-permute-start.9
  250.2 0.1 collective-permute-start.7
  250.3 0.5 collective-permute-start.8
  250.7 0.1 broadcast_select_fusion.8
  250.8 0.1 collective-permute-start.10
  251.0 0.2 fusion.9
  251.2 0.6 fusion.22
  251.9 0.6 select_add_fusion.2
  252.5 0.1 broadcast_select_fusion.5
  252.6 0.1 broadcast_select_fusion.1
  252.8 0.1 maximum_select_fusion
  252.9 0.1 maximum_select_fusion.1
  253.0 1.3 copy.66
  254.3 0.7 copy.67
  255.0 0.1 maximum_bitcast_fusion
  255.1 1.3 copy.68
  256.4 0.1 select_add_fusion
  256.6 0.3 copy.79
  257.0 4.0 %fusion = f32[732,24]{0,1:T(8,128)S(1)} fusion(s32[8192]{0:T(1024)S(1)} %copy-done.19, bf16[12,8192]{1,0:T(8,128)(2,1)S(1)} %get-tuple-element.181, bf16[12,8192]{1,0:T(8,128)(2,1)S(1)} %get-tuple-element.182), kind=kOutput, calls=%fused_computation.1 | convolution fusion | flops 294617088 | bytes 496256 | tf_op jit(solution)/shard_map/dot_general | solution.py:64
  261.0 0.6 fusion.17
  261.6 0.0 all-reduce.7.cloned.1.call-update
  261.7 0.7 copy.69
  262.4 102.3 %all-reduce.7.cloned.1.call-done = (f32[16,768]{1,0:T(8,128)}, f32[1,732,12]{1,2,0:T(8,128)}, f32[1,124,12]{1,2,0:T(8,128)}) async-done(((f32[16,768]{1,0:T(8,128)}, f32[1,732,12]{1,2,0:T(8,128)}, f32[1,124,12]{1,2,0:T(8,128)}), (f32[16,768]{1,0:T(8,128)}, f32[1,732,12]{1,2,0:T(8,128)}, f32[1,124,12]{1,2,0:T(8,128)})) %all-reduce.7.cloned.1.call-update) | async-done | bytes 90256 | tf_op jit(solution)/shard_map/psum | solution.py:841
  364.8 0.7 slice_bitcast_fusion.8
  365.5 1.7 fusion.26
  367.2 1.5 copy.70
  368.6 1.3 copy.71
  369.9 0.6 copy.78
  370.5 0.8 copy.98
  371.3 0.7 copy.99
  372.0 0.8 copy.100
  372.8 0.8 copy.101
  (75 shorter events, 0.6 us)
Async XLA Ops:
  7.2 9.4 %copy-start = (bf16[2,197,768]{2,0,1:T(2,128)(2,1)S(1)}, bf16[2,197,768]{2,0,1:T(2,128)(2,1)}, u32[]{:S(2)}) copy-start(bf16[2,197,768]{2,0,1:T(2,128)(2,1)} %param.27) | copy-start | bytes 1815556
  7.2 11.6 %copy-start.20 = (s32[1024]{0:T(1024)S(1)}, s32[1024]{0:T(1024)}, u32[]{:S(2)}) copy-start(s32[1024]{0:T(1024)} %constant.63) | copy-start | bytes 12292
  7.2 11.8 %copy-start.19 = (s32[8192]{0:T(1024)S(1)}, s32[8192]{0:T(1024)}, u32[]{:S(2)}) copy-start(s32[8192]{0:T(1024)} %constant.62) | copy-start | bytes 98308
  7.2 11.6 %copy-start.18 = (bf16[1,124,12]{1,2,0:T(8,128)(2,1)S(1)}, bf16[1,124,12]{1,2,0:T(8,128)(2,1)}, u32[]{:S(2)}) copy-start(bf16[1,124,12]{1,2,0:T(8,128)(2,1)} %param.49) | copy-start | bytes 8932
  7.2 11.8 %copy-start.17 = (bf16[1,732,12]{1,2,0:T(8,128)(2,1)S(1)}, bf16[1,732,12]{1,2,0:T(8,128)(2,1)}, u32[]{:S(2)}) copy-start(bf16[1,732,12]{1,2,0:T(8,128)(2,1)} %param.48) | copy-start | bytes 52708
  7.3 357.5 %all-reduce.7.cloned.1.call-start = ((), (), s32[]{:S(2)}) async-start(), calls=%async_computation | async-start | bytes 212992 | tf_op jit(solution)/shard_map/psum | solution.py:841
  7.3 23.9 %collective-permute-start.5 = (bf16[768,3072]{1,0:T(8,128)(2,1)}, bf16[768,3072]{1,0:T(8,128)(2,1)}, u32[]{:S(2)}, u32[]{:S(2)}) collective-permute-start(bf16[768,3072]{1,0:T(8,128)(2,1)} %bitcast.74), channel_id=1, source_target_pairs={{0,16},{16,0},{1,17},{17,1},{2,18},{18,2},{3,19},{19,3},{4,20},{20... | collective-permute-start | bytes 14155784 | tf_op jit(solution)/shard_map/ppermute | solution.py:748
  7.8 23.4 %collective-permute-start.6 = (bf16[3072,768]{1,0:T(8,128)(2,1)}, bf16[3072,768]{1,0:T(8,128)(2,1)}, u32[]{:S(2)}, u32[]{:S(2)}) collective-permute-start(bf16[3072,768]{1,0:T(8,128)(2,1)} %bitcast.79), channel_id=1, source_target_pairs={{0,16},{16,0},{1,17},{17,1},{2,18},{18,2},{3,19},{19,3},{4,20},{20... | collective-permute-start | bytes 14155784 | tf_op jit(solution)/shard_map/ppermute | solution.py:748
  7.9 23.3 %collective-permute-start.3 = (bf16[768,2304]{1,0:T(8,128)(2,1)}, bf16[768,2304]{1,0:T(8,128)(2,1)}, u32[]{:S(2)}, u32[]{:S(2)}) collective-permute-start(bf16[768,2304]{1,0:T(8,128)(2,1)} %bitcast.84), channel_id=1, source_target_pairs={{0,16},{16,0},{1,17},{17,1},{2,18},{18,2},{3,19},{19,3},{4,20},{20... | collective-permute-start | bytes 10616840 | tf_op jit(solution)/shard_map/ppermute | solution.py:748
  10.7 12.3 %collective-permute-start = (bf16[14,768]{1,0:T(8,128)(2,1)S(1)}, bf16[14,768]{1,0:T(8,128)(2,1)S(1)}, u32[]{:S(2)}, u32[]{:S(2)}) collective-permute-start(bf16[14,768]{1,0:T(8,128)(2,1)S(1)} %concatenate.30), channel_id=1, source_target_pairs={{0,16},{16,0},{1,17},{17,1},{2,18},{18,2},{3,19},{19,3},{4,20},{20... | collective-permute-start | bytes 64520 | tf_op jit(solution)/shard_map/ppermute | solution.py:748
  10.8 20.4 %collective-permute-start.4 = (bf16[768,768]{1,0:T(8,128)(2,1)}, bf16[768,768]{1,0:T(8,128)(2,1)S(1)}, u32[]{:S(2)}, u32[]{:S(2)}) collective-permute-start(bf16[768,768]{1,0:T(8,128)(2,1)} %bitcast.89), channel_id=1, source_target_pairs={{0,16},{16,0},{1,17},{17,1},{2,18},{18,2},{3,19},{19,3},{4,20},{20... | collective-permute-start | bytes 3538952 | tf_op jit(solution)/shard_map/ppermute | solution.py:748
  23.0 5.9 %collective-permute-start.2 = (bf16[12,8,128]{2,1,0:T(8,128)(2,1)S(1)}, bf16[12,8,128]{2,1,0:T(8,128)(2,1)S(1)}, u32[]{:S(2)}, u32[]{:S(2)}) collective-permute-start(bf16[12,8,128]{2,1,0:T(8,128)(2,1)S(1)} %slice.116), channel_id=1, source_target_pairs={{0,16},{16,0},{1,17},{17,1},{2,18},{18,2},{3,19},{19,3},{4,20},{20... | collective-permute-start | bytes 73736 | tf_op jit(solution)/shard_map/ppermute | solution.py:748
  28.9 1.4 collective-permute-start.1
  31.2 1.0 copy-start.2
  111.3 138.0 %copy-start.14 = (f32[12,8,128]{2,1,0:T(8,128)S(1)}, f32[12,8,128]{2,1,0:T(8,128)}, u32[]{:S(2)}) copy-start(f32[12,8,128]{2,1,0:T(8,128)} %get-tuple-element.112) | copy-start | bytes 147460
  111.3 138.0 %copy-start.15 = (f32[12,8,128]{2,1,0:T(8,128)S(1)}, f32[12,8,128]{2,1,0:T(8,128)}, u32[]{:S(2)}) copy-start(f32[12,8,128]{2,1,0:T(8,128)} %get-tuple-element.111) | copy-start | bytes 147460
  111.3 138.1 %copy-start.12 = (f32[16,768]{1,0:T(8,128)S(1)}, f32[16,768]{1,0:T(8,128)}, u32[]{:S(2)}) copy-start(f32[16,768]{1,0:T(8,128)} %get-tuple-element.108) | copy-start | bytes 147460
  111.4 138.1 %copy-start.13 = (f32[16,768]{1,0:T(8,128)S(1)}, f32[16,768]{1,0:T(8,128)}, u32[]{:S(2)}) copy-start(f32[16,768]{1,0:T(8,128)} %get-tuple-element.107) | copy-start | bytes 147460
  111.4 138.7 %copy-start.4 = (bf16[256,768]{1,0:T(8,128)(2,1)S(1)}, bf16[256,768]{1,0:T(8,128)(2,1)}, u32[]{:S(2)}) copy-start(bf16[256,768]{1,0:T(8,128)(2,1)} %get-tuple-element.77.g_ref) | copy-start | bytes 1179652
  111.4 138.7 %copy-start.8 = (bf16[256,768]{1,0:T(8,128)(2,1)S(1)}, bf16[256,768]{1,0:T(8,128)(2,1)}, u32[]{:S(2)}) copy-start(bf16[256,768]{1,0:T(8,128)(2,1)} %get-tuple-element.86) | copy-start | bytes 1179652
  111.4 138.7 %copy-start.3 = (bf16[256,768]{1,0:T(8,128)(2,1)S(1)}, bf16[256,768]{1,0:T(8,128)(2,1)}, u32[]{:S(2)}) copy-start(bf16[256,768]{1,0:T(8,128)(2,1)} %get-tuple-element.67.x_ref) | copy-start | bytes 1179652
  111.4 138.7 %copy-start.7 = (bf16[256,768]{1,0:T(8,128)(2,1)S(1)}, bf16[256,768]{1,0:T(8,128)(2,1)}, u32[]{:S(2)}) copy-start(bf16[256,768]{1,0:T(8,128)(2,1)} %get-tuple-element.68) | copy-start | bytes 1179652
  111.4 139.3 %copy-start.5 = (f32[12,16,512]{2,1,0:T(8,128)S(1)}, f32[12,16,512]{2,1,0:T(8,128)}, u32[]{:S(2)}) copy-start(f32[12,16,512]{2,1,0:T(8,128)} %get-tuple-element.110) | copy-start | bytes 1179652
  111.4 139.3 %copy-start.6 = (f32[12,16,512]{2,1,0:T(8,128)S(1)}, f32[12,16,512]{2,1,0:T(8,128)}, u32[]{:S(2)}) copy-start(f32[12,16,512]{2,1,0:T(8,128)} %get-tuple-element.109) | copy-start | bytes 1179652
  249.4 1.6 collective-permute-start.11
  249.5 2.4 collective-permute-start.9
  250.2 2.3 collective-permute-start.7
  250.3 2.4 collective-permute-start.8
  250.8 5.6 %collective-permute-start.10 = (f32[12,16,512]{2,1,0:T(8,128)S(1)}, f32[12,16,512]{2,1,0:T(8,128)S(1)}, u32[]{:S(2)}, u32[]{:S(2)}) collective-permute-start(f32[12,16,512]{2,1,0:T(8,128)S(1)} %broadcast_select_fusion.8), channel_id=1, source_target_pairs={{0,16},{16,0},{1,17},{17,1},{2,18},{18,2},{3,19},{19,3},{4,20},{20... | collective-permute-start | bytes 1179656 | tf_op jit(solution)/shard_map/ppermute | solution.py:748
  256.9 113.6 %copy-start.11 = (f32[48,2304]{1,0:T(8,128)S(1)}, f32[48,2304]{1,0:T(8,128)}, u32[]{:S(2)}) copy-start(f32[48,2304]{1,0:T(8,128)} %get-tuple-element.103) | copy-start | bytes 1327108
  256.9 114.4 %copy-start.16 = (f32[48,768]{1,0:T(8,128)S(1)}, f32[48,768]{1,0:T(8,128)}, u32[]{:S(2)}) copy-start(f32[48,768]{1,0:T(8,128)} %get-tuple-element.104) | copy-start | bytes 442372
  256.9 115.0 %copy-start.10 = (f32[48,3072]{1,0:T(8,128)S(1)}, f32[48,3072]{1,0:T(8,128)}, u32[]{:S(2)}) copy-start(f32[48,3072]{1,0:T(8,128)} %get-tuple-element.105) | copy-start | bytes 1769476
  256.9 116.6 %copy-start.1 = (bf16[2,197,768]{2,0,1:T(2,128)(2,1)S(1)}, bf16[2,197,768]{2,0,1:T(2,128)(2,1)}, u32[]{:S(2)}) copy-start(bf16[2,197,768]{2,0,1:T(2,128)(2,1)} %param.27) | copy-start | bytes 1815556
  261.0 111.8 %copy-start.9 = (f32[192,768]{1,0:T(8,128)S(1)}, f32[192,768]{1,0:T(8,128)}, u32[]{:S(2)}) copy-start(f32[192,768]{1,0:T(8,128)} %get-tuple-element.106) | copy-start | bytes 1769476
Sparse Core Ops, SparseCore 0:
  261.8 102.9 all-reduce.6

commit v3 on v2

--- a/solution.py
+++ b/solution.py
@@ -42,31 +42,6 @@
 INDEX_L = spread_index(GRID_L, 8, LANES_L, FRONT_L, LOCAL_ROW - 128)
 
 
-def one_hot(index, count):
-    flat = jnp.asarray(index.reshape(1, -1))
-    return (lax.broadcasted_iota(jnp.int32, (count, flat.shape[1]), 0) == flat).astype(BF16)
-
-
-def spread(table, index):
-    heads = table.shape[1]
-    flat = lax.dot_general(
-        table, one_hot(index, table.shape[0]), (((0,), (0,)), ((), ())), preferred_element_type=F32
-    )
-    return flat.astype(BF16).reshape(heads, *index.shape)
-
-
-def gather_back(values, index, count):
-    heads = values.shape[0]
-    flat = values.reshape(heads, -1)
-    high = flat.astype(BF16)
-    low = (flat - high.astype(F32)).astype(BF16)
-    both = jnp.concatenate([high, low], 0)
-    sums = lax.dot_general(
-        one_hot(index, count), both, (((1,), (1,)), ((), ())), preferred_element_type=F32
-    )
-    return sums[:, :heads] + sums[:, heads:]
-
-
 def dot(a, b):
     return lax.dot_general(a, b, (((1,), (0,)), ((), ())), preferred_element_type=F32)
 
@@ -77,24 +52,6 @@
 
 def dot_rows(a, b):
     return lax.dot_general(a, b, (((0,), (0,)), ((), ())), preferred_element_type=F32)
-
-
-def fetch(layer, pairs, sems):
-    section = lax.axis_index("pipe")
-    for number, (own, other, held) in enumerate(pairs):
-
-        @pl.when(section == layer)
-        def _():
-            pltpu.make_async_copy(own, held, sems.at[number]).start()
-
-        @pl.when(section != layer)
-        def _():
-            pltpu.make_async_copy(other, held, sems.at[number]).start()
-
-
-def arrive(pairs, sems, number):
-    own, other, held = pairs[number]
-    pltpu.make_async_copy(own, held, sems.at[number]).wait()
 
 
 def normalised(x):
@@ -138,109 +95,294 @@
     return jnp.concatenate([top, bottom], 0)
 
 
+MESH = pl.DeviceIdType.MESH
+SIDE = 2
+TABLE_ROW, TABLE_ROW_L, SMALL_ROWS = 16, 32, 48
+
+
+def remote(source, target, sent, came, **device):
+    return pltpu.make_async_remote_copy(
+        src_ref=source, dst_ref=target, send_sem=sent, recv_sem=came,
+        device_id=device, device_id_type=MESH,
+    )
+
+
+def hot(index_row, count):
+    number = lax.broadcasted_iota(jnp.int32, (count, index_row.shape[1]), 0)
+    return jnp.where(number == index_row, 1.0, 0.0).astype(BF16)
+
+
+def place_crops(target, global_ref, local_ref, section, live_g=None, live_l=None):
+    target[...] = jnp.zeros_like(target)
+    for ref, start, live in ((global_ref, 0, live_g), (local_ref, LOCAL_ROW, live_l)):
+        rows = jnp.where(section == 0, ref[:, 0, :].astype(F32), ref[:, 1, :].astype(F32))
+        if live is not None:
+            rows = rows * live
+        target[start:start + ref.shape[0], :] = rows.astype(BF16)
+
+
 def forward_kernel(
-    layer, scale,
-    x_ref, vec_ref, sg_ref, sl_ref,
-    own_qkv, own_proj, own_fc1, own_fc2, oth_qkv, oth_proj, oth_fc1, oth_fc2,
-    out_ref, n1_ref, q_ref, k_ref, v_ref, p_ref, merged_ref, branch_ref, middle_ref,
-    n2_ref, act_ref, dact_ref, branch2_ref,
-    w_qkv, w_proj, w_fc1, w_fc2, bias, sems,
+    scale,
+    xg_ref, xl_ref, vec_refs, tg_ref, tl_ref, index_g, index_l, own_qkv, own_proj, own_fc1, own_fc2,
+    oth_qkv, oth_proj, oth_fc1, oth_fc2,
+    out_all, n1_all, q_all, k_all, v_all, p_all, merged_all, branch_all, middle_all,
+    n2_all, act_all, dact_all, branch2_all, small_out,
+    w_qkv, w_proj, w_fc1, w_fc2, small_in, small, vec_all, x_in, out_ref, n1_ref, q_ref, k_ref, v_ref, p_ref,
+    merged_ref, branch_ref, middle_ref, n2_ref, act_ref, dact_ref, branch2_ref,
+    spread_g, spread_l, bias, own_sem, sent, came, keep_sem, store_sem, small_sem,
 ):
-    pairs = (
-        (own_qkv, oth_qkv, w_qkv), (own_proj, oth_proj, w_proj),
-        (own_fc1, oth_fc1, w_fc1), (own_fc2, oth_fc2, w_fc2),
+    section = lax.axis_index("pipe")
+    partner = 1 - section
+    own = (own_qkv, own_proj, own_fc1, own_fc2)
+    oth = (oth_qkv, oth_proj, oth_fc1, oth_fc2)
+    held = (w_qkv, w_proj, w_fc1, w_fc2)
+    width = x_in.shape[1]
+    heads = p_ref.shape[0]
+    half = SMALL_ROWS
+
+    barrier = pltpu.get_barrier_semaphore()
+    pl.semaphore_signal(barrier, inc=1, device_id={"pipe": partner}, device_id_type=MESH)
+    for i in range(4):
+        pltpu.make_async_copy(own[i], held[i].at[section], own_sem.at[i]).start()
+    small_rows = small.at[pl.ds(pl.multiple_of(section * half, half), half), :]
+    small_in[...] = jnp.zeros_like(small_in)
+    row = 0
+    for ref in vec_refs:
+        for b in range(0, ref.shape[1], width):
+            small_in[row:row + 1, :] = ref[:, b:b + width].astype(F32)
+            row += 1
+    small_in[TABLE_ROW:TABLE_ROW + heads, 0:tg_ref.shape[1]] = tg_ref[...].astype(F32)
+    small_in[TABLE_ROW_L:TABLE_ROW_L + heads, 0:tl_ref.shape[1]] = tl_ref[...].astype(F32)
+    pl.semaphore_wait(barrier, 1)
+    small_copy = remote(small_in, small_rows, small_sem.at[0], small_sem.at[1], pipe=partner)
+    small_copy.start()
+
+    def weight_copy(i):
+        return remote(own[i], held[i].at[section], sent.at[i], came.at[i], pipe=partner)
+
+    for i in range(4):
+        weight_copy(i).start()
+    small_rows[...] = small_in[...]
+    place_crops(x_in, xg_ref, xl_ref, section)
+    small_copy.wait_recv()
+    vec_all[...] = small[...]
+    small_out[...] = vec_all[...]
+    tables_g = jnp.concatenate(
+        [small[TABLE_ROW:TABLE_ROW + 16, :], small[half + TABLE_ROW:half + TABLE_ROW + 16, :]], 0
+    ).astype(BF16)
+    tables_l = jnp.concatenate(
+        [small[TABLE_ROW_L:TABLE_ROW_L + 16, :128], small[half + TABLE_ROW_L:half + TABLE_ROW_L + 16, :128]], 0
+    ).astype(BF16)
+    for r in range(16):
+        found = dot(tables_g, hot(index_g[r:r + 1, :], width))
+        spread_g[0, :, r, :] = found[:16]
+        spread_g[1, :, r, :] = found[16:]
+    for r in range(8):
+        found = dot(tables_l, hot(index_l[r:r + 1, :], 128))
+        spread_l[0, :, r, :] = found[:16]
+        spread_l[1, :, r, :] = found[16:]
+
+    stores = (
+        (out_ref, out_all), (n1_ref, n1_all), (q_ref, q_all), (k_ref, k_all), (v_ref, v_all),
+        (p_ref, p_all), (merged_ref, merged_all), (branch_ref, branch_all), (middle_ref, middle_all),
+        (n2_ref, n2_all), (act_ref, act_all), (dact_ref, dact_all), (branch2_ref, branch2_all),
     )
-    fetch(layer, pairs, sems)
-    width = x_ref.shape[1]
-    heads = p_ref.shape[0]
-
-    def vec(row):
-        return vec_ref[row:row + 1, :]
-
-    def norm1(rows):
-        xhat, _ = normalised(x_ref[rows, :].astype(F32))
-        n1_ref[rows, :] = (xhat * vec(N1G) + vec(N1S)).astype(BF16)
-
-    row_steps(32, norm1)
-    arrive(pairs, sems, 0)
-    n1 = n1_ref[...]
-    for b in range(0, width, BLOCK):
-        cols = slice(b, b + BLOCK)
-        mixed = dot(n1, w_qkv[:, b:b + BLOCK]) + vec_ref[QB:QB + 1, cols]
-        q_ref[:, cols] = (mixed * scale).astype(BF16)
-        k_ref[:, cols] = dot(n1, w_qkv[:, width + b:width + b + BLOCK]).astype(BF16)
-        mixed = dot(n1, w_qkv[:, 2 * width + b:2 * width + b + BLOCK]) + vec_ref[VB:VB + 1, cols]
-        v_ref[:, cols] = mixed.astype(BF16)
+    OUT, N1, Q, K, V, PR, ME, BR, MI, N2, AC, DA, B2 = range(13)
+
+    def store_copy(number, layer):
+        source, target = stores[number]
+        if number == OUT:
+            source = source.at[layer]
+        return pltpu.make_async_copy(source, target.at[layer], store_sem.at[number])
+
+    def store(layer, *numbers):
+        for number in numbers:
+            store_copy(number, layer).start()
+
+    def stored(layer, *numbers):
+        for number in numbers:
+            store_copy(number, layer).wait()
+
+    def weight(i, layer):
+        @pl.when(section == layer)
+        def _():
+            pltpu.make_async_copy(own[i], held[i].at[section], own_sem.at[i]).wait()
+
+        @pl.when(section != layer)
+        def _():
+            here = held[i].at[partner]
+            remote(here, here, sent.at[i], came.at[i], pipe=partner).wait_recv()
+            pltpu.make_async_copy(here, oth[i], keep_sem.at[i]).start()
+
     lane = lax.broadcasted_iota(jnp.int32, (1, 128), 1)
-    for pair in range(heads // 2):
-        cols = slice(pair * 128, pair * 128 + 128)
-        q, k, v = q_ref[:, cols], k_ref[:, cols], v_ref[:, cols]
-        result = None
-        for half in range(2):
-            head = 2 * pair + half
-            mine = (lane < 64) if half == 0 else (lane >= 64)
-            scores = dot_cols(q, jnp.where(mine, k, jnp.zeros_like(k))) + build_bias(
-                sg_ref[head].astype(F32), sl_ref[head].astype(F32), bias.at[head % 2]
-            )
-            expo = jnp.exp(scores - jnp.max(scores, axis=-1, keepdims=True))
-            probs = expo * (1.0 / jnp.sum(expo, axis=-1, keepdims=True))
-            p_ref[head] = probs
-            part = dot(probs.astype(BF16), jnp.where(mine, v, jnp.zeros_like(v)))
-            result = part if result is None else result + part
-        merged_ref[:, cols] = result.astype(BF16)
-    arrive(pairs, sems, 1)
-    merged = merged_ref[...]
-    for b in range(0, width, BLOCK):
-        cols = slice(b, b + BLOCK)
-        branch = dot(merged, w_proj[:, cols]) + vec_ref[PB:PB + 1, cols]
-        branch_ref[:, cols] = branch
-        middle_ref[:, cols] = x_ref[:, cols].astype(F32) + vec_ref[SA:SA + 1, cols] * branch
-
-    def norm2(rows):
-        xhat, _ = normalised(middle_ref[rows, :])
-        n2_ref[rows, :] = (xhat * vec(N2G) + vec(N2S)).astype(BF16)
-
-    row_steps(32, norm2)
-    arrive(pairs, sems, 2)
-    n2 = n2_ref[...]
-    for b in range(0, w_fc1.shape[1], BLOCK):
-        cols = slice(b, b + BLOCK)
-        part = b // width
-        hidden = dot(n2, w_fc1[:, cols]) + vec_ref[
-            F1B + part:F1B + part + 1, b - part * width:b - part * width + BLOCK
-        ]
-        cdf = 0.5 + 0.5 * lax.erf(hidden * INV_SQRT2)
-        act_ref[:, cols] = (hidden * cdf).astype(BF16)
-        dact_ref[:, cols] = cdf + hidden * (INV_SQRT_2PI * jnp.exp(-0.5 * hidden * hidden))
-    arrive(pairs, sems, 3)
-    for b in range(0, width, BLOCK):
-        cols = slice(b, b + BLOCK)
-        branch2 = dot(act_ref[...], w_fc2[:, cols]) + vec_ref[F2B:F2B + 1, cols]
-        branch2_ref[:, cols] = branch2
-        out_ref[:, cols] = (middle_ref[:, cols] + vec_ref[SM:SM + 1, cols] * branch2).astype(BF16)
+    for layer in range(2):
+        entering = x_in if layer == 0 else out_ref.at[0]
+        base = layer * half
+
+        def vec(row):
+            return vec_all[base + row:base + row + 1, :]
+
+        def norm1(rows):
+            xhat, _ = normalised(entering[rows, :].astype(F32))
+            n1_ref[rows, :] = (xhat * vec(N1G) + vec(N1S)).astype(BF16)
+
+        row_steps(32, norm1)
+        store(layer, N1)
+        weight(0, layer)
+        n1 = n1_ref[...]
+        for b in range(0, width, BLOCK):
+            cols = slice(b, b + BLOCK)
+            mixed = dot(n1, w_qkv[layer, :, b:b + BLOCK]) + vec(QB)[:, cols]
+            q_ref[:, cols] = (mixed * scale).astype(BF16)
+            k_ref[:, cols] = dot(n1, w_qkv[layer, :, width + b:width + b + BLOCK]).astype(BF16)
+            mixed = dot(n1, w_qkv[layer, :, 2 * width + b:2 * width + b + BLOCK]) + vec(VB)[:, cols]
+            v_ref[:, cols] = mixed.astype(BF16)
+        store(layer, Q, K, V)
+        for pair in range(heads // 2):
+            cols = slice(pair * 128, pair * 128 + 128)
+            q, k, v = q_ref[:, cols], k_ref[:, cols], v_ref[:, cols]
+            result = None
+            for part in range(2):
+                head = 2 * pair + part
+                mine = (lane < 64) if part == 0 else (lane >= 64)
+                scores = dot_cols(q, jnp.where(mine, k, jnp.zeros_like(k))) + build_bias(
+                    spread_g[layer, head], spread_l[layer, head], bias.at[head % 2]
+                )
+                expo = jnp.exp(scores - jnp.max(scores, axis=-1, keepdims=True))
+                probs = expo * (1.0 / jnp.sum(expo, axis=-1, keepdims=True))
+                p_ref[head] = probs
+                piece = dot(probs.astype(BF16), jnp.where(mine, v, jnp.zeros_like(v)))
+                result = piece if result is None else result + piece
+            merged_ref[:, cols] = result.astype(BF16)
+        store(layer, PR, ME)
+        weight(1, layer)
+        merged = merged_ref[...]
+        for b in range(0, width, BLOCK):
+            cols = slice(b, b + BLOCK)
+            branch = dot(merged, w_proj[layer, :, cols]) + vec(PB)[:, cols]
+            branch_ref[:, cols] = branch
+            middle_ref[:, cols] = entering[:, cols].astype(F32) + vec(SA)[:, cols] * branch
+        store(layer, BR, MI)
+
+        def norm2(rows):
+            xhat, _ = normalised(middle_ref[rows, :])
+            n2_ref[rows, :] = (xhat * vec(N2G) + vec(N2S)).astype(BF16)
+
+        row_steps(32, norm2)
+        store(layer, N2)
+        weight(2, layer)
+        if layer == 1:
+            stored(0, AC, DA, B2)
+        n2 = n2_ref[...]
+        for b in range(0, w_fc1.shape[2], BLOCK):
+            cols = slice(b, b + BLOCK)
+            part = b // width
+            hidden = dot(n2, w_fc1[layer, :, cols]) + vec(F1B + part)[:, b - part * width:b - part * width + BLOCK]
+            cdf = 0.5 + 0.5 * lax.erf(hidden * INV_SQRT2)
+            act_ref[:, cols] = (hidden * cdf).astype(BF16)
+            dact_ref[:, cols] = cdf + hidden * (INV_SQRT_2PI * jnp.exp(-0.5 * hidden * hidden))
+        store(layer, AC, DA)
+        weight(3, layer)
+        for b in range(0, width, BLOCK):
+            cols = slice(b, b + BLOCK)
+            branch2 = dot(act_ref[...], w_fc2[layer, :, cols]) + vec(F2B)[:, cols]
+            branch2_ref[:, cols] = branch2
+            out_ref[layer, :, cols] = (middle_ref[:, cols] + vec(SM)[:, cols] * branch2).astype(BF16)
+        store(layer, B2, OUT)
+        if layer == 0:
+            stored(0, N1, Q, K, V, PR, ME, BR, MI, N2, OUT)
+    stored(1, *range(13))
+    for i in range(4):
+        weight_copy(i).wait_send()
+        pltpu.make_async_copy(held[i].at[partner], oth[i], keep_sem.at[i]).wait()
+    small_copy.wait_send()
 
 
 def backward_kernel(
-    layer, scale,
-    x_ref, g_ref, vec_ref, q_ref, k_ref, v_ref, p_ref, branch_ref, middle_ref, dact_ref, branch2_ref,
-    own_qkv, own_proj, own_fc1, own_fc2, oth_qkv, oth_proj, oth_fc1, oth_fc2,
-    gx_ref, gmixed_ref, gbranch_ref, ghidden_ref, gb2_ref, small_ref, tg_ref, tl_ref,
-    w_qkv, w_proj, w_fc1, w_fc2, gmid, gnorm, gmerged, gs_ref, sems,
+    layer, scale, *refs,
 ):
-    pairs = (
-        (own_fc2, oth_fc2, w_fc2), (own_fc1, oth_fc1, w_fc1),
-        (own_proj, oth_proj, w_proj), (own_qkv, oth_qkv, w_qkv),
+    if layer == 1:
+        cg_ref, cl_ref, gcount, lcount = refs[:4]
+        refs = refs[4:]
+    else:
+        gin_ref, refs = refs[0], refs[1:]
+    vec_all, x_all, q_all, k_all, v_all, p_all, branch_all, middle_all, dact_all, branch2_all = refs[:10]
+    own, oth = refs[10:14], refs[14:18]
+    gx_ref, gmixed_out, gbranch_out, ghidden_out, gb2_out, small_ref, tg_ref, tl_ref = refs[18:26]
+    (
+        g_ref, x_ref, q_ref, k_ref, v_ref, p_ref, branch_ref, middle_ref, dact_ref, branch2_ref,
+        w_qkv, w_proj, w_fc1, w_fc2, gmixed_ref, gbranch_ref, ghidden_ref, gb2_ref,
+        gmid, gnorm, gmerged, gs_ref, load_sem, weight_sem, store_sem,
+    ) = refs[26:]
+    section = lax.axis_index("pipe")
+    held = (w_qkv, w_proj, w_fc1, w_fc2)
+    loads = (
+        (x_all, x_ref), (q_all, q_ref), (k_all, k_ref), (v_all, v_ref), (p_all, p_ref),
+        (branch_all, branch_ref), (middle_all, middle_ref), (dact_all, dact_ref), (branch2_all, branch2_ref),
     )
-    fetch(layer, pairs, sems)
-    width = x_ref.shape[1]
+    X, Q, K, V, PR, BR, MI, DA, B2 = range(9)
+
+    def load_copy(number):
+        source, target = loads[number]
+        if layer == 1 or number != X:
+            source = source.at[0 if number == X else layer]
+        return pltpu.make_async_copy(source, target, load_sem.at[number])
+
+    def load_weight(i):
+        @pl.when(section == layer)
+        def _():
+            pltpu.make_async_copy(own[i], held[i], weight_sem.at[i]).start()
+
+        @pl.when(section != layer)
+        def _():
+            pltpu.make_async_copy(oth[i], held[i], weight_sem.at[i]).start()
+
+    def weight(i):
+        pltpu.make_async_copy(own[i], held[i], weight_sem.at[i]).wait()
+
+    def loaded(*numbers):
+        for number in numbers:
+            load_copy(number).wait()
+
+    load_copy(B2).start()
+    load_weight(3)
+    load_copy(DA).start()
+    load_weight(2)
+    for number in (MI, BR):
+        load_copy(number).start()
+    load_weight(1)
+    for number in (V, PR, K, Q):
+        load_copy(number).start()
+    load_weight(0)
+    if layer == 1:
+        load_copy(X).start()
+
+    width = g_ref.shape[1]
     heads = p_ref.shape[0]
     small_ref[...] = jnp.zeros_like(small_ref)
 
     def vec(row):
-        return vec_ref[row:row + 1, :]
+        return vec_all[layer * SMALL_ROWS + row:layer * SMALL_ROWS + row + 1, :]
 
     def add_small(row, values):
         small_ref[row:row + 1, :] += jnp.sum(values, axis=0, keepdims=True)
+
+    if layer == 1:
+        live_g = jnp.where(gcount[0] > section, 1.0, 0.0)
+        live_l = jnp.where(lcount[0] > section, 1.0, 0.0)
+        place_crops(g_ref, cg_ref, cl_ref, section, live_g, live_l)
+    else:
+        g_ref = gin_ref
+        place_crops(x_ref, *x_all, section)
+
+    stores = (
+        (gmixed_ref, gmixed_out), (gbranch_ref, gbranch_out), (ghidden_ref, ghidden_out), (gb2_ref, gb2_out),
+    )
+
+    def store_copy(number):
+        return pltpu.make_async_copy(*stores[number], store_sem.at[number])
+
+    loaded(B2)
 
     def scaled(rows):
         grad = g_ref[rows, :].astype(F32)
@@ -250,7 +392,9 @@
         add_small(F2B, low.astype(F32))
 
     row_steps(32, scaled)
-    arrive(pairs, sems, 0)
+    store_copy(3).start()
+    weight(3)
+    loaded(DA)
     gb2 = gb2_ref[...]
     for b in range(0, w_fc1.shape[1], BLOCK):
         cols = slice(b, b + BLOCK)
@@ -260,7 +404,8 @@
         small_ref[F1B + part:F1B + part + 1, b - part * width:b - part * width + BLOCK] = jnp.sum(
             ghidden.astype(F32), axis=0, keepdims=True
         )
-    arrive(pairs, sems, 1)
+    store_copy(2).start()
+    weight(2)
     for b in range(0, width, BLOCK):
         gnorm[:, b:b + BLOCK] = dot_cols(ghidden_ref[...], w_fc1[b:b + BLOCK, :])
 
@@ -270,6 +415,8 @@
         mean1 = jnp.mean(scaled_grad, axis=-1, keepdims=True)
         mean2 = jnp.mean(scaled_grad * xhat, axis=-1, keepdims=True)
         return xhat, rstd * (scaled_grad - mean1 - xhat * mean2)
+
+    loaded(MI, BR)
 
     def norm2(rows):
         grad = gnorm[rows, :]
@@ -284,10 +431,12 @@
         add_small(PB, low.astype(F32))
 
     row_steps(32, norm2)
-    arrive(pairs, sems, 2)
+    store_copy(1).start()
+    weight(1)
     for b in range(0, width, BLOCK):
         gmerged[:, b:b + BLOCK] = dot_cols(gbranch_ref[...], w_proj[b:b + BLOCK, :]).astype(BF16)
     lane = lax.broadcasted_iota(jnp.int32, (1, 128), 1)
+    loaded(V, PR, K, Q)
     lane_all = lax.broadcasted_iota(jnp.int32, (1, ROWS), 1)
     for pair in range(heads // 2):
         cols = slice(pair * 128, pair * 128 + 128)
@@ -319,9 +468,9 @@
             to_class = jnp.sum(wide[:LOCAL_ROW, :], axis=0, keepdims=True) - first_row
             to_class = jnp.where(lane_all == 0, to_class, 0.0)
             blank = jnp.zeros((1, LANES_G - ROWS), F32)
-            tg_ref[head, 0:GRID_G, :] = acc
-            tg_ref[head, 14:15, :] = jnp.concatenate([first_row, blank], 1)
-            tg_ref[head, 15:16, :] = jnp.concatenate([to_class, blank], 1)
+            tg_ref[0:GRID_G, head, :] = acc
+            tg_ref[14, head:head + 1, :] = jnp.concatenate([first_row, blank], 1)
+            tg_ref[15, head:head + 1, :] = jnp.concatenate([to_class, blank], 1)
             acc = jnp.zeros((GRID_L, LANES_L), F32)
             for r in range(GRID_L):
                 block = gs[pl.ds(LOCAL_ROW + 1 + GRID_L * r, GRID_L), pl.ds(128, 128)]
@@ -329,9 +478,9 @@
             first_row = wide[LOCAL_ROW:LOCAL_ROW + 1, 128:]
             to_class = jnp.sum(wide[LOCAL_ROW:, 128:], axis=0, keepdims=True) - first_row
             to_class = jnp.where(lane == LOCAL_ROW - 128, to_class, 0.0)
-            tl_ref[head, 0:GRID_L, :] = acc
-            tl_ref[head, 6:7, :] = first_row
-            tl_ref[head, 7:8, :] = to_class
+            tl_ref[0:GRID_L, head, :] = acc
+            tl_ref[6, head:head + 1, :] = first_row
+            tl_ref[7, head:head + 1, :] = to_class
         gmixed_ref[:, cols] = gq.astype(BF16) * jnp.asarray(scale, BF16)
         gmixed_ref[:, slice(width + cols.start, width + cols.stop)] = gk.astype(BF16)
         gmixed_ref[:, slice(2 * width + cols.start, 2 * width + cols.stop)] = gv.astype(BF16)
@@ -340,8 +489,11 @@
         add_small(QB, gmixed_ref[rows, :width].astype(F32))
         add_small(VB, gmixed_ref[rows, 2 * width:].astype(F32))
 
+    store_copy(0).start()
     row_steps(32, biases)
-    arrive(pairs, sems, 3)
+    weight(0)
+    if layer == 1:
+        loaded(X)
     for b in range(0, width, BLOCK):
         gnorm[:, b:b + BLOCK] = dot_cols(gmixed_ref[...], w_qkv[b:b + BLOCK, :])
 
@@ -353,72 +505,98 @@
         gx_ref[rows, :] = (gmid[rows, :] + through).astype(BF16)
 
     row_steps(32, norm1)
+    for number in range(4):
+        store_copy(number).wait()
 
 
 def shape(*dims, dtype=BF16):
     return jax.ShapeDtypeStruct(dims, dtype)
 
 
-def forward(layer, x, vec, sg, sl, own, other):
-    width = x.shape[1]
-    hidden = own[2].shape[1]
-    heads = sg.shape[0]
-    scale = (width // heads) ** (-0.5)
-    inside = pl.BlockSpec(memory_space=pltpu.VMEM)
-    outside = pl.BlockSpec(memory_space=pl.ANY)
-    return pl.pallas_call(
-        functools.partial(forward_kernel, layer, scale),
-        out_shape=(
-            shape(ROWS, width), shape(ROWS, width), shape(ROWS, width), shape(ROWS, width),
-            shape(ROWS, width), shape(heads, ROWS, ROWS, dtype=F32), shape(ROWS, width),
-            shape(ROWS, width, dtype=F32), shape(ROWS, width, dtype=F32), shape(ROWS, width),
-            shape(ROWS, hidden), shape(ROWS, hidden, dtype=F32), shape(ROWS, width, dtype=F32),
-        ),
-        in_specs=[inside] * 4 + [outside] * 8,
-        out_specs=(inside,) * 13,
-        scratch_shapes=[pltpu.VMEM(w.shape, BF16) for w in own]
-        + [pltpu.VMEM((2, ROWS, ROWS), F32), pltpu.SemaphoreType.DMA((4,))],
-        compiler_params=pltpu.CompilerParams(vmem_limit_bytes=60 * 2**20),
-        name="layer_forward",
-    )(x, vec, sg, sl, *own, *other)
-
-
-def backward(layer, x, grad, vec, kept, heads, own, other):
-    width = x.shape[1]
+INSIDE = pl.BlockSpec(memory_space=pltpu.VMEM)
+OUTSIDE = pl.BlockSpec(memory_space=pl.ANY)
+SCALARS = pl.BlockSpec(memory_space=pltpu.SMEM)
+DMA = pltpu.SemaphoreType.DMA
+
+
+def forward(x_global, x_local, vec, tables, own):
+    width = x_global.shape[2]
+    heads = tables[0].shape[0]
     hidden = own[2].shape[1]
     scale = (width // heads) ** (-0.5)
-    inside = pl.BlockSpec(memory_space=pltpu.VMEM)
-    outside = pl.BlockSpec(memory_space=pl.ANY)
+    kept = (
+        ((ROWS, width), BF16), ((ROWS, width), BF16), ((ROWS, width), BF16), ((ROWS, width), BF16),
+        ((ROWS, width), BF16), ((heads, ROWS, ROWS), F32), ((ROWS, width), BF16),
+        ((ROWS, width), F32), ((ROWS, width), F32), ((ROWS, width), BF16),
+        ((ROWS, hidden), BF16), ((ROWS, hidden), F32), ((ROWS, width), F32),
+    )
+    scratch = [pltpu.VMEM((2, *w.shape), BF16) for w in own]
+    scratch += [pltpu.VMEM((SMALL_ROWS, width), F32)] + [pltpu.VMEM((2 * SMALL_ROWS, width), F32)] * 2
+    scratch += [pltpu.VMEM((ROWS, width), BF16), pltpu.VMEM((2, ROWS, width), BF16)]
+    scratch += [pltpu.VMEM(dims, kind) for dims, kind in kept[1:]]
+    scratch += [
+        pltpu.VMEM((2, 16, 16, LANES_G), F32), pltpu.VMEM((2, 16, 8, LANES_L), F32),
+        pltpu.VMEM((2, ROWS, ROWS), F32),
+        DMA((4,)), DMA((4,)), DMA((4,)), DMA((4,)), DMA((13,)), DMA((2,)),
+    ]
+
+    def kernel(xg, xl, *refs):
+        count = len(vec)
+        forward_kernel(scale, xg, xl, refs[:count], *refs[count:])
+
+    return pl.pallas_call(
+        kernel,
+        out_shape=tuple(shape(*w.shape) for w in own)
+        + tuple(shape(2, *dims, dtype=kind) for dims, kind in kept)
+        + (shape(2 * SMALL_ROWS, width, dtype=F32),),
+        in_specs=[INSIDE] * (6 + len(vec)) + [OUTSIDE] * 4,
+        out_specs=(OUTSIDE,) * 17 + (INSIDE,),
+        scratch_shapes=scratch,
+        compiler_params=pltpu.CompilerParams(
+            vmem_limit_bytes=60 * 2**20, collective_id=2, has_side_effects=True
+        ),
+        name="forward_layers",
+    )(x_global, x_local, *vec, *tables, jnp.asarray(INDEX_G), jnp.asarray(INDEX_L), *own)
+
+
+def backward(layer, grads, entering, vec, kept, heads, own, other):
+    width = vec.shape[1]
+    hidden = own[2].shape[1]
+    scale = (width // heads) ** (-0.5)
     _, n1, q, k, v, probs, merged, branch, middle, n2, act, dact, branch2 = kept
+    if layer == 1:
+        inputs = (*grads, vec, entering, q, k, v, probs, branch, middle, dact, branch2, *own, *other)
+        specs = [INSIDE] * 2 + [SCALARS] * 2 + [INSIDE] + [OUTSIDE] * 17
+        kernel = functools.partial(backward_kernel, 1, scale)
+    else:
+        inputs = (grads, vec, *entering, q, k, v, probs, branch, middle, dact, branch2, *own, *other)
+        specs = [INSIDE] * 4 + [OUTSIDE] * 16
+
+        def kernel(gin, vec_all, xg, xl, *refs):
+            backward_kernel(0, scale, gin, vec_all, (xg, xl), *refs)
+
     return pl.pallas_call(
-        functools.partial(backward_kernel, layer, scale),
+        kernel,
         out_shape=(
             shape(ROWS, width), shape(ROWS, 3 * width), shape(ROWS, width), shape(ROWS, hidden),
             shape(ROWS, width), shape(16, width, dtype=F32),
-            shape(heads, 16, LANES_G, dtype=F32), shape(heads, 8, LANES_L, dtype=F32),
+            shape(16, heads, LANES_G, dtype=F32), shape(8, heads, LANES_L, dtype=F32),
         ),
-        in_specs=[inside] * 11 + [outside] * 8,
-        out_specs=(inside,) * 8,
-        scratch_shapes=[pltpu.VMEM(w.shape, BF16) for w in own]
+        in_specs=specs,
+        out_specs=(INSIDE,) + (OUTSIDE,) * 4 + (INSIDE,) * 3,
+        scratch_shapes=[pltpu.VMEM((ROWS, width), BF16) for _ in range(5)]
+        + [pltpu.VMEM((heads, ROWS, ROWS), F32), pltpu.VMEM((ROWS, width), F32),
+           pltpu.VMEM((ROWS, width), F32), pltpu.VMEM((ROWS, hidden), F32), pltpu.VMEM((ROWS, width), F32)]
+        + [pltpu.VMEM(w.shape, BF16) for w in own]
+        + [pltpu.VMEM((ROWS, c), BF16) for c in (3 * width, width, hidden, width)]
         + [
             pltpu.VMEM((ROWS, width), F32), pltpu.VMEM((ROWS, width), F32),
             pltpu.VMEM((ROWS, width), BF16), pltpu.VMEM((2, ROWS, ROWS), F32),
-            pltpu.SemaphoreType.DMA((4,)),
+            DMA((9,)), DMA((4,)), DMA((4,)),
         ],
         compiler_params=pltpu.CompilerParams(vmem_limit_bytes=60 * 2**20),
         name="layer_backward",
-    )(x, grad, vec, q, k, v, probs, branch, middle, dact, branch2, *own, *other)
-
-
-MESH = pl.DeviceIdType.MESH
-SIDE = 2
-
-
-def remote(source, target, sent, came, **device):
-    return pltpu.make_async_remote_copy(
-        src_ref=source, dst_ref=target, send_sem=sent, recv_sem=came,
-        device_id=device, device_id_type=MESH,
-    )
+    )(*inputs)
 
 
 def add_rows(total, start, extra, count):
@@ -432,13 +610,21 @@
 
 
 def scatter_kernel(count, *refs):
-    first, second = refs[:8], refs[8:16]
-    out_qkv, out_proj, out_fc1, out_fc2 = refs[16:20]
-    held = refs[20:28]
-    sum_a, sum_b, sum_c = refs[28:31]
-    in_a1, in_a2, in_a3, in_b1, in_b2, in_b3, in_c1, in_c2, in_c3 = refs[31:40]
-    local_sem, swap_sent, swap_came = refs[40:43]
-    sent, came = refs[43:52], refs[52:61]
+    kept, back0, back1 = refs[:4], refs[4:8], refs[8:12]
+    small0, tg0, tl0, small1, tg1, tl1, index_g, index_l = refs[12:20]
+    outs_all, gx0, gx1, gcount, lcount = refs[20:25]
+    refs = refs[25:]
+    out_qkv, out_proj, out_fc1, out_fc2, out_g, out_l, gin_g, gin_l = refs[:8]
+    out_small, out_tg, out_tl = refs[8:19], *refs[19:21]
+    refs = refs[21:]
+    held = refs[:8]
+    sum_a, sum_b, sum_c = refs[8:11]
+    in_a1, in_a2, in_a3, in_b1, in_b2, in_b3, in_c1, in_c2, in_c3 = refs[11:20]
+    local_sem, swap_sent, swap_came = refs[20:23]
+    sent, came = refs[23:32], refs[32:41]
+    pair_small, pair_tg, pair_tl, pair_out, pair_gx, sums, slots_z, extra_sent, extra_came = refs[41:]
+    first = tuple(r.at[0] for r in kept) + tuple(back0)
+    second = tuple(r.at[1] for r in kept) + tuple(back1)
     depth = count // (SIDE * SIDE)
     width = held[0].shape[1]
     section = lax.axis_index("pipe")
@@ -461,6 +647,26 @@
         pl.semaphore_signal(barrier, inc=1, device_id={"dp": peer}, device_id_type=MESH)
     pl.semaphore_wait(barrier, 3 + depth - 1)
 
+    extras = (
+        (small0, small1, pair_small), (tg0, tg1, pair_tg), (tl0, tl1, pair_tl),
+        (outs_all.at[0], outs_all.at[1], pair_out), (gx0, gx1, pair_gx),
+    )
+
+    def extra_copy(i, layer):
+        return remote(
+            extras[i][layer], extras[i][2], extra_sent.at[i], extra_came.at[i], pipe=1 - section
+        )
+
+    @pl.when(section == 0)
+    def _():
+        for i in range(3):
+            extra_copy(i, 1).start()
+
+    @pl.when(section != 0)
+    def _():
+        for i in range(3):
+            extra_copy(i, 0).start()
+
     order = (0, 4, 2, 6, 1, 5, 3, 7)
     for i in order:
         mine = held[i].at[pl.ds(0, ROWS), :]
@@ -475,6 +681,101 @@
         def _():
             remote(first[i], theirs, swap_sent.at[i], swap_came.at[i], pipe=1 - section).start()
             pltpu.make_async_copy(second[i], mine, local_sem.at[i]).start()
+
+    @pl.when(section == 0)
+    def _():
+        for i in range(3, 5):
+            extra_copy(i, 1).start()
+
+    @pl.when(section != 0)
+    def _():
+        for i in range(3, 5):
+            extra_copy(i, 0).start()
+
+    def swapped_outputs():
+        extra_copy(3, 0).wait_recv()
+        extra_copy(4, 0).wait_recv()
+
+        def live(count_ref, crop):
+            return jnp.where(count_ref[0] > crop, 1.0, 0.0)
+
+        def place(crop, values, grads):
+            for out, gin, start, count_ref in ((out_g, gin_g, 0, gcount), (out_l, gin_l, LOCAL_ROW, lcount)):
+                rows = slice(start, start + out.shape[0])
+                out[:, crop, :] = (values[rows].astype(F32) * live(count_ref, crop)).astype(BF16)
+                gin[:, crop, :] = grads[rows]
+
+        @pl.when(section == 0)
+        def _():
+            place(0, outs_all[0], gx0[...])
+            place(1, pair_out[...], pair_gx[...])
+
+        @pl.when(section != 0)
+        def _():
+            place(0, pair_out[...], pair_gx[...])
+            place(1, outs_all[1], gx1[...])
+
+    def fold_back(mine, pair, index_ref, entries):
+        heads = pair.shape[1]
+
+        def one(r, result):
+            total = jnp.where(section == 0, mine[0][r], mine[1][r]) + pair[r]
+            high = total.astype(BF16)
+            low = (total - high.astype(F32)).astype(BF16)
+            spot = hot(index_ref[pl.ds(r, 1), :], entries)
+            return result + dot_cols(high, spot) + dot_cols(low, spot)
+
+        return lax.fori_loop(0, index_ref.shape[0], one, jnp.zeros((heads, entries), F32))
+
+    def small_start():
+        for i in range(3):
+            extra_copy(i, 0).wait_recv()
+        sums[0] = jnp.zeros((SMALL_ROWS, width), F32)
+        sums[0, 0:16, :] = jnp.where(section == 0, small0[...], small1[...]) + pair_small[...]
+        heads = pair_tg.shape[1]
+        sums[0, TABLE_ROW:TABLE_ROW + heads, :] = fold_back((tg0, tg1), pair_tg, index_g, width)
+        sums[0, TABLE_ROW_L:TABLE_ROW_L + heads, 0:128] = fold_back((tl0, tl1), pair_tl, index_l, 128)
+        small_x().start()
+
+    def small_x():
+        return remote(sums.at[0], sums.at[3], extra_sent.at[5], extra_came.at[5], dp=across_x)
+
+    def small_y():
+        return remote(sums.at[1], sums.at[4], extra_sent.at[6], extra_came.at[6], dp=across_y)
+
+    def small_z(step):
+        peer = index((z + step) % depth, y, x)
+        return remote(
+            sums.at[2], slots_z.at[z], extra_sent.at[6 + step], extra_came.at[6 + step], dp=peer
+        )
+
+    def small_second():
+        small_x().wait_recv()
+        sums[1] = sums[0] + sums[3]
+        small_y().start()
+
+    def small_third():
+        small_y().wait_recv()
+        sums[2] = sums[1] + sums[4]
+        for step in range(1, depth):
+            small_z(step).start()
+        slots_z[z] = sums[2]
+
+    def small_end():
+        for step in range(1, depth):
+            here = slots_z.at[(z + depth - step) % depth]
+            peer = index((z + step) % depth, y, x)
+            remote(here, here, extra_sent.at[6 + step], extra_came.at[6 + step], dp=peer).wait_recv()
+        total = slots_z[0]
+        for zz in range(1, depth):
+            total = total + slots_z[zz]
+        row = 0
+        for ref in out_small:
+            for b in range(0, ref.shape[1], width):
+                ref[:, b:b + width] = total[row:row + 1]
+                row += 1
+        for ref, start in ((out_tg, TABLE_ROW), (out_tl, TABLE_ROW_L)):
+            ref[:, 0, :] = total[start:start + ref.shape[0], 0:ref.shape[2]]
 
     def operands(*numbers):
         for i in numbers:
@@ -528,8 +829,10 @@
         accumulate(total, targets[k], yy, xx, here)
 
     c_parts = ((1 - y, 1 - x), (y, 1 - x), (1 - y, x), (y, x))
+    small_start()
     operands(0, 4)
     product(held[0], held[4], sum_c, 0)
+    small_second()
 
     @pl.when(starts_line)
     def _():
@@ -629,6 +932,7 @@
     operands(2, 6, 1, 5)
     product(held[2], held[6], sum_a, 0)
     product(held[1], held[5], sum_a, held[6].shape[1])
+    small_third()
     for i in range(2 * depth):
         first_copy(0, i).start()
     operands(3, 7)
@@ -636,6 +940,7 @@
     for i in range(2 * depth):
         first_copy(1, i).start()
 
+    swapped_outputs()
     for i in range(depth):
         first_receive(1, i)
         first_receive(0, i)
@@ -688,9 +993,16 @@
     line(0, depth - 1)
     copy_c3().wait_recv()
     out_qkv[...] = sum_c[chunk(sum_c, z, y, x), :].astype(F32) + in_c3[...].astype(F32)
+    small_end()
     finish(1)
     finish(0)
 
+    for i in range(5):
+        extra_copy(i, 0).wait_send()
+    small_x().wait_send()
+    small_y().wait_send()
+    for step in range(1, depth):
+        small_z(step).wait_send()
     for i in order:
         theirs = held[i].at[pl.ds(ROWS, ROWS), :]
         remote(first[i], theirs, swap_sent.at[i], swap_came.at[i], pipe=1 - section).wait_send()
@@ -710,42 +1022,121 @@
     copy_c3().wait_send()
 
 
-def scattered(count, first, second):
-    widths = [a.shape[1] for a in first]
+def scattered(count, kept, back0, back1, counts, tokens, entries):
+    lefts = [kept[i] for i in (1, 6, 9, 10)]
+    widths = [a.shape[2] for a in lefts] + [back0[i].shape[1] for i in (1, 2, 3, 4)]
     n1, merged, n2, act, gmixed, gbranch, ghidden, gb2 = widths
+    heads = back0[6].shape[1]
     depth = count // (SIDE * SIDE)
-    inside = pl.BlockSpec(memory_space=pltpu.VMEM)
-    outside = pl.BlockSpec(memory_space=pl.ANY)
     rows, rows_b = n1 // count, act // count
     cols_a = ghidden + gbranch
-    dma = pltpu.SemaphoreType.DMA
     copies = (2 * depth, depth, depth - 1, 2 * depth, depth, depth - 1, 4 * (depth - 1), 2, 1)
     arrivals = (2 * depth, depth, depth + 1, 2 * depth, depth, depth + 1, 4 * (depth + 1), 2, 1)
+    tokens_g, tokens_l = tokens
     return pl.pallas_call(
         functools.partial(scatter_kernel, count),
         out_shape=(
             shape(rows, gmixed, dtype=F32), shape(rows, gbranch, dtype=F32),
             shape(rows, ghidden, dtype=F32), shape(rows_b, gb2, dtype=F32),
+            shape(tokens_g, 2, n1), shape(tokens_l, 2, n1), shape(tokens_g, 2, n1), shape(tokens_l, 2, n1),
+            *(shape(1, n1, dtype=F32) for _ in range(10)), shape(1, act, dtype=F32),
+            shape(heads, 1, entries[0], dtype=F32), shape(heads, 1, entries[1], dtype=F32),
         ),
-        in_specs=[outside] * 16,
-        out_specs=(inside,) * 4,
+        in_specs=[OUTSIDE] * 12 + [INSIDE] * 11 + [SCALARS] * 2,
+        out_specs=(INSIDE,) * 21,
         scratch_shapes=[pltpu.VMEM((2 * ROWS, w), BF16) for w in widths]
         + [pltpu.VMEM((n1, cols_a), BF16), pltpu.VMEM((act, gb2), BF16), pltpu.VMEM((n1, gmixed), BF16)]
         + [pltpu.VMEM((slots, rows, cols_a), BF16) for slots in (2 * depth, depth, depth + 1)]
         + [pltpu.VMEM((slots, rows_b, gb2), BF16) for slots in (2 * depth, depth, depth + 1)]
         + [pltpu.VMEM((4 * (depth + 1), rows, gmixed), BF16), pltpu.VMEM((2, rows, gmixed), BF16),
            pltpu.VMEM((rows, gmixed), BF16)]
-        + [dma((8,)), dma((8,)), dma((8,))]
-        + [dma((c,)) for c in copies] + [dma((a,)) for a in arrivals],
+        + [DMA((8,)), DMA((8,)), DMA((8,))]
+        + [DMA((c,)) for c in copies] + [DMA((a,)) for a in arrivals]
+        + [
+            pltpu.VMEM((16, n1), F32), pltpu.VMEM((16, heads, LANES_G), F32),
+            pltpu.VMEM((8, heads, LANES_L), F32), pltpu.VMEM((ROWS, n1), BF16), pltpu.VMEM((ROWS, n1), BF16),
+            pltpu.VMEM((5, SMALL_ROWS, n1), F32), pltpu.VMEM((depth, SMALL_ROWS, n1), F32),
+            DMA((6 + depth,)), DMA((6 + depth,)),
+        ],
         compiler_params=pltpu.CompilerParams(
             vmem_limit_bytes=60 * 2**20, collective_id=1, has_side_effects=True
         ),
         name="gradient_scatter",
-    )(*first, *second)
+    )(
+        *lefts, *back0[1:5], *back1[1:5], *back0[5:8], *back1[5:8],
+        jnp.asarray(INDEX_G), jnp.asarray(INDEX_L), kept[0], back0[0], back1[0], *counts,
+    )
 
 
 def swapped(value):
     return lax.ppermute(value, "pipe", [(0, 1), (1, 0)])
+
+
+def plain_scattered(kept, back0, back1, counts, tokens, entries):
+    section = lax.axis_index("pipe")
+    tokens_g, tokens_l = tokens
+
+    def exchange(layer0, layer1):
+        keep = jnp.where(section == 0, layer0, layer1)
+        send = jnp.where(section == 0, layer1, layer0)
+        return keep, swapped(send)
+
+    lefts = [exchange(kept[i][0], kept[i][1]) for i in (1, 6, 9, 10)]
+    rights = [exchange(back0[i], back1[i]) for i in (1, 2, 3, 4)]
+    shares = [
+        lax.psum_scatter(
+            dot_rows(jnp.concatenate(a, 0), jnp.concatenate(b, 0)).astype(BF16),
+            "dp", scatter_dimension=0, tiled=True,
+        ).astype(F32)
+        for a, b in zip(lefts, rights)
+    ]
+    small, tg, tl = (a + b for a, b in (exchange(back0[i], back1[i]) for i in (5, 6, 7)))
+    width = small.shape[1]
+
+    def fold(values, index, count):
+        flat = jnp.transpose(values, (1, 0, 2)).reshape(values.shape[1], -1)
+        high = flat.astype(BF16)
+        low = (flat - high.astype(F32)).astype(BF16)
+        spot = hot(jnp.asarray(index.reshape(1, -1)), count)
+        sums = dot_cols(jnp.concatenate([high, low], 0), spot)
+        return sums[: values.shape[1]] + sums[values.shape[1]:]
+
+    small, tg, tl = lax.psum((small, fold(tg, INDEX_G, width), fold(tl, INDEX_L, 128)), "dp")
+
+    def both_crops(keep, came):
+        low = jnp.where(section == 0, keep, came)
+        high = jnp.where(section == 0, came, keep)
+        return (
+            jnp.stack([low[:tokens_g], high[:tokens_g]], 1),
+            jnp.stack([low[LOCAL_ROW:LOCAL_ROW + tokens_l], high[LOCAL_ROW:LOCAL_ROW + tokens_l]], 1),
+        )
+
+    out_g, out_l = both_crops(*exchange(kept[0][0], kept[0][1]))
+    crop = jnp.arange(2, dtype=jnp.int32)[None, :, None]
+    out_g = jnp.where(crop < counts[0][0], out_g, jnp.zeros_like(out_g))
+    out_l = jnp.where(crop < counts[1][0], out_l, jnp.zeros_like(out_l))
+    gin_g, gin_l = both_crops(*exchange(back0[0], back1[0]))
+    hidden = back0[3].shape[1]
+    rows = [small[i:i + 1] for i in range(F1B)]
+    rows.append(small[F1B:F1B + hidden // width].reshape(1, hidden))
+    tables = (tg[:, None, :entries[0]], tl[:, None, :entries[1]])
+    return (*shares, out_g, out_l, gin_g, gin_l, *rows, *tables)
+
+
+def finish_kernel(*refs):
+    half = len(refs) // 2
+    for source, target in zip(refs[:half], refs[half:]):
+        target[...] = source[...]
+
+
+def finished(arrays):
+    return pl.pallas_call(
+        finish_kernel,
+        out_shape=tuple(shape(*a.shape, dtype=a.dtype) for a in arrays),
+        in_specs=[INSIDE] * len(arrays),
+        out_specs=(INSIDE,) * len(arrays),
+        name="results",
+    )(*arrays)
 
 
 def body(
@@ -755,99 +1146,34 @@
     norm2_gain, norm2_shift, fc1_bias, fc2_bias, scale_mlp,
     table_global, table_local,
 ):
-    section = lax.axis_index("pipe")
     width = x_global.shape[2]
-    heads = table_global.shape[2]
-    tokens_g, tokens_l = x_global.shape[1], x_local.shape[1]
+    entries_g, heads = table_global.shape[1:]
+    entries_l = table_local.shape[1]
+    tokens = (x_global.shape[1], x_local.shape[1])
     own = (w_qkv[0], w_proj[0], w_fc1[0], w_fc2[0])
-    other = tuple(swapped(w) for w in own)
-    vec = jnp.concatenate(
-        [norm1_gain, norm1_shift, q_bias, v_bias, proj_bias, scale_attn, norm2_gain, norm2_shift,
-         fc2_bias, scale_mlp, fc1_bias.reshape(-1, width)], 0)
-    sg = spread(table_global[0], INDEX_G)
-    sl = spread(table_local[0], INDEX_L)
-    smalls_own = (vec, sg, sl)
-    smalls_other = tuple(swapped(s) for s in smalls_own)
-
-    def by_layer(mine, theirs):
-        first = jnp.where(section == 0, mine, theirs)
-        second = jnp.where(section == 0, theirs, mine)
-        return first, second
-
-    (vec0, vec1), (sg0, sg1), (sl0, sl1) = (by_layer(a, b) for a, b in zip(smalls_own, smalls_other))
-    vec0, vec1 = vec0.astype(F32), vec1.astype(F32)
-
-    def packed(array_g, array_l):
-        crop_g = lax.dynamic_index_in_dim(array_g, section, 0, keepdims=False)
-        crop_l = lax.dynamic_index_in_dim(array_l, section, 0, keepdims=False)
-        crop_g = jnp.pad(crop_g, ((0, LOCAL_ROW - tokens_g), (0, 0)))
-        crop_l = jnp.pad(crop_l, ((0, ROWS - LOCAL_ROW - tokens_l), (0, 0)))
-        return jnp.concatenate([crop_g, crop_l], 0)
-
-    x = packed(x_global, x_local)
-    live_g = (global_count[0] > section).astype(BF16)
-    live_l = (local_count[0] > section).astype(BF16)
-    cot = packed(cot_global * live_g, cot_local * live_l)
-
-    kept0 = forward(0, x, vec0, sg0, sl0, own, other)
-    first = kept0[0]
-    kept1 = forward(1, first, vec1, sg1, sl1, own, other)
-    second = kept1[0]
-    back1 = backward(1, first, cot, vec1, kept1, heads, own, other)
-    grad_first = back1[0]
-    back0 = backward(0, x, grad_first, vec0, kept0, heads, own, other)
-    grad_x = back0[0]
-
-    def exchange(layer0, layer1):
-        keep = jnp.where(section == 0, layer0, layer1)
-        send = jnp.where(section == 0, layer1, layer0)
-        return keep, swapped(send)
-
-    def both_crops(keep, came):
-        low = jnp.where(section == 0, keep, came)
-        high = jnp.where(section == 0, came, keep)
-        return (
-            jnp.stack([low[:tokens_g], high[:tokens_g]]),
-            jnp.stack([low[LOCAL_ROW:LOCAL_ROW + tokens_l], high[LOCAL_ROW:LOCAL_ROW + tokens_l]]),
-        )
-
-    out_g, out_l = both_crops(*exchange(first, second))
-    crop = jnp.arange(2, dtype=jnp.int32)[:, None, None]
-    out_g = jnp.where(crop < global_count[0], out_g, jnp.zeros_like(out_g))
-    out_l = jnp.where(crop < local_count[0], out_l, jnp.zeros_like(out_l))
-    gin_g, gin_l = both_crops(*exchange(grad_x, grad_first))
-
+    vec = (norm1_gain, norm1_shift, q_bias, v_bias, proj_bias, scale_attn, norm2_gain, norm2_shift,
+           fc2_bias, scale_mlp, fc1_bias)
+    tables = (table_global[0].T, table_local[0].T)
+    crops = tuple(jnp.transpose(a, (1, 0, 2)) for a in (x_global, x_local))
+    cots = tuple(jnp.transpose(a, (1, 0, 2)) for a in (cot_global, cot_local))
+    results = forward(*crops, vec, tables, own)
+    other, kept, vec = results[:4], results[4:17], results[17]
+    counts = (global_count, local_count)
+    back1 = backward(1, (*cots, *counts), kept[0], vec, kept, heads, own, other)
+    back0 = backward(0, back1[0], crops, vec, kept, heads, own, other)
     count = lax.axis_size("dp")
-    first_operands = [kept0[i] for i in (1, 6, 9, 10)] + [back0[i] for i in (1, 2, 3, 4)]
-    second_operands = [kept1[i] for i in (1, 6, 9, 10)] + [back1[i] for i in (1, 2, 3, 4)]
+    given = (kept, back0, back1, counts, tokens, (entries_g, entries_l))
     if count % (2 * SIDE * SIDE) == 0 and width % (16 * count) == 0:
-        shares = scattered(count, first_operands, second_operands)
+        results = finished(scattered(count, *given))
     else:
-        whole = [jnp.concatenate(exchange(a, b), 0) for a, b in zip(first_operands, second_operands)]
-        shares = [
-            lax.psum_scatter(
-                dot_rows(a, b).astype(BF16), "dp", scatter_dimension=0, tiled=True
-            ).astype(F32)
-            for a, b in zip(whole[:4], whole[4:])
-        ]
-    keep, came = [], []
-    for i in (5, 6, 7):
-        a, b = exchange(back0[i], back1[i])
-        keep.append(a)
-        came.append(b)
-    small, tg, tl = (a + b for a, b in zip(keep, came))
-    tg = gather_back(tg, INDEX_G, table_global.shape[1])
-    tl = gather_back(tl, INDEX_L, table_local.shape[1])
-    small, tg, tl = lax.psum((small, tg, tl), "dp")
-    hidden = fc1_bias.shape[1]
+        results = plain_scattered(*given)
+    shares, crops, small, tables = results[:4], results[4:8], results[8:19], results[19:]
+    vectors = [small[i] for i in (N1G, N1S, QB, VB, PB, SA, N2G, N2S, F1B, F2B, SM)]
     return (
-        out_g[None], out_l[None], gin_g[None], gin_l[None],
+        *(jnp.transpose(c, (1, 0, 2))[None] for c in crops),
         *(s[None] for s in shares),
-        small[N1G:N1G + 1], small[N1S:N1S + 1], small[QB:QB + 1], small[VB:VB + 1],
-        small[PB:PB + 1], small[SA:SA + 1], small[N2G:N2G + 1], small[N2S:N2S + 1],
-        small[F1B:F1B + hidden // width].reshape(1, hidden),
-        small[F2B:F2B + 1], small[SM:SM + 1],
-        tg[None], tl[None],
+        *vectors,
+        *(jnp.transpose(t, (1, 2, 0)) for t in tables),
     )
 
 

time: 387 us -> 236 us (0.61)
  the two profiles are of different devices: /device:TPU:0 before, /device:TPU:22 now
where the time goes in v3:
time: 236 us; the launch traced here: 233 us
  Pallas kernels  230 us (97%)
    pallas_call x1, Pallas kernels, scattered(): pl.pallas_call(functools.partial(scatter_kernel, count), out_shape=(shape...  150 us
    pallas_call x2, Pallas kernels, backward(): pl.pallas_call(kernel, out_shape=(shape(ROWS, width), shape(ROWS, 3 * wid...  42.3 us
    pallas_call x1, Pallas kernels, forward(): pl.pallas_call(kernel, out_shape=tuple((shape(*w.shape) for w in own)) +...  34.4 us

profile of v3, /device:TPU:22, one launch (start us, length us, event | category | flops | bytes accessed | tf_op | source)
XLA Modules:
  0.0 232.6 jit_solution(14696065407292970806)
XLA Ops:
  2.0 34.4 %forward_layers.1 = (bf16[768,2304]{1,0:T(8,128)(2,1)}, bf16[768,768]{1,0:T(8,128)(2,1)}, bf16[768,3072]{1,0:T(8,128)(2,1)}, bf16[3072,768]{1,0:T(8,128)(2,1)}, ...) custom-call(bf16[197,2,768]{2,1,0:T(2,128)(2,1)} %bitcast.44, ...), custom_call_target="tpu_custom_call" | custom-call | tf_op jit(solution)/shard_map/forward_layers/pallas_call | solution.py:547
  36.3 21.3 %layer_backward.2 = (bf16[256,768]{1,0:T(8,128)(2,1)}, bf16[256,2304]{1,0:T(8,128)(2,1)}, bf16[256,768]{1,0:T(8,128)(2,1)}, bf16[256,3072]{1,0:T(8,128)(2,1)}, b...) custom-call(bf16[197,2,768]{2,1,0:T(2,128)(2,1)} %bitcast.46, ...), custom_call_target="tpu_custom_call" | custom-call | tf_op jit(solution)/shard_map/layer_backward/pallas_call | solution.py:578
  57.7 21.0 %layer_backward.3 = (bf16[256,768]{1,0:T(8,128)(2,1)}, bf16[256,2304]{1,0:T(8,128)(2,1)}, bf16[256,768]{1,0:T(8,128)(2,1)}, bf16[256,3072]{1,0:T(8,128)(2,1)}, b...) custom-call(bf16[256,768]{1,0:T(8,128)(2,1)} %get-tuple-element.115.gin.refs_22_, ...), custom_call_target="tpu_custom_call" | custom-call | tf_op jit(solution)/shard_map/layer_backward/pallas_call | solution.py:578
  78.7 149.9 %gradient_scatter.1 = (f32[48,2304]{1,0:T(8,128)}, f32[48,768]{1,0:T(8,128)}, f32[48,3072]{1,0:T(8,128)}, f32[192,768]{1,0:T(8,128)}, bf16[197,2,768]{2,1,0:T(2,...) custom-call(bf16[2,256,768]{2,1,0:T(8,128)(2,1)} %get-tuple-element., ...), custom_call_target="tpu_custom_call" | custom-call | tf_op jit(solution)/shard_map/gradient_scatter/pallas_call | solution.py:1036
  228.6 3.8 %results.1 = (f32[48,2304]{1,0:T(8,128)}, f32[48,768]{1,0:T(8,128)}, f32[48,3072]{1,0:T(8,128)}, f32[192,768]{1,0:T(8,128)}, bf16[197,2,768]{2,1,0:T(2,128)(2,1)...) custom-call(f32[48,2304]{1,0:T(8,128)} %get-tuple-element.131.refs_0, ...), custom_call_target="tpu_custom_call" | custom-call | tf_op jit(solution)/shard_map/results/pallas_call | solution.py:1133

commit v4 on v3

--- a/solution.py
+++ b/solution.py
@@ -97,6 +97,7 @@
 
 MESH = pl.DeviceIdType.MESH
 SIDE = 2
+FLIGHT = 4
 TABLE_ROW, TABLE_ROW_L, SMALL_ROWS = 16, 32, 48
 
 
@@ -122,14 +123,14 @@
 
 
 def forward_kernel(
-    scale,
+    scale, keep_both,
     xg_ref, xl_ref, vec_refs, tg_ref, tl_ref, index_g, index_l, own_qkv, own_proj, own_fc1, own_fc2,
     oth_qkv, oth_proj, oth_fc1, oth_fc2,
     out_all, n1_all, q_all, k_all, v_all, p_all, merged_all, branch_all, middle_all,
     n2_all, act_all, dact_all, branch2_all, small_out,
     w_qkv, w_proj, w_fc1, w_fc2, small_in, small, vec_all, x_in, out_ref, n1_ref, q_ref, k_ref, v_ref, p_ref,
     merged_ref, branch_ref, middle_ref, n2_ref, act_ref, dact_ref, branch2_ref,
-    spread_g, spread_l, bias, own_sem, sent, came, keep_sem, store_sem, small_sem,
+    spread_g, spread_l, bias, own_sem, sent, came, keep_sem, store_sem, give_sent, give_came, small_sem,
 ):
     section = lax.axis_index("pipe")
     partner = 1 - section
@@ -137,7 +138,7 @@
     oth = (oth_qkv, oth_proj, oth_fc1, oth_fc2)
     held = (w_qkv, w_proj, w_fc1, w_fc2)
     width = x_in.shape[1]
-    heads = p_ref.shape[0]
+    heads = p_ref.shape[1]
     half = SMALL_ROWS
 
     barrier = pltpu.get_barrier_semaphore()
@@ -169,39 +170,66 @@
     small_out[...] = vec_all[...]
     tables_g = jnp.concatenate(
         [small[TABLE_ROW:TABLE_ROW + 16, :], small[half + TABLE_ROW:half + TABLE_ROW + 16, :]], 0
-    ).astype(BF16)
+    )
     tables_l = jnp.concatenate(
         [small[TABLE_ROW_L:TABLE_ROW_L + 16, :128], small[half + TABLE_ROW_L:half + TABLE_ROW_L + 16, :128]], 0
-    ).astype(BF16)
-    for r in range(16):
-        found = dot(tables_g, hot(index_g[r:r + 1, :], width))
-        spread_g[0, :, r, :] = found[:16]
-        spread_g[1, :, r, :] = found[16:]
-    for r in range(8):
-        found = dot(tables_l, hot(index_l[r:r + 1, :], 128))
-        spread_l[0, :, r, :] = found[:16]
-        spread_l[1, :, r, :] = found[16:]
-
-    stores = (
-        (out_ref, out_all), (n1_ref, n1_all), (q_ref, q_all), (k_ref, k_all), (v_ref, v_all),
-        (p_ref, p_all), (merged_ref, merged_all), (branch_ref, branch_all), (middle_ref, middle_all),
-        (n2_ref, n2_all), (act_ref, act_all), (dact_ref, dact_all), (branch2_ref, branch2_all),
+    )
+    for tables, index_ref, spread, grid, cls_lane in (
+        (tables_g, index_g, spread_g, GRID_G, 0), (tables_l, index_l, spread_l, GRID_L, LOCAL_ROW - 128),
+    ):
+        span, lanes = tables.shape[1], index_ref.shape[1]
+        shifted = [tables] + [pltpu.roll(tables, span - r, 1) for r in range(1, grid)]
+        found = dot(jnp.concatenate(shifted, 0).astype(BF16), hot(index_ref[0:1, :], span))
+        cls = (2 * grid - 1) ** 2
+        lane_all = lax.broadcasted_iota(jnp.int32, (1, lanes), 1)
+        to_patch = jnp.where(lane_all == cls_lane, tables[:, cls + 2:cls + 3], tables[:, cls:cls + 1])
+        to_class = jnp.broadcast_to(tables[:, cls + 1:cls + 2], to_patch.shape)
+        for layer in range(2):
+            for r in range(grid):
+                spread[layer, :, r, :] = found[32 * r + 16 * layer:32 * r + 16 * layer + 16]
+            spread[layer, :, grid, :] = to_patch[16 * layer:16 * layer + 16]
+            spread[layer, :, grid + 1, :] = to_class[16 * layer:16 * layer + 16]
+
+    slots = (
+        out_ref, n1_ref, q_ref, k_ref, v_ref, p_ref, merged_ref, branch_ref, middle_ref,
+        n2_ref, act_ref, dact_ref, branch2_ref,
+    )
+    results = (
+        out_all, n1_all, q_all, k_all, v_all, p_all, merged_all, branch_all, middle_all,
+        n2_all, act_all, dact_all, branch2_all,
     )
     OUT, N1, Q, K, V, PR, ME, BR, MI, N2, AC, DA, B2 = range(13)
+    GIVEN = (OUT, N1, ME, N2, AC)
 
     def store_copy(number, layer):
-        source, target = stores[number]
-        if number == OUT:
-            source = source.at[layer]
-        return pltpu.make_async_copy(source, target.at[layer], store_sem.at[number])
+        return pltpu.make_async_copy(
+            slots[number].at[layer], results[number].at[layer], store_sem.at[layer, number]
+        )
+
+    def give_copy(number, layer):
+        spot = number if layer == 0 else 13 + GIVEN.index(number)
+        return remote(
+            slots[number].at[layer], results[number].at[2], give_sent.at[spot], give_came.at[spot],
+            pipe=partner,
+        )
 
     def store(layer, *numbers):
         for number in numbers:
             store_copy(number, layer).start()
+            if layer == 0 or number in GIVEN:
+
+                @pl.when(section != layer)
+                def _():
+                    give_copy(number, layer).start()
 
     def stored(layer, *numbers):
         for number in numbers:
             store_copy(number, layer).wait()
+            if layer == 0 or number in GIVEN:
+
+                @pl.when(section != layer)
+                def _():
+                    give_copy(number, layer).wait_send()
 
     def weight(i, layer):
         @pl.when(section == layer)
@@ -212,11 +240,16 @@
         def _():
             here = held[i].at[partner]
             remote(here, here, sent.at[i], came.at[i], pipe=partner).wait_recv()
-            pltpu.make_async_copy(here, oth[i], keep_sem.at[i]).start()
+            if layer == 1 or keep_both:
+                pltpu.make_async_copy(here, oth[i], keep_sem.at[i]).start()
 
     lane = lax.broadcasted_iota(jnp.int32, (1, 128), 1)
     for layer in range(2):
-        entering = x_in if layer == 0 else out_ref.at[0]
+        entering = x_in if layer == 0 else slots[OUT].at[0]
+        (
+            out_ref, n1_ref, q_ref, k_ref, v_ref, p_ref, merged_ref, branch_ref, middle_ref,
+            n2_ref, act_ref, dact_ref, branch2_ref,
+        ) = (slot.at[layer] for slot in slots)
         base = layer * half
 
         def vec(row):
@@ -250,8 +283,9 @@
                 )
                 expo = jnp.exp(scores - jnp.max(scores, axis=-1, keepdims=True))
                 probs = expo * (1.0 / jnp.sum(expo, axis=-1, keepdims=True))
-                p_ref[head] = probs
-                piece = dot(probs.astype(BF16), jnp.where(mine, v, jnp.zeros_like(v)))
+                low = probs.astype(BF16)
+                p_ref[head] = low
+                piece = dot(low, jnp.where(mine, v, jnp.zeros_like(v)))
                 result = piece if result is None else result + piece
             merged_ref[:, cols] = result.astype(BF16)
         store(layer, PR, ME)
@@ -271,8 +305,6 @@
         row_steps(32, norm2)
         store(layer, N2)
         weight(2, layer)
-        if layer == 1:
-            stored(0, AC, DA, B2)
         n2 = n2_ref[...]
         for b in range(0, w_fc1.shape[2], BLOCK):
             cols = slice(b, b + BLOCK)
@@ -280,107 +312,61 @@
             hidden = dot(n2, w_fc1[layer, :, cols]) + vec(F1B + part)[:, b - part * width:b - part * width + BLOCK]
             cdf = 0.5 + 0.5 * lax.erf(hidden * INV_SQRT2)
             act_ref[:, cols] = (hidden * cdf).astype(BF16)
-            dact_ref[:, cols] = cdf + hidden * (INV_SQRT_2PI * jnp.exp(-0.5 * hidden * hidden))
+            slope = cdf + hidden * (INV_SQRT_2PI * jnp.exp(-0.5 * hidden * hidden))
+            dact_ref[:, cols] = slope.astype(BF16)
         store(layer, AC, DA)
         weight(3, layer)
         for b in range(0, width, BLOCK):
             cols = slice(b, b + BLOCK)
             branch2 = dot(act_ref[...], w_fc2[layer, :, cols]) + vec(F2B)[:, cols]
             branch2_ref[:, cols] = branch2
-            out_ref[layer, :, cols] = (middle_ref[:, cols] + vec(SM)[:, cols] * branch2).astype(BF16)
+            out_ref[:, cols] = (middle_ref[:, cols] + vec(SM)[:, cols] * branch2).astype(BF16)
         store(layer, B2, OUT)
-        if layer == 0:
-            stored(0, N1, Q, K, V, PR, ME, BR, MI, N2, OUT)
+    stored(0, *range(13))
     stored(1, *range(13))
     for i in range(4):
         weight_copy(i).wait_send()
-        pltpu.make_async_copy(held[i].at[partner], oth[i], keep_sem.at[i]).wait()
     small_copy.wait_send()
 
-
-def backward_kernel(
-    layer, scale, *refs,
+    def weights_kept():
+        for i in range(4):
+            pltpu.make_async_copy(held[i].at[partner], oth[i], keep_sem.at[i]).wait()
+
+    @pl.when(section == 0)
+    def _():
+        weights_kept()
+        for number in range(13):
+            give_copy(number, 0).wait_recv()
+
+    @pl.when(section != 0)
+    def _():
+        if keep_both:
+            weights_kept()
+        for number in GIVEN:
+            give_copy(number, 1).wait_recv()
+
+
+X, Q, K, V, PR, BR, MI, DA, B2 = range(9)
+
+
+def clear(*refs):
+    for ref in refs:
+        ref[...] = jnp.zeros_like(ref)
+
+
+def backward_steps(
+    scale, vec, weight, loaded, done, g_ref, gx_ref, kept, weights, grads, sums, scratch,
 ):
-    if layer == 1:
-        cg_ref, cl_ref, gcount, lcount = refs[:4]
-        refs = refs[4:]
-    else:
-        gin_ref, refs = refs[0], refs[1:]
-    vec_all, x_all, q_all, k_all, v_all, p_all, branch_all, middle_all, dact_all, branch2_all = refs[:10]
-    own, oth = refs[10:14], refs[14:18]
-    gx_ref, gmixed_out, gbranch_out, ghidden_out, gb2_out, small_ref, tg_ref, tl_ref = refs[18:26]
-    (
-        g_ref, x_ref, q_ref, k_ref, v_ref, p_ref, branch_ref, middle_ref, dact_ref, branch2_ref,
-        w_qkv, w_proj, w_fc1, w_fc2, gmixed_ref, gbranch_ref, ghidden_ref, gb2_ref,
-        gmid, gnorm, gmerged, gs_ref, load_sem, weight_sem, store_sem,
-    ) = refs[26:]
-    section = lax.axis_index("pipe")
-    held = (w_qkv, w_proj, w_fc1, w_fc2)
-    loads = (
-        (x_all, x_ref), (q_all, q_ref), (k_all, k_ref), (v_all, v_ref), (p_all, p_ref),
-        (branch_all, branch_ref), (middle_all, middle_ref), (dact_all, dact_ref), (branch2_all, branch2_ref),
-    )
-    X, Q, K, V, PR, BR, MI, DA, B2 = range(9)
-
-    def load_copy(number):
-        source, target = loads[number]
-        if layer == 1 or number != X:
-            source = source.at[0 if number == X else layer]
-        return pltpu.make_async_copy(source, target, load_sem.at[number])
-
-    def load_weight(i):
-        @pl.when(section == layer)
-        def _():
-            pltpu.make_async_copy(own[i], held[i], weight_sem.at[i]).start()
-
-        @pl.when(section != layer)
-        def _():
-            pltpu.make_async_copy(oth[i], held[i], weight_sem.at[i]).start()
-
-    def weight(i):
-        pltpu.make_async_copy(own[i], held[i], weight_sem.at[i]).wait()
-
-    def loaded(*numbers):
-        for number in numbers:
-            load_copy(number).wait()
-
-    load_copy(B2).start()
-    load_weight(3)
-    load_copy(DA).start()
-    load_weight(2)
-    for number in (MI, BR):
-        load_copy(number).start()
-    load_weight(1)
-    for number in (V, PR, K, Q):
-        load_copy(number).start()
-    load_weight(0)
-    if layer == 1:
-        load_copy(X).start()
-
+    x_ref, q_ref, k_ref, v_ref, p_ref, branch_ref, middle_ref, dact_ref, branch2_ref = kept
+    w_qkv, w_proj, w_fc1, w_fc2 = weights
+    gmixed_ref, gbranch_ref, ghidden_ref, gb2_ref = grads
+    small_ref, tg_ref, tl_ref = sums
+    gmid, gnorm, gmerged = scratch
     width = g_ref.shape[1]
     heads = p_ref.shape[0]
-    small_ref[...] = jnp.zeros_like(small_ref)
-
-    def vec(row):
-        return vec_all[layer * SMALL_ROWS + row:layer * SMALL_ROWS + row + 1, :]
 
     def add_small(row, values):
         small_ref[row:row + 1, :] += jnp.sum(values, axis=0, keepdims=True)
-
-    if layer == 1:
-        live_g = jnp.where(gcount[0] > section, 1.0, 0.0)
-        live_l = jnp.where(lcount[0] > section, 1.0, 0.0)
-        place_crops(g_ref, cg_ref, cl_ref, section, live_g, live_l)
-    else:
-        g_ref = gin_ref
-        place_crops(x_ref, *x_all, section)
-
-    stores = (
-        (gmixed_ref, gmixed_out), (gbranch_ref, gbranch_out), (ghidden_ref, ghidden_out), (gb2_ref, gb2_out),
-    )
-
-    def store_copy(number):
-        return pltpu.make_async_copy(*stores[number], store_sem.at[number])
 
     loaded(B2)
 
@@ -392,7 +378,7 @@
         add_small(F2B, low.astype(F32))
 
     row_steps(32, scaled)
-    store_copy(3).start()
+    done(3, B2)
     weight(3)
     loaded(DA)
     gb2 = gb2_ref[...]
@@ -401,10 +387,10 @@
         part = b // width
         ghidden = (dot_cols(gb2, w_fc2[cols, :]) * dact_ref[:, cols]).astype(BF16)
         ghidden_ref[:, cols] = ghidden
-        small_ref[F1B + part:F1B + part + 1, b - part * width:b - part * width + BLOCK] = jnp.sum(
+        small_ref[F1B + part:F1B + part + 1, b - part * width:b - part * width + BLOCK] += jnp.sum(
             ghidden.astype(F32), axis=0, keepdims=True
         )
-    store_copy(2).start()
+    done(2, DA)
     weight(2)
     for b in range(0, width, BLOCK):
         gnorm[:, b:b + BLOCK] = dot_cols(ghidden_ref[...], w_fc1[b:b + BLOCK, :])
@@ -431,7 +417,7 @@
         add_small(PB, low.astype(F32))
 
     row_steps(32, norm2)
-    store_copy(1).start()
+    done(1, MI, BR)
     weight(1)
     for b in range(0, width, BLOCK):
         gmerged[:, b:b + BLOCK] = dot_cols(gbranch_ref[...], w_proj[b:b + BLOCK, :]).astype(BF16)
@@ -449,15 +435,16 @@
             def only(values):
                 return jnp.where(mine, values, jnp.zeros_like(values))
 
-            probs = p_ref[head]
+            low = p_ref[head]
+            probs = low.astype(F32)
             grad_probs = dot_cols(gm, only(v))
             total = jnp.sum(probs * grad_probs, axis=-1, keepdims=True)
             gscores = (probs * (grad_probs - total)).astype(BF16)
-            gv += dot_rows(probs.astype(BF16), only(gm))
+            gv += dot_rows(low, only(gm))
             gq += dot(gscores, only(k))
             gk += dot_rows(gscores, only(q))
             wide = gscores.astype(F32)
-            gs = gs_ref.at[head % 2]
+            gs = gnorm.at[:, pl.ds(ROWS * (head % 2), ROWS)]
             gs[...] = jnp.where((lane_all == 0) | (lane_all == LOCAL_ROW), 0.0, wide)
             acc = jnp.zeros((GRID_G, LANES_G), F32)
             for r in range(GRID_G):
@@ -468,9 +455,9 @@
             to_class = jnp.sum(wide[:LOCAL_ROW, :], axis=0, keepdims=True) - first_row
             to_class = jnp.where(lane_all == 0, to_class, 0.0)
             blank = jnp.zeros((1, LANES_G - ROWS), F32)
-            tg_ref[0:GRID_G, head, :] = acc
-            tg_ref[14, head:head + 1, :] = jnp.concatenate([first_row, blank], 1)
-            tg_ref[15, head:head + 1, :] = jnp.concatenate([to_class, blank], 1)
+            tg_ref[0:GRID_G, head, :] += acc
+            tg_ref[14, head:head + 1, :] += jnp.concatenate([first_row, blank], 1)
+            tg_ref[15, head:head + 1, :] += jnp.concatenate([to_class, blank], 1)
             acc = jnp.zeros((GRID_L, LANES_L), F32)
             for r in range(GRID_L):
                 block = gs[pl.ds(LOCAL_ROW + 1 + GRID_L * r, GRID_L), pl.ds(128, 128)]
@@ -478,9 +465,9 @@
             first_row = wide[LOCAL_ROW:LOCAL_ROW + 1, 128:]
             to_class = jnp.sum(wide[LOCAL_ROW:, 128:], axis=0, keepdims=True) - first_row
             to_class = jnp.where(lane == LOCAL_ROW - 128, to_class, 0.0)
-            tl_ref[0:GRID_L, head, :] = acc
-            tl_ref[6, head:head + 1, :] = first_row
-            tl_ref[7, head:head + 1, :] = to_class
+            tl_ref[0:GRID_L, head, :] += acc
+            tl_ref[6, head:head + 1, :] += first_row
+            tl_ref[7, head:head + 1, :] += to_class
         gmixed_ref[:, cols] = gq.astype(BF16) * jnp.asarray(scale, BF16)
         gmixed_ref[:, slice(width + cols.start, width + cols.stop)] = gk.astype(BF16)
         gmixed_ref[:, slice(2 * width + cols.start, 2 * width + cols.stop)] = gv.astype(BF16)
@@ -489,11 +476,10 @@
         add_small(QB, gmixed_ref[rows, :width].astype(F32))
         add_small(VB, gmixed_ref[rows, 2 * width:].astype(F32))
 
-    store_copy(0).start()
+    done(0, V, PR, K, Q)
     row_steps(32, biases)
     weight(0)
-    if layer == 1:
-        loaded(X)
+    loaded(X)
     for b in range(0, width, BLOCK):
         gnorm[:, b:b + BLOCK] = dot_cols(gmixed_ref[...], w_qkv[b:b + BLOCK, :])
 
@@ -505,6 +491,80 @@
         gx_ref[rows, :] = (gmid[rows, :] + through).astype(BF16)
 
     row_steps(32, norm1)
+
+
+def backward_kernel(
+    layer, scale, given, vec_all,
+    x_all, q_all, k_all, v_all, p_all, branch_all, middle_all, dact_all, branch2_all,
+    own_qkv, own_proj, own_fc1, own_fc2, oth_qkv, oth_proj, oth_fc1, oth_fc2,
+    gx_ref, gmixed_out, gbranch_out, ghidden_out, gb2_out, small_ref, tg_ref, tl_ref,
+    g_ref, x_ref, q_ref, k_ref, v_ref, p_ref, branch_ref, middle_ref, dact_ref, branch2_ref,
+    w_qkv, w_proj, w_fc1, w_fc2, gmixed_ref, gbranch_ref, ghidden_ref, gb2_ref,
+    gmid, gnorm, gmerged, load_sem, weight_sem, store_sem,
+):
+    own = (own_qkv, own_proj, own_fc1, own_fc2)
+    oth = (oth_qkv, oth_proj, oth_fc1, oth_fc2)
+    section = lax.axis_index("pipe")
+    held = (w_qkv, w_proj, w_fc1, w_fc2)
+    kept = (x_ref, q_ref, k_ref, v_ref, p_ref, branch_ref, middle_ref, dact_ref, branch2_ref)
+    sources = (x_all, q_all, k_all, v_all, p_all, branch_all, middle_all, dact_all, branch2_all)
+    grads = (gmixed_ref, gbranch_ref, ghidden_ref, gb2_ref)
+    targets = (gmixed_out, gbranch_out, ghidden_out, gb2_out)
+
+    def load_copy(number):
+        source = sources[number].at[0 if number == X else layer]
+        return pltpu.make_async_copy(source, kept[number], load_sem.at[number])
+
+    def load_weight(i):
+        @pl.when(section == layer)
+        def _():
+            pltpu.make_async_copy(own[i], held[i], weight_sem.at[i]).start()
+
+        @pl.when(section != layer)
+        def _():
+            pltpu.make_async_copy(oth[i], held[i], weight_sem.at[i]).start()
+
+    def weight(i):
+        pltpu.make_async_copy(own[i], held[i], weight_sem.at[i]).wait()
+
+    def loaded(*numbers):
+        for number in numbers:
+            if layer == 1 or number != X:
+                load_copy(number).wait()
+
+    def store_copy(number):
+        return pltpu.make_async_copy(grads[number], targets[number], store_sem.at[number])
+
+    def done(number, *unused):
+        store_copy(number).start()
+
+    def vec(row):
+        return vec_all[layer * SMALL_ROWS + row:layer * SMALL_ROWS + row + 1, :]
+
+    load_copy(B2).start()
+    load_weight(3)
+    load_copy(DA).start()
+    load_weight(2)
+    for number in (MI, BR):
+        load_copy(number).start()
+    load_weight(1)
+    for number in (V, PR, K, Q):
+        load_copy(number).start()
+    load_weight(0)
+    clear(small_ref, tg_ref, tl_ref)
+    if layer == 1:
+        cg_ref, cl_ref, gcount, lcount = given
+        load_copy(X).start()
+        live_g = jnp.where(gcount[0] > section, 1.0, 0.0)
+        live_l = jnp.where(lcount[0] > section, 1.0, 0.0)
+        place_crops(g_ref, cg_ref, cl_ref, section, live_g, live_l)
+    else:
+        g_ref, xg_ref, xl_ref = given
+        place_crops(x_ref, xg_ref, xl_ref, section)
+    backward_steps(
+        scale, vec, weight, loaded, done, g_ref, gx_ref, kept, held, grads,
+        (small_ref, tg_ref, tl_ref), (gmid, gnorm, gmerged),
+    )
     for number in range(4):
         store_copy(number).wait()
 
@@ -519,35 +579,35 @@
 DMA = pltpu.SemaphoreType.DMA
 
 
-def forward(x_global, x_local, vec, tables, own):
+def forward(x_global, x_local, vec, tables, own, keep_both):
     width = x_global.shape[2]
     heads = tables[0].shape[0]
     hidden = own[2].shape[1]
     scale = (width // heads) ** (-0.5)
     kept = (
         ((ROWS, width), BF16), ((ROWS, width), BF16), ((ROWS, width), BF16), ((ROWS, width), BF16),
-        ((ROWS, width), BF16), ((heads, ROWS, ROWS), F32), ((ROWS, width), BF16),
+        ((ROWS, width), BF16), ((heads, ROWS, ROWS), BF16), ((ROWS, width), BF16),
         ((ROWS, width), F32), ((ROWS, width), F32), ((ROWS, width), BF16),
-        ((ROWS, hidden), BF16), ((ROWS, hidden), F32), ((ROWS, width), F32),
+        ((ROWS, hidden), BF16), ((ROWS, hidden), BF16), ((ROWS, width), F32),
     )
     scratch = [pltpu.VMEM((2, *w.shape), BF16) for w in own]
     scratch += [pltpu.VMEM((SMALL_ROWS, width), F32)] + [pltpu.VMEM((2 * SMALL_ROWS, width), F32)] * 2
-    scratch += [pltpu.VMEM((ROWS, width), BF16), pltpu.VMEM((2, ROWS, width), BF16)]
-    scratch += [pltpu.VMEM(dims, kind) for dims, kind in kept[1:]]
+    scratch += [pltpu.VMEM((ROWS, width), BF16)]
+    scratch += [pltpu.VMEM((2, *dims), kind) for dims, kind in kept]
     scratch += [
         pltpu.VMEM((2, 16, 16, LANES_G), F32), pltpu.VMEM((2, 16, 8, LANES_L), F32),
         pltpu.VMEM((2, ROWS, ROWS), F32),
-        DMA((4,)), DMA((4,)), DMA((4,)), DMA((4,)), DMA((13,)), DMA((2,)),
+        DMA((4,)), DMA((4,)), DMA((4,)), DMA((4,)), DMA((2, 13)), DMA((18,)), DMA((18,)), DMA((2,)),
     ]
 
     def kernel(xg, xl, *refs):
         count = len(vec)
-        forward_kernel(scale, xg, xl, refs[:count], *refs[count:])
+        forward_kernel(scale, keep_both, xg, xl, refs[:count], *refs[count:])
 
     return pl.pallas_call(
         kernel,
         out_shape=tuple(shape(*w.shape) for w in own)
-        + tuple(shape(2, *dims, dtype=kind) for dims, kind in kept)
+        + tuple(shape(3, *dims, dtype=kind) for dims, kind in kept)
         + (shape(2 * SMALL_ROWS, width, dtype=F32),),
         in_specs=[INSIDE] * (6 + len(vec)) + [OUTSIDE] * 4,
         out_specs=(OUTSIDE,) * 17 + (INSIDE,),
@@ -559,44 +619,46 @@
     )(x_global, x_local, *vec, *tables, jnp.asarray(INDEX_G), jnp.asarray(INDEX_L), *own)
 
 
-def backward(layer, grads, entering, vec, kept, heads, own, other):
+def backward(layer, given, vec, kept, heads, own, other):
     width = vec.shape[1]
     hidden = own[2].shape[1]
     scale = (width // heads) ** (-0.5)
-    _, n1, q, k, v, probs, merged, branch, middle, n2, act, dact, branch2 = kept
-    if layer == 1:
-        inputs = (*grads, vec, entering, q, k, v, probs, branch, middle, dact, branch2, *own, *other)
-        specs = [INSIDE] * 2 + [SCALARS] * 2 + [INSIDE] + [OUTSIDE] * 17
-        kernel = functools.partial(backward_kernel, 1, scale)
-    else:
-        inputs = (grads, vec, *entering, q, k, v, probs, branch, middle, dact, branch2, *own, *other)
-        specs = [INSIDE] * 4 + [OUTSIDE] * 16
-
-        def kernel(gin, vec_all, xg, xl, *refs):
-            backward_kernel(0, scale, gin, vec_all, (xg, xl), *refs)
+    first, n1, q, k, v, probs, merged, branch, middle, n2, act, dact, branch2 = kept
+    count = len(given)
+
+    def kernel(*refs):
+        backward_kernel(layer, scale, refs[:count], *refs[count:])
 
     return pl.pallas_call(
         kernel,
         out_shape=(
             shape(ROWS, width), shape(ROWS, 3 * width), shape(ROWS, width), shape(ROWS, hidden),
             shape(ROWS, width), shape(16, width, dtype=F32),
-            shape(16, heads, LANES_G, dtype=F32), shape(8, heads, LANES_L, dtype=F32),
+            shape(16, 16, LANES_G, dtype=F32), shape(8, 16, LANES_L, dtype=F32),
         ),
-        in_specs=specs,
+        in_specs=[SCALARS if g.ndim == 1 else INSIDE for g in given] + [INSIDE] + [OUTSIDE] * 17,
         out_specs=(INSIDE,) + (OUTSIDE,) * 4 + (INSIDE,) * 3,
-        scratch_shapes=[pltpu.VMEM((ROWS, width), BF16) for _ in range(5)]
-        + [pltpu.VMEM((heads, ROWS, ROWS), F32), pltpu.VMEM((ROWS, width), F32),
-           pltpu.VMEM((ROWS, width), F32), pltpu.VMEM((ROWS, hidden), F32), pltpu.VMEM((ROWS, width), F32)]
+        scratch_shapes=[pltpu.VMEM((ROWS, width), BF16)] + kept_scratch(heads, width, hidden)
         + [pltpu.VMEM(w.shape, BF16) for w in own]
         + [pltpu.VMEM((ROWS, c), BF16) for c in (3 * width, width, hidden, width)]
-        + [
-            pltpu.VMEM((ROWS, width), F32), pltpu.VMEM((ROWS, width), F32),
-            pltpu.VMEM((ROWS, width), BF16), pltpu.VMEM((2, ROWS, ROWS), F32),
-            DMA((9,)), DMA((4,)), DMA((4,)),
-        ],
+        + work_scratch(width) + [DMA((9,)), DMA((4,)), DMA((4,))],
         compiler_params=pltpu.CompilerParams(vmem_limit_bytes=60 * 2**20),
         name="layer_backward",
-    )(*inputs)
+    )(*given, vec, first, q, k, v, probs, branch, middle, dact, branch2, *own, *other)
+
+
+def kept_scratch(heads, width, hidden):
+    return [pltpu.VMEM((ROWS, width), BF16) for _ in range(4)] + [
+        pltpu.VMEM((heads, ROWS, ROWS), BF16), pltpu.VMEM((ROWS, width), F32),
+        pltpu.VMEM((ROWS, width), F32), pltpu.VMEM((ROWS, hidden), BF16), pltpu.VMEM((ROWS, width), F32),
+    ]
+
+
+def work_scratch(width):
+    return [
+        pltpu.VMEM((ROWS, width), F32), pltpu.VMEM((ROWS, width), F32),
+        pltpu.VMEM((ROWS, width), BF16),
+    ]
 
 
 def add_rows(total, start, extra, count):
@@ -609,11 +671,10 @@
     lax.fori_loop(0, count // 16, one, 0)
 
 
-def scatter_kernel(count, *refs):
-    kept, back0, back1 = refs[:4], refs[4:8], refs[8:12]
-    small0, tg0, tl0, small1, tg1, tl1, index_g, index_l = refs[12:20]
-    outs_all, gx0, gx1, gcount, lcount = refs[20:25]
-    refs = refs[25:]
+def scatter_kernel(count, scale, *refs):
+    lefts, back1, kept_all, own = refs[:4], refs[4:8], refs[8:16], refs[16:20]
+    small1, tg1, tl1, index_g, index_l, outs_all, gx1, vec_all, xg_ref, xl_ref, gcount, lcount = refs[20:32]
+    refs = refs[32:]
     out_qkv, out_proj, out_fc1, out_fc2, out_g, out_l, gin_g, gin_l = refs[:8]
     out_small, out_tg, out_tl = refs[8:19], *refs[19:21]
     refs = refs[21:]
@@ -622,9 +683,9 @@
     in_a1, in_a2, in_a3, in_b1, in_b2, in_b3, in_c1, in_c2, in_c3 = refs[11:20]
     local_sem, swap_sent, swap_came = refs[20:23]
     sent, came = refs[23:32], refs[32:41]
-    pair_small, pair_tg, pair_tl, pair_out, pair_gx, sums, slots_z, extra_sent, extra_came = refs[41:]
-    first = tuple(r.at[0] for r in kept) + tuple(back0)
-    second = tuple(r.at[1] for r in kept) + tuple(back1)
+    small_ref, tg_ref, tl_ref, pair_small, pair_tg, pair_tl, pair_gx, gx0, sums, slots_z = refs[41:51]
+    extra_sent, extra_came, load_sem, weight_sem = refs[51:55]
+    kept, scratch = refs[55:64], refs[64:67]
     depth = count // (SIDE * SIDE)
     width = held[0].shape[1]
     section = lax.axis_index("pipe")
@@ -647,55 +708,123 @@
         pl.semaphore_signal(barrier, inc=1, device_id={"dp": peer}, device_id_type=MESH)
     pl.semaphore_wait(barrier, 3 + depth - 1)
 
-    extras = (
-        (small0, small1, pair_small), (tg0, tg1, pair_tg), (tl0, tl1, pair_tl),
-        (outs_all.at[0], outs_all.at[1], pair_out), (gx0, gx1, pair_gx),
+    extras = ((small1, pair_small), (tg1, pair_tg), (tl1, pair_tl), (gx1, pair_gx))
+    GX = 3
+
+    def extra_copy(i):
+        source, target = extras[i]
+        return remote(source, target, extra_sent.at[i], extra_came.at[i], pipe=1 - section)
+
+    order = (2, 1, 0, 3)
+
+    def mine(i, crop=0):
+        return held[i].at[pl.ds(crop * ROWS, ROWS), :]
+
+    def swap_copy(i):
+        return remote(back1[i], mine(4 + i, 1), swap_sent.at[i], swap_came.at[i], pipe=1 - section)
+
+    def own_copy(i):
+        if i < 4:
+            return pltpu.make_async_copy(lefts[i].at[1], mine(i), local_sem.at[i])
+        return pltpu.make_async_copy(back1[i - 4], mine(i), local_sem.at[i])
+
+    def given_copy(i):
+        return pltpu.make_async_copy(lefts[i].at[2], mine(i, 1), local_sem.at[8 + i])
+
+    def left_copy(i, crop):
+        return pltpu.make_async_copy(lefts[i].at[2 * crop], mine(i, crop), local_sem.at[4 * crop + i])
+
+    def load_copy(crop, number):
+        return pltpu.make_async_copy(
+            kept_all[number - Q].at[2 * crop], kept[number], load_sem.at[number]
+        )
+
+    def sum_copy(i):
+        return pltpu.make_async_copy(extras[i][0], (small_ref, tg_ref, tl_ref)[i], load_sem.at[i])
+
+    hidden = held[3].shape[1]
+    weights = (
+        sum_c, sum_a.at[:, pl.ds(hidden, width)], sum_a.at[:, pl.ds(0, hidden)], sum_b,
     )
 
-    def extra_copy(i, layer):
-        return remote(
-            extras[i][layer], extras[i][2], extra_sent.at[i], extra_came.at[i], pipe=1 - section
-        )
+    def weight_copy(i):
+        return pltpu.make_async_copy(own[i], weights[i], weight_sem.at[i])
+
+    extra_copy(GX).start()
 
     @pl.when(section == 0)
     def _():
-        for i in range(3):
-            extra_copy(i, 1).start()
+        for i in order:
+            swap_copy(i).start()
+        for i in range(GX):
+            extra_copy(i).start()
+        load_copy(0, B2).start()
+        weight_copy(3).start()
+        load_copy(0, DA).start()
+        weight_copy(2).start()
+        for number in (MI, BR):
+            load_copy(0, number).start()
+        weight_copy(1).start()
+        for number in (V, PR, K, Q):
+            load_copy(0, number).start()
+        weight_copy(0).start()
+        for i in range(4):
+            left_copy(i, 0).start()
+            left_copy(i, 1).start()
 
     @pl.when(section != 0)
     def _():
-        for i in range(3):
-            extra_copy(i, 0).start()
-
-    order = (0, 4, 2, 6, 1, 5, 3, 7)
-    for i in order:
-        mine = held[i].at[pl.ds(0, ROWS), :]
-        theirs = held[i].at[pl.ds(ROWS, ROWS), :]
-
-        @pl.when(section == 0)
-        def _():
-            remote(second[i], theirs, swap_sent.at[i], swap_came.at[i], pipe=1 - section).start()
-            pltpu.make_async_copy(first[i], mine, local_sem.at[i]).start()
-
-        @pl.when(section != 0)
-        def _():
-            remote(first[i], theirs, swap_sent.at[i], swap_came.at[i], pipe=1 - section).start()
-            pltpu.make_async_copy(second[i], mine, local_sem.at[i]).start()
+        for i in order:
+            own_copy(i).start()
+            given_copy(i).start()
+            own_copy(4 + i).start()
+        for i in range(GX):
+            sum_copy(i).start()
+
+    def first_layer(crop):
+        def vec(row):
+            return vec_all[row:row + 1, :]
+
+        def weight(i):
+            if crop == 0:
+                weight_copy(i).wait()
+
+        def loaded(*numbers):
+            for number in numbers:
+                if number != X:
+                    load_copy(crop, number).wait()
+
+        def done(unused, *numbers):
+            if crop == 0:
+                for number in numbers:
+                    load_copy(1, number).start()
+
+        if crop == 1:
+            extra_copy(GX).wait_recv()
+        x_ref = kept[0]
+        clear(x_ref)
+        for ref, start in ((xg_ref, 0), (xl_ref, LOCAL_ROW)):
+            x_ref[start:start + ref.shape[0], :] = ref[:, crop, :]
+        backward_steps(
+            scale, vec, weight, loaded, done, gx1 if crop == 0 else pair_gx, gx0.at[crop], kept, weights,
+            tuple(mine(4 + i, crop) for i in range(4)), (small_ref, tg_ref, tl_ref), scratch,
+        )
 
     @pl.when(section == 0)
     def _():
-        for i in range(3, 5):
-            extra_copy(i, 1).start()
-
-    @pl.when(section != 0)
-    def _():
-        for i in range(3, 5):
-            extra_copy(i, 0).start()
+        clear(small_ref, tg_ref, tl_ref)
+        first_layer(0)
+        first_layer(1)
+
+    def second_sums():
+        for i in range(GX):
+            extra_copy(i).wait_recv()
+            sum_copy(i).wait()
+        small_ref[...] += pair_small[...]
+        tg_ref[...] += pair_tg[...]
+        tl_ref[...] += pair_tl[...]
 
     def swapped_outputs():
-        extra_copy(3, 0).wait_recv()
-        extra_copy(4, 0).wait_recv()
-
         def live(count_ref, crop):
             return jnp.where(count_ref[0] > crop, 1.0, 0.0)
 
@@ -707,34 +836,46 @@
 
         @pl.when(section == 0)
         def _():
-            place(0, outs_all[0], gx0[...])
-            place(1, pair_out[...], pair_gx[...])
+            place(0, outs_all[0], gx0[0])
+            place(1, outs_all[2], gx0[1])
 
         @pl.when(section != 0)
         def _():
-            place(0, pair_out[...], pair_gx[...])
+            extra_copy(GX).wait_recv()
+            place(0, outs_all[2], pair_gx[...])
             place(1, outs_all[1], gx1[...])
 
-    def fold_back(mine, pair, index_ref, entries):
-        heads = pair.shape[1]
-
-        def one(r, result):
-            total = jnp.where(section == 0, mine[0][r], mine[1][r]) + pair[r]
-            high = total.astype(BF16)
-            low = (total - high.astype(F32)).astype(BF16)
-            spot = hot(index_ref[pl.ds(r, 1), :], entries)
-            return result + dot_cols(high, spot) + dot_cols(low, spot)
-
-        return lax.fori_loop(0, index_ref.shape[0], one, jnp.zeros((heads, entries), F32))
+    def fold_back(values, index_ref, entries, grid, cls_lane):
+        lanes = index_ref.shape[1]
+        total = values[0:grid].reshape(grid * 16, lanes)
+        high = total.astype(BF16)
+        low = (total - high.astype(F32)).astype(BF16)
+        found = dot_cols(jnp.concatenate([high, low], 0), hot(index_ref[0:1, :], entries))
+        found = found[:grid * 16] + found[grid * 16:]
+        result = found[:16]
+        for r in range(1, grid):
+            result = result + pltpu.roll(found[16 * r:16 * r + 16], r, 1)
+        lane = lax.broadcasted_iota(jnp.int32, (1, lanes), 1)
+        entry = lax.broadcasted_iota(jnp.int32, (1, entries), 1)
+        cls = (2 * grid - 1) ** 2
+        to_patch, to_class = values[grid], values[grid + 1]
+        for spot, column in (
+            (cls, jnp.sum(jnp.where(lane == cls_lane, 0.0, to_patch), axis=1, keepdims=True)),
+            (cls + 1, jnp.sum(to_class, axis=1, keepdims=True)),
+            (cls + 2, jnp.sum(jnp.where(lane == cls_lane, to_patch, 0.0), axis=1, keepdims=True)),
+        ):
+            result = result + jnp.where(entry == spot, column, 0.0)
+        return result
+
+    def small_fold():
+        sums[0] = jnp.zeros((SMALL_ROWS, width), F32)
+        sums[0, 0:16, :] = small_ref[...]
+        sums[0, TABLE_ROW:TABLE_ROW + 16, :] = fold_back(tg_ref, index_g, width, GRID_G, 0)
+        sums[0, TABLE_ROW_L:TABLE_ROW_L + 16, 0:128] = fold_back(
+            tl_ref, index_l, 128, GRID_L, LOCAL_ROW - 128
+        )
 
     def small_start():
-        for i in range(3):
-            extra_copy(i, 0).wait_recv()
-        sums[0] = jnp.zeros((SMALL_ROWS, width), F32)
-        sums[0, 0:16, :] = jnp.where(section == 0, small0[...], small1[...]) + pair_small[...]
-        heads = pair_tg.shape[1]
-        sums[0, TABLE_ROW:TABLE_ROW + heads, :] = fold_back((tg0, tg1), pair_tg, index_g, width)
-        sums[0, TABLE_ROW_L:TABLE_ROW_L + heads, 0:128] = fold_back((tl0, tl1), pair_tl, index_l, 128)
         small_x().start()
 
     def small_x():
@@ -778,11 +919,27 @@
             ref[:, 0, :] = total[start:start + ref.shape[0], 0:ref.shape[2]]
 
     def operands(*numbers):
-        for i in numbers:
-            mine = held[i].at[pl.ds(0, ROWS), :]
-            theirs = held[i].at[pl.ds(ROWS, ROWS), :]
-            pltpu.make_async_copy(first[i], mine, local_sem.at[i]).wait()
-            remote(first[i], theirs, swap_sent.at[i], swap_came.at[i], pipe=1 - section).wait_recv()
+        @pl.when(section == 0)
+        def _():
+            for i in numbers:
+                if i < 4:
+                    left_copy(i, 0).wait()
+                    left_copy(i, 1).wait()
+
+        @pl.when(section != 0)
+        def _():
+            for i in numbers:
+                own_copy(i).wait()
+                if i < 4:
+                    given_copy(i).wait()
+                else:
+                    swap_copy(i - 4).wait_recv()
+
+    def when_core(number, *steps):
+        @pl.when(section == number)
+        def _():
+            for step in steps:
+                step()
 
     def product(left, right, total, offset):
         def one(i, carry):
@@ -829,19 +986,20 @@
         accumulate(total, targets[k], yy, xx, here)
 
     c_parts = ((1 - y, 1 - x), (y, 1 - x), (1 - y, x), (y, x))
-    small_start()
-    operands(0, 4)
-    product(held[0], held[4], sum_c, 0)
-    small_second()
-
-    @pl.when(starts_line)
-    def _():
-        for k in range(depth - 1):
-            for c, (yy, xx) in enumerate(c_parts):
-                line_copy(sum_c, in_c1, 6, k, c, yy, xx, 4)[1].start()
-
-    def line_c(k, c):
+    items_c = 4 * (depth - 1)
+
+    def copy_c(n):
+        return line_copy(sum_c, in_c1, 6, n // 4, n % 4, *c_parts[n % 4], 4)
+
+    def line_c(n):
+        k, c = n // 4, n % 4
         yy, xx = c_parts[c]
+
+        @pl.when(starts_line)
+        def _():
+            copy_c(n)[1].wait_send()
+            if n + FLIGHT < items_c:
+                copy_c(n + FLIGHT)[1].start()
 
         @pl.when(jnp.logical_not(starts_line))
         def _():
@@ -871,6 +1029,8 @@
 
     def first_receive(which, i):
         first_copy(which, i).wait_recv()
+        if i + FLIGHT < 2 * depth:
+            first_copy(which, i + FLIGHT).start()
         zz = targets[i % depth]
         if which == 0:
             where = (zz, 1 - y if i < depth else y, x)
@@ -881,19 +1041,18 @@
         if i < depth:
             second_copy(which, i).start()
 
+    def line_z(which, k):
+        total, slots, group = (sum_a, in_a3, 2) if which == 0 else (sum_b, in_b3, 5)
+        source = total.at[chunk(total, targets[k], y, x), :]
+        peer = index(targets[k], y, x)
+        return remote(source, slots.at[z], sent[group].at[k], came[group].at[z], dp=peer)
+
     def line(which, k):
-        total, came_in, slots = (sum_a, in_a2, in_a3) if which == 0 else (sum_b, in_b2, in_b3)
-        group = 2 if which == 0 else 5
+        total, came_in = (sum_a, in_a2) if which == 0 else (sum_b, in_b2)
         second_copy(which, k).wait_recv()
         accumulate(total, targets[k], y, x, came_in.at[k])
         if k < depth - 1:
-            slot, copy = line_copy(total, slots, group, k, 0, y, x, 1)
-
-            @pl.when(jnp.logical_not(starts_line))
-            def _():
-                line_receive(total, slots, group, k, slot, y, x)
-
-            copy.start()
+            line_z(which, k).start()
 
     def line_end(total, slots, group, slot_below, slot_above, add):
         @pl.when(z > 0)
@@ -927,35 +1086,48 @@
             def add(here):
                 out_fc2[...] += here[...].astype(F32)
 
-        line_end(total, slots, group, z + 1, z, add)
+        for step in range(1, depth):
+            source = (z + step) % depth
+            here = slots.at[source]
+            peer = index(source, y, x)
+            remote(here, here, sent[group].at[0], came[group].at[source], dp=peer).wait_recv()
+            add(here)
 
     operands(2, 6, 1, 5)
     product(held[2], held[6], sum_a, 0)
     product(held[1], held[5], sum_a, held[6].shape[1])
-    small_third()
-    for i in range(2 * depth):
+    for i in range(FLIGHT):
         first_copy(0, i).start()
+    operands(0, 4)
+    product(held[0], held[4], sum_c, 0)
+
+    @pl.when(starts_line)
+    def _():
+        for n in range(min(FLIGHT, items_c)):
+            copy_c(n)[1].start()
+
     operands(3, 7)
     product(held[3], held[7], sum_b, 0)
+    for i in range(FLIGHT):
+        first_copy(1, i).start()
+
+    when_core(1, second_sums)
+    small_fold()
+    small_start()
+    done_c = 0
     for i in range(2 * depth):
-        first_copy(1, i).start()
-
-    swapped_outputs()
-    for i in range(depth):
         first_receive(1, i)
         first_receive(0, i)
-        if i < 4:
-            line_c(0, i)
-    for c in range(depth, 4):
-        line_c(0, c)
-    for i in range(depth):
-        first_receive(1, depth + i)
-        first_receive(0, depth + i)
-        if i < 4 and depth > 2:
-            line_c(1, i)
-    for k in range(2, depth - 1):
-        for c in range(4):
-            line_c(k, c)
+        while done_c < items_c * (i + 1) // (2 * depth):
+            line_c(done_c)
+            done_c += 1
+        if i == depth - 1:
+            small_second()
+        if i >= depth and i < 2 * depth - 1:
+            line(1, i - depth)
+            line(0, i - depth)
+        if i == 2 * depth - 2:
+            small_third()
 
     def end_c(c):
         yy, xx = c_parts[c]
@@ -973,68 +1145,69 @@
         source = sum_c.at[chunk(sum_c, z, 1 - y, x), :]
         return remote(source, in_c3, sent[8].at[0], came[8].at[0], dp=across_y)
 
-    line(1, 0)
-    line(0, 0)
     for c in range(2):
         end_c(c)
         copy_c2(c).start()
     end_c(2)
     end_c(3)
-    for k in range(1, depth - 1):
-        line(1, k)
-        line(0, k)
-        if k == 1:
-            copy_c2(0).wait_recv()
-            accumulate(sum_c, z, 1 - y, x, in_c2.at[0])
-            copy_c3().start()
-            copy_c2(1).wait_recv()
-            accumulate(sum_c, z, y, x, in_c2.at[1])
+    copy_c2(0).wait_recv()
+    accumulate(sum_c, z, 1 - y, x, in_c2.at[0])
+    copy_c3().start()
+    copy_c2(1).wait_recv()
+    accumulate(sum_c, z, y, x, in_c2.at[1])
+    swapped_outputs()
     line(1, depth - 1)
     line(0, depth - 1)
     copy_c3().wait_recv()
     out_qkv[...] = sum_c[chunk(sum_c, z, y, x), :].astype(F32) + in_c3[...].astype(F32)
-    small_end()
     finish(1)
     finish(0)
-
-    for i in range(5):
-        extra_copy(i, 0).wait_send()
+    small_end()
+
+    extra_copy(GX).wait_send()
+
+    @pl.when(section == 0)
+    def _():
+        for i in range(GX):
+            extra_copy(i).wait_send()
+        for i in order:
+            swap_copy(i).wait_send()
+
     small_x().wait_send()
     small_y().wait_send()
     for step in range(1, depth):
         small_z(step).wait_send()
-    for i in order:
-        theirs = held[i].at[pl.ds(ROWS, ROWS), :]
-        remote(first[i], theirs, swap_sent.at[i], swap_came.at[i], pipe=1 - section).wait_send()
     for which in range(2):
         for i in range(2 * depth):
             first_copy(which, i).wait_send()
         for i in range(depth):
             second_copy(which, i).wait_send()
         for k in range(depth - 1):
-            total, slots = (sum_a, in_a3) if which == 0 else (sum_b, in_b3)
-            line_copy(total, slots, 2 if which == 0 else 5, k, 0, y, x, 1)[1].wait_send()
-    for k in range(depth - 1):
-        for c, (yy, xx) in enumerate(c_parts):
-            line_copy(sum_c, in_c1, 6, k, c, yy, xx, 4)[1].wait_send()
+            line_z(which, k).wait_send()
+    @pl.when(jnp.logical_not(starts_line))
+    def _():
+        for n in range(items_c):
+            copy_c(n)[1].wait_send()
+
     copy_c2(0).wait_send()
     copy_c2(1).wait_send()
     copy_c3().wait_send()
 
 
-def scattered(count, kept, back0, back1, counts, tokens, entries):
+def scattered(count, kept, back1, crops, vec, own, counts, tokens, entries):
     lefts = [kept[i] for i in (1, 6, 9, 10)]
-    widths = [a.shape[2] for a in lefts] + [back0[i].shape[1] for i in (1, 2, 3, 4)]
+    widths = [a.shape[2] for a in lefts] + [back1[i].shape[1] for i in (1, 2, 3, 4)]
     n1, merged, n2, act, gmixed, gbranch, ghidden, gb2 = widths
-    heads = back0[6].shape[1]
+    heads = kept[5].shape[1]
+    scale = (n1 // heads) ** (-0.5)
     depth = count // (SIDE * SIDE)
     rows, rows_b = n1 // count, act // count
     cols_a = ghidden + gbranch
     copies = (2 * depth, depth, depth - 1, 2 * depth, depth, depth - 1, 4 * (depth - 1), 2, 1)
-    arrivals = (2 * depth, depth, depth + 1, 2 * depth, depth, depth + 1, 4 * (depth + 1), 2, 1)
+    arrivals = (2 * depth, depth, depth, 2 * depth, depth, depth, 4 * (depth + 1), 2, 1)
     tokens_g, tokens_l = tokens
     return pl.pallas_call(
-        functools.partial(scatter_kernel, count),
+        functools.partial(scatter_kernel, count, scale),
         out_shape=(
             shape(rows, gmixed, dtype=F32), shape(rows, gbranch, dtype=F32),
             shape(rows, ghidden, dtype=F32), shape(rows_b, gb2, dtype=F32),
@@ -1042,29 +1215,33 @@
             *(shape(1, n1, dtype=F32) for _ in range(10)), shape(1, act, dtype=F32),
             shape(heads, 1, entries[0], dtype=F32), shape(heads, 1, entries[1], dtype=F32),
         ),
-        in_specs=[OUTSIDE] * 12 + [INSIDE] * 11 + [SCALARS] * 2,
+        in_specs=[OUTSIDE] * 23 + [INSIDE] * 7 + [SCALARS] * 2,
         out_specs=(INSIDE,) * 21,
         scratch_shapes=[pltpu.VMEM((2 * ROWS, w), BF16) for w in widths]
         + [pltpu.VMEM((n1, cols_a), BF16), pltpu.VMEM((act, gb2), BF16), pltpu.VMEM((n1, gmixed), BF16)]
-        + [pltpu.VMEM((slots, rows, cols_a), BF16) for slots in (2 * depth, depth, depth + 1)]
-        + [pltpu.VMEM((slots, rows_b, gb2), BF16) for slots in (2 * depth, depth, depth + 1)]
+        + [pltpu.VMEM((slots, rows, cols_a), BF16) for slots in (2 * depth, depth, depth)]
+        + [pltpu.VMEM((slots, rows_b, gb2), BF16) for slots in (2 * depth, depth, depth)]
         + [pltpu.VMEM((4 * (depth + 1), rows, gmixed), BF16), pltpu.VMEM((2, rows, gmixed), BF16),
            pltpu.VMEM((rows, gmixed), BF16)]
-        + [DMA((8,)), DMA((8,)), DMA((8,))]
+        + [DMA((12,)), DMA((4,)), DMA((4,))]
         + [DMA((c,)) for c in copies] + [DMA((a,)) for a in arrivals]
+        + 2 * [
+            pltpu.VMEM((16, n1), F32), pltpu.VMEM((16, 16, LANES_G), F32),
+            pltpu.VMEM((8, 16, LANES_L), F32),
+        ]
         + [
-            pltpu.VMEM((16, n1), F32), pltpu.VMEM((16, heads, LANES_G), F32),
-            pltpu.VMEM((8, heads, LANES_L), F32), pltpu.VMEM((ROWS, n1), BF16), pltpu.VMEM((ROWS, n1), BF16),
+            pltpu.VMEM((ROWS, n1), BF16), pltpu.VMEM((2, ROWS, n1), BF16),
             pltpu.VMEM((5, SMALL_ROWS, n1), F32), pltpu.VMEM((depth, SMALL_ROWS, n1), F32),
-            DMA((6 + depth,)), DMA((6 + depth,)),
-        ],
+            DMA((6 + depth,)), DMA((6 + depth,)), DMA((9,)), DMA((4,)),
+        ]
+        + kept_scratch(heads, n1, act) + work_scratch(n1),
         compiler_params=pltpu.CompilerParams(
-            vmem_limit_bytes=60 * 2**20, collective_id=1, has_side_effects=True
+            vmem_limit_bytes=62 * 2**20, collective_id=1, has_side_effects=True
         ),
-        name="gradient_scatter",
+        name="first_backward_and_scatter",
     )(
-        *lefts, *back0[1:5], *back1[1:5], *back0[5:8], *back1[5:8],
-        jnp.asarray(INDEX_G), jnp.asarray(INDEX_L), kept[0], back0[0], back1[0], *counts,
+        *lefts, *back1[1:5], *(kept[i] for i in (2, 3, 4, 5, 7, 8, 11, 12)), *own, *back1[5:8],
+        jnp.asarray(INDEX_G), jnp.asarray(INDEX_L), kept[0], back1[0], vec, *crops, *counts,
     )
 
 
@@ -1119,7 +1296,8 @@
     hidden = back0[3].shape[1]
     rows = [small[i:i + 1] for i in range(F1B)]
     rows.append(small[F1B:F1B + hidden // width].reshape(1, hidden))
-    tables = (tg[:, None, :entries[0]], tl[:, None, :entries[1]])
+    heads = kept[5].shape[1]
+    tables = (tg[:heads, None, :entries[0]], tl[:heads, None, :entries[1]])
     return (*shares, out_g, out_l, gin_g, gin_l, *rows, *tables)
 
 
@@ -1156,17 +1334,18 @@
     tables = (table_global[0].T, table_local[0].T)
     crops = tuple(jnp.transpose(a, (1, 0, 2)) for a in (x_global, x_local))
     cots = tuple(jnp.transpose(a, (1, 0, 2)) for a in (cot_global, cot_local))
-    results = forward(*crops, vec, tables, own)
+    count = lax.axis_size("dp")
+    whole_tiles = count % (2 * SIDE * SIDE) == 0 and width % (16 * count) == 0
+    results = forward(*crops, vec, tables, own, not whole_tiles)
     other, kept, vec = results[:4], results[4:17], results[17]
     counts = (global_count, local_count)
-    back1 = backward(1, (*cots, *counts), kept[0], vec, kept, heads, own, other)
-    back0 = backward(0, back1[0], crops, vec, kept, heads, own, other)
-    count = lax.axis_size("dp")
-    given = (kept, back0, back1, counts, tokens, (entries_g, entries_l))
-    if count % (2 * SIDE * SIDE) == 0 and width % (16 * count) == 0:
-        results = finished(scattered(count, *given))
+    back1 = backward(1, (*cots, *counts), vec, kept, heads, own, other)
+    entries = (entries_g, entries_l)
+    if whole_tiles:
+        results = finished(scattered(count, kept, back1, crops, vec, own, counts, tokens, entries))
     else:
-        results = plain_scattered(*given)
+        back0 = backward(0, (back1[0], *crops), vec, kept, heads, own, other)
+        results = plain_scattered(kept, back0, back1, counts, tokens, entries)
     shares, crops, small, tables = results[:4], results[4:8], results[8:19], results[19:]
     vectors = [small[i] for i in (N1G, N1S, QB, VB, PB, SA, N2G, N2S, F1B, F2B, SM)]
     return (

time: 236 us -> 217 us (0.919)
  the two profiles are of different devices: /device:TPU:22 before, /device:TPU:0 now
where the time goes in v4:
time: 217 us; the launch traced here: 214 us
  Pallas kernels  212 us (98%)
  between operations  2.27 us (1%)
    pallas_call x1, Pallas kernels, scattered(): pl.pallas_call(functools.partial(scatter_kernel, count, scale), out_shape...  149 us
    pallas_call x1, Pallas kernels, forward(): pl.pallas_call(kernel, out_shape=tuple((shape(*w.shape) for w in own)) +...  38.6 us
    pallas_call x1, Pallas kernels, backward(): pl.pallas_call(kernel, out_shape=(shape(ROWS, width), shape(ROWS, 3 * wid...  21 us

profile of v4, /device:TPU:0, one launch (start us, length us, event | category | flops | bytes accessed | tf_op | source)
XLA Modules:
  0.0 214.5 jit_solution(12734064337112887579)
XLA Ops:
  2.0 38.6 %forward_layers.1 = (bf16[768,2304]{1,0:T(8,128)(2,1)}, bf16[768,768]{1,0:T(8,128)(2,1)}, bf16[768,3072]{1,0:T(8,128)(2,1)}, bf16[3072,768]{1,0:T(8,128)(2,1)}, ...) custom-call(bf16[197,2,768]{2,1,0:T(2,128)(2,1)} %bitcast.44, ...), custom_call_target="tpu_custom_call" | custom-call | tf_op jit(solution)/shard_map/forward_layers/pallas_call | solution.py:607
  40.6 21.0 %layer_backward.1 = (bf16[256,768]{1,0:T(8,128)(2,1)}, bf16[256,2304]{1,0:T(8,128)(2,1)}, bf16[256,768]{1,0:T(8,128)(2,1)}, bf16[256,3072]{1,0:T(8,128)(2,1)}, b...) custom-call(bf16[197,2,768]{2,1,0:T(2,128)(2,1)} %bitcast.46, ...), custom_call_target="tpu_custom_call" | custom-call | tf_op jit(solution)/shard_map/layer_backward/pallas_call | solution.py:632
  61.6 148.9 %first_backward_and_scatter.1 = (f32[48,2304]{1,0:T(8,128)}, f32[48,768]{1,0:T(8,128)}, f32[48,3072]{1,0:T(8,128)}, f32[192,768]{1,0:T(8,128)}, bf16[197,2,768]{...) custom-call(bf16[3,256,768]{2,1,0:T(8,128)(2,1)} %get-tuple-element., ...), custom_call_target="tpu_custom_call" | custom-call | tf_op jit(solution)/shard_map/first_backward_and_scatter/pallas_call | solution.py:1209
  210.4 3.8 %results.1 = (f32[48,2304]{1,0:T(8,128)}, f32[48,768]{1,0:T(8,128)}, f32[48,3072]{1,0:T(8,128)}, f32[192,768]{1,0:T(8,128)}, bf16[197,2,768]{2,1,0:T(2,128)(2,1)...) custom-call(f32[48,2304]{1,0:T(8,128)} %get-tuple-element.115.refs_0, ...), custom_call_target="tpu_custom_call" | custom-call | tf_op jit(solution)/shard_map/results/pallas_call | solution.py:1311
